TPU v7x, 512 devices: a whole 4x8x8 slice. The times are simulated.
512 devices in a mesh: row: 64 (over z, y), chan: 8 (over x, core).
Axes of the slice: x: 4, y: 8, z: 8, core: 2. Of those that a mesh axis runs over, the one named last changes fastest.
Arguments:
- pair: bfloat16 [1024, 1024, 128], P('row'), may hold values from -6 to 6
- ln_gain: float32 [128], replicated, may hold values from 0.25 to 1.75
- ln_bias: float32 [128], replicated, may hold values from -3 to 3
- w_a_gate: bfloat16 [128, 128], P(None, 'chan'), may hold values from -0.5 to 0.5
- w_a_proj: bfloat16 [128, 128], P(None, 'chan'), may hold values from -0.5 to 0.5
- w_b_gate: bfloat16 [128, 128], P(None, 'chan'), may hold values from -0.5 to 0.5
- w_b_proj: bfloat16 [128, 128], P(None, 'chan'), may hold values from -0.5 to 0.5
- w_gate: bfloat16 [128, 128], replicated, may hold values from -0.5 to 0.5
- out_gain: float32 [128], replicated, may hold values from 0.25 to 1.75
- out_bias: float32 [128], replicated, may hold values from -3 to 3
- w_out: bfloat16 [128, 128], replicated, may hold values from -0.5 to 0.5
Outputs:
- update: bfloat16 [1024, 1024, 128], P('row', 'chan')
All inputs are finite; a program needn't handle non-finite values.
Results may differ from a plain program's by a relative error of at most 0.014.
Values may be sent and summed in bfloat16 or wider, within the bound.
No kernel may reach another device: no remote copies, remote signals or barrier semaphores. Data moves between devices by JAX's collectives and lax.ppermute only.
A program may use at most 128 MiB of HBM per device.

v0:
```python
import jax
import jax.numpy as jnp
from jax import lax
from jax.sharding import PartitionSpec as P


def shards(
    pair,
    ln_gain,
    ln_bias,
    w_a_gate,
    w_a_proj,
    w_b_gate,
    w_b_proj,
    w_gate,
    out_gain,
    out_bias,
    w_out,
):
    values = pair.astype(jnp.float32)
    mean = jnp.mean(values, axis=-1, keepdims=True)
    var = jnp.mean((values - mean) ** 2, axis=-1, keepdims=True)
    normed = ((values - mean) * lax.rsqrt(var + 1e-05) * ln_gain + ln_bias).astype(jnp.bfloat16)

    def project(w_g, w_p):
        g = jnp.einsum("kip,pc->cki", normed, w_g, preferred_element_type=jnp.float32)
        p = jnp.einsum("kip,pc->cki", normed, w_p, preferred_element_type=jnp.float32)
        return (jax.nn.sigmoid(g) * p).astype(jnp.bfloat16)

    left = project(w_a_gate, w_a_proj)
    right = project(w_b_gate, w_b_proj)
    slab = left.shape[0]
    width = normed.shape[1]
    left_cols = lax.all_to_all(left, "row", split_axis=2, concat_axis=1, tiled=True)
    mixed = jnp.einsum(
        "cki,ckj->cij",
        left_cols,
        lax.all_gather(right, "row", axis=1, tiled=True),
        preferred_element_type=jnp.float32,
    )
    chan_count = lax.axis_size("chan")
    chan_pos = lax.axis_index("chan")
    col_width = width // chan_count
    normed_cols = lax.dynamic_slice_in_dim(normed, chan_pos * col_width, col_width, 1)
    gate = jax.nn.sigmoid(
        jnp.einsum("ijp,po->ijo", normed_cols, w_gate, preferred_element_type=jnp.float32)
    )
    total_ch = slab * chan_count
    first = jnp.sum(mixed, axis=0)
    second = jnp.sum(mixed * mixed, axis=0)
    first, second = (
        lax.psum(first.astype(jnp.bfloat16), "chan").astype(jnp.float32),
        lax.psum(second.astype(jnp.bfloat16), "chan").astype(jnp.float32),
    )
    mu = first / total_ch
    sigma = second / total_ch - mu * mu
    gain_part = lax.dynamic_slice_in_dim(out_gain, chan_pos * slab, slab, 0)
    bias_part = lax.dynamic_slice_in_dim(out_bias, chan_pos * slab, slab, 0)
    scaled = (
        (mixed - mu[None]) * lax.rsqrt(sigma[None] + 1e-05) * gain_part[:, None, None]
        + bias_part[:, None, None]
    ).astype(jnp.bfloat16)
    out_part = lax.dynamic_slice_in_dim(w_out, chan_pos * slab, slab, 0)
    summed = lax.psum_scatter(
        jnp.einsum("cij,co->jio", scaled, out_part, preferred_element_type=jnp.float32),
        "chan",
        scatter_dimension=0,
        tiled=True,
    )
    proj = jnp.transpose(summed, (1, 0, 2))
    return (proj * gate).astype(jnp.bfloat16)


def solution(mesh):
    in_specs = (
        P("row", None, None),
        P(),
        P(),
        P(None, "chan"),
        P(None, "chan"),
        P(None, "chan"),
        P(None, "chan"),
        P(),
        P(),
        P(),
        P(),
    )
    out_specs = P("row", "chan", None)
    return jax.shard_map(shards, mesh=mesh, in_specs=in_specs, out_specs=out_specs, check_vma=False)
```

profile of v0, /device:TPU:1, one launch (start us, length us, event | category | flops | bytes accessed | tf_op | source)
XLA Modules:
  0.0 476.2 jit_solution(13120651536571539582)
XLA Ops:
  6.6 3.5 convert_reduce_fusion
  10.1 4.8 %fusion.4 = f32[16,1024]{1,0:T(8,128)S(1)} fusion(bf16[16,1024,128]{2,1,0:T(8,128)(2,1)S(1)} %copy-done.1, f32[16,1024]{1,0:T(8,128)S(1)} %broadcast_multiply_fusion), kind=kLoop, calls=%fused_computation.6 | loop fusion | flops 8372224 | bytes 4325376 | tf_op jit(solution)/shard_map/reduce_sum | solution.py:22
  14.9 5.0 %fusion.7 = bf16[16,1024,128]{2,1,0:T(8,128)(2,1)S(1)} fusion(bf16[16,1024,128]{2,1,0:T(8,128)(2,1)S(1)} %copy-done.1, f32[128]{0:T(128)S(1)} %copy-done.6, f32[128]{0:T(128)S(1)} %copy-done.7, f32[16,1024]{1,0:T(8,128)S(1)} %add_rsqrt_fusion.1, f32[16,1024]{1,0:T(8,128)S(1)} %broadcast_multiply_fusion), kind=kLoop, calls=%fused_computation.9 | loop fusion | flops 12582912 | bytes 8520704 | tf_op jit(solution)/shard_map/convert_element_type | solution.py:23
  20.0 1.2 fusion.11
  21.2 0.8 copy-done.2
  22.0 2.0 fusion.21
  24.1 3.6 fusion.14
  27.7 1.2 fusion.22
  28.9 4.7 copy.23
  33.6 6.4 %reshape.26 = bf16[64,2,2048]{2,1,0:T(2,128)(2,1)S(1)} reshape(bf16[1024,16,16]{2,1,0:T(8,128)(2,1)} %bitcast.41) | data formatting | bytes 1048576
  40.0 40.3 %all_to_all.18 = bf16[64,2,2048]{2,1,0:T(2,128)(2,1)S(1)} all-to-all(bf16[64,2,2048]{2,1,0:T(2,128)(2,1)S(1)} %reshape.26), channel_id=1, replica_groups=mesh['row'=64,'chan'=8] {'row'}, dimensions={0} | all-to-all | bytes 1048576 | tf_op jit(solution)/shard_map/all_to_all | solution.py:34
  80.3 4.1 reshape.27
  84.4 9.5 %copy.25 = bf16[16,64,16,16]{2,1,3,0:T(8,128)(2,1)} copy(bf16[16,64,16,16]{0,2,3,1:T(8,128)(2,1)} %bitcast.42) | data formatting | bytes 1048576 | tf_op jit(solution)/shard_map/all_to_all | solution.py:34
  93.9 8.2 %all_to_all.16 = bf16[16,1024,16]{1,2,0:T(8,128)(2,1)S(1)} reshape(bf16[16,64,16,16]{2,1,3,0:T(8,128)(2,1)} %copy.25) | data formatting | bytes 1048576 | tf_op jit(solution)/shard_map/all_to_all | solution.py:34
  102.1 158.9 %all-gather.2.cloned.1.call-done = bf16[16,1024,1024]{2,0,1:T(8,128)(2,1)} async-done(((bf16[16,16,1024]{2,0,1:T(8,128)(2,1)}), bf16[16,1024,1024]{2,0,1:T(8,128)(2,1)}) %all-gather.2.cloned.1.call-update) | async-done | bytes 33554448 | tf_op jit(solution)/shard_map/all_gather | solution.py:38
  261.0 75.5 %fusion.34 = (bf16[16,1024]{1,0:T(8,128)(2,1)}, bf16[16,1024]{1,0:T(8,128)(2,1)}, f32[16,16,1024]{2,1,0:T(8,128)S(1)}) fusion(bf16[16,1024,16]{1,2,0:T(8,128)(2,1)S(1)} %all_to_all.16, bf16[16,1024,1024]{2,0,1:T(8,128)(2,1)} %all-gather.2.cloned.1.call-done), kind=kOutput, calls=%fused_computation.48 | convolution fusion | flops 537624576 | bytes 35192832 | tf_op jit(solution)/shard_map/cki,ckj->cij/dot_general | solution.py:35
  336.6 0.1 dynamic_slice.13
  336.7 66.3 %all-reduce.3.cloned.1.call-done = (bf16[16,1024]{1,0:T(8,128)(2,1)}, bf16[16,1024]{1,0:T(8,128)(2,1)}) async-done(((bf16[16,1024]{1,0:T(8,128)(2,1)}, bf16[16,1024]{1,0:T(8,128)(2,1)}), (bf16[16,1024]{1,0:T(8,128)(2,1)}, bf16[16,1024]{1,0:T(8,128)(2,1)})) %all-reduce.3.cloned.1.call-update) | async-done | bytes 65552 | tf_op jit(solution)/shard_map/psum | solution.py:53
  403.0 0.8 convert_multiply_fusion
  403.8 0.3 add_convert_fusion
  404.1 4.5 convolution_bitcast_fusion
  408.7 57.7 %reduce-scatter.2.cloned.1.call-done = f32[128,16,128]{0,2,1:T(8,128)} async-done(((f32[1024,16,128]{0,2,1:T(8,128)}), f32[128,16,128]{0,2,1:T(8,128)}) %reduce-scatter.2.cloned.1.call-update) | async-done | bytes 1048592 | tf_op jit(solution)/shard_map/reduce_scatter | solution.py:64
  466.4 1.9 fusion.18
  468.3 1.0 copy.29
  (34 shorter events, 0.3 us)
Async XLA Ops:
  6.5 397.6 %copy-start = (bf16[128,128]{1,0:T(8,128)(2,1)S(1)}, bf16[128,128]{1,0:T(8,128)(2,1)}, u32[]{:S(2)}) copy-start(bf16[128,128]{1,0:T(8,128)(2,1)} %param.21) | copy-start | bytes 98308
  6.5 8.4 %copy-start.7 = (f32[128]{0:T(128)S(1)}, f32[128]{0:T(128)}, u32[]{:S(2)}) copy-start(f32[128]{0:T(128)} %param.12) | copy-start | bytes 1540
  6.5 8.4 %copy-start.6 = (f32[128]{0:T(128)S(1)}, f32[128]{0:T(128)}, u32[]{:S(2)}) copy-start(f32[128]{0:T(128)} %param.13) | copy-start | bytes 1540
  6.5 254.5 %all-gather.2.cloned.1.call-start = ((), (), s32[]{:S(2)}) async-start(), calls=%async_computation.2 | async-start | bytes 34078720 | tf_op jit(solution)/shard_map/all_gather | solution.py:38
  6.5 3.5 copy-start.1
  14.9 5.0 %copy-start.9 = (bf16[128,16]{0,1:T(8,128)(2,1)S(1)}, bf16[128,16]{0,1:T(8,128)(2,1)}, u32[]{:S(2)}) copy-start(bf16[128,16]{0,1:T(8,128)(2,1)} %param.16) | copy-start | bytes 12292
  19.9 2.1 copy-start.2
  20.0 2.1 copy-start.4
  22.0 2.1 copy-start.10
  24.0 3.7 copy-start.5
  24.1 379.0 %all-reduce.3.cloned.1.call-start = ((), (), s32[]{:S(2)}) async-start(), calls=%async_computation.4 | async-start | bytes 131072 | tf_op jit(solution)/shard_map/psum | solution.py:53
  24.1 3.6 copy-start.3
  102.1 234.5 %copy-start.11 = (f32[128]{0:T(128)S(1)}, f32[128]{0:T(128)}, u32[]{:S(2)}) copy-start(f32[128]{0:T(128)} %param.19) | copy-start | bytes 1540
  102.1 234.6 %copy-start.12 = (f32[128]{0:T(128)S(1)}, f32[128]{0:T(128)}, u32[]{:S(2)}) copy-start(f32[128]{0:T(128)} %param.20) | copy-start | bytes 1540
  336.5 129.9 %reduce-scatter.2.cloned.1.call-start = ((), (), s32[]{:S(2)}) async-start(), calls=%async_computation.3 | async-start | bytes 9437184 | tf_op jit(solution)/shard_map/reduce_scatter | solution.py:64
  408.6 57.8 %copy-start.8 = (bf16[128,128]{1,0:T(8,128)(2,1)S(1)}, bf16[128,128]{1,0:T(8,128)(2,1)}, u32[]{:S(2)}) copy-start(bf16[128,128]{1,0:T(8,128)(2,1)} %param.18) | copy-start | bytes 98308
Sparse Core Ops, SparseCore 0:
  24.2 236.8 all-gather.1
  336.6 66.3 all-reduce.2
  408.8 57.5 reduce-scatter.1
where the time goes:
time: 483 us; the launch traced here: 476 us
  waiting for transfers between devices  283 us (59%)
  matrix products  89.8 us (19%)
  blocking collectives  40.3 us (8%)
  local copies, waits for them, and re-layouts  34.9 us (7%)
  other arithmetic  14.4 us (3%)
  between operations  13.7 us (3%)
    all_gather x1, waiting for transfers between devices, shards(): lax.all_gather(right, 'row', axis=1, tiled=True)  159 us
    dot_general x1, matrix products, shards(): jnp.einsum('cki,ckj->cij', left_cols, lax.all_gather(right, 'row', axis=1...  75.5 us
    psum x1, waiting for transfers between devices, shards(): lax.psum(second.astype(jnp.bfloat16), 'chan').astype(jnp.float32)  66.3 us
    reduce_scatter x1, waiting for transfers between devices, shards(): lax.psum_scatter(jnp.einsum('cij,co->jio', scaled, out_part, preferred_el...  57.7 us
    all_to_all x1, blocking collectives, shards(): lax.all_to_all(left, 'row', split_axis=2, concat_axis=1, tiled=True)  40.3 us
    all_to_all x2, local copies, waits for them, and re-layouts, shards(): lax.all_to_all(left, 'row', split_axis=2, concat_axis=1, tiled=True)  17.7 us
    unnamed x28, local copies, waits for them, and re-layouts  11.3 us
  transfers between devices with their start and end apart: 3, of which 3 were waited for; matrix products, arithmetic and copies ran while one was open for 6% of the time, Pallas kernels for 0%

commit v1 on v0

v1 whole, which is shorter than its diff:
```python
import jax
import jax.numpy as jnp
from jax import lax
from jax.experimental import pallas as pl
from jax.experimental.pallas import tpu as pltpu
from jax.sharding import Mesh
from jax.sharding import PartitionSpec as P

F32 = jnp.float32
BF16 = jnp.bfloat16
VMEM_LIMIT = 48 * 1024 * 1024
EPS = 1e-05


def params():
    return pltpu.CompilerParams(vmem_limit_bytes=VMEM_LIMIT)


def norm_kernel(pos, pair, gain, bias, out):
    values = pair[...].astype(F32)
    mean = jnp.mean(values, axis=-1, keepdims=True)
    centred = values - mean
    var = jnp.mean(centred * centred, axis=-1, keepdims=True)
    out[...] = (centred * lax.rsqrt(var + EPS) * gain[...] + bias[...]).astype(BF16)


def norm_columns(pos, pair, gain, bias, width):
    rows, _, chans = pair.shape
    step = rows // 4
    return pl.pallas_call(
        norm_kernel,
        out_shape=jax.ShapeDtypeStruct((rows, width, chans), BF16),
        grid_spec=pltpu.PrefetchScalarGridSpec(
            num_scalar_prefetch=1,
            grid=(4,),
            in_specs=[
                pl.BlockSpec((step, width, chans), lambda s, pos: (s, pos[0], 0)),
                pl.BlockSpec((1, 1, chans), lambda s, pos: (0, 0, 0)),
                pl.BlockSpec((1, 1, chans), lambda s, pos: (0, 0, 0)),
            ],
            out_specs=pl.BlockSpec((step, width, chans), lambda s, pos: (s, 0, 0)),
        ),
        compiler_params=params(),
        cost_estimate=pl.CostEstimate(
            flops=8 * rows * width * chans, bytes_accessed=4 * rows * width * chans, transcendentals=rows * width
        ),
    )(pos, pair, gain.reshape(1, 1, chans), bias.reshape(1, 1, chans))


def project_kernel(normed, weights, out):
    rows, width, chans = normed.shape
    slab = weights.shape[0] // 2
    flat = normed[...].reshape(rows * width, chans)
    both = lax.dot_general(weights[...], flat, (((1,), (1,)), ((), ())), preferred_element_type=F32)
    value = jax.nn.sigmoid(both[:slab]) * both[slab:]
    parts = [value[:, k * width : (k + 1) * width] for k in range(rows)]
    out[...] = jnp.swapaxes(jnp.stack(parts, axis=0), 0, 1).astype(BF16)


def project(normed, weights):
    rows, width, chans = normed.shape
    slab = weights.shape[0] // 2
    lanes = 128
    return pl.pallas_call(
        project_kernel,
        out_shape=jax.ShapeDtypeStruct((slab, rows, width), BF16),
        grid=(width // lanes,),
        in_specs=[
            pl.BlockSpec((rows, lanes, chans), lambda s: (0, s, 0)),
            pl.BlockSpec((2 * slab, chans), lambda s: (0, 0)),
        ],
        out_specs=pl.BlockSpec((slab, rows, lanes), lambda s: (0, 0, s)),
        compiler_params=params(),
        cost_estimate=pl.CostEstimate(
            flops=4 * rows * width * slab * chans,
            bytes_accessed=2 * rows * width * (slab + chans),
            transcendentals=rows * width * slab,
        ),
    )(normed, weights)


def gate_kernel(pos, normed, weights, out):
    rows, width, chans = normed.shape
    flat = normed[...].reshape(rows * width, chans)
    got = jnp.dot(flat, weights[...], preferred_element_type=F32)
    out[...] = jax.nn.sigmoid(got).reshape(rows, width, chans)


def output_gate(pos, normed, weights, width):
    rows, _, chans = normed.shape
    step = rows // 2
    return pl.pallas_call(
        gate_kernel,
        out_shape=jax.ShapeDtypeStruct((rows, width, chans), F32),
        grid_spec=pltpu.PrefetchScalarGridSpec(
            num_scalar_prefetch=1,
            grid=(2,),
            in_specs=[
                pl.BlockSpec((step, width, chans), lambda s, pos: (s, pos[1], 0)),
                pl.BlockSpec((chans, chans), lambda s, pos: (0, 0)),
            ],
            out_specs=pl.BlockSpec((step, width, chans), lambda s, pos: (s, 0, 0)),
        ),
        compiler_params=params(),
        cost_estimate=pl.CostEstimate(
            flops=2 * rows * width * chans * chans,
            bytes_accessed=6 * rows * width * chans,
            transcendentals=rows * width * chans,
        ),
    )(pos, normed, weights)


def mix_kernel(pos, left, right, out):
    half = right.shape[1] // 2
    core = pos[1]
    block = left[0]
    for which in range(2):
        at = pl.multiple_of((core if which == 0 else 1 - core) * half, half)
        mixed = lax.dot_general(
            block, right[:, pl.ds(at, half)], (((0,), (0,)), ((), ())), preferred_element_type=F32
        )
        rows = out.shape[1] // 2
        out[:, which * rows : (which + 1) * rows, :] = mixed.reshape(out.shape[0], rows, half).astype(BF16)


def mix(pos, left, right, rows):
    slices, depth, height = left.shape
    width = right.shape[1]
    per = height // rows
    return pl.pallas_call(
        mix_kernel,
        out_shape=jax.ShapeDtypeStruct((slices * per, 2 * rows, width // 2), BF16),
        grid_spec=pltpu.PrefetchScalarGridSpec(
            num_scalar_prefetch=1,
            grid=(slices,),
            in_specs=[
                pl.BlockSpec((1, depth, height), lambda s, pos: (s, 0, 0)),
                pl.BlockSpec((depth, width), lambda s, pos: (0, 0)),
            ],
            out_specs=pl.BlockSpec((per, 2 * rows, width // 2), lambda s, pos: (s, 0, 0)),
        ),
        compiler_params=params(),
        cost_estimate=pl.CostEstimate(
            flops=2 * slices * depth * height * width,
            bytes_accessed=2 * (slices * depth * height + depth * width + slices * height * width),
            transcendentals=0,
        ),
    )(pos, left, right)


def finish_kernel(pos, own, other, gain, bias, weights, gate, out):
    core = pos[1]
    slab, rows, width = own.shape
    mine = own[...].astype(F32)
    theirs = other[...].astype(F32)
    total = 2 * slab
    mean = (jnp.sum(mine, axis=0) + jnp.sum(theirs, axis=0)) / total
    mine = mine - mean[None]
    theirs = theirs - mean[None]
    var = (jnp.sum(mine * mine, axis=0) + jnp.sum(theirs * theirs, axis=0)) / total
    scale = lax.rsqrt(var + EPS)
    mine = jnp.swapaxes(mine * scale[None], 0, 1)
    theirs = jnp.swapaxes(theirs * scale[None], 0, 1)
    mine = (mine * gain[core][None] + bias[core][None]).astype(BF16)
    theirs = (theirs * gain[1 - core][None] + bias[1 - core][None]).astype(BF16)
    contract = (((0,), (0,)), ((), ()))
    for row in range(rows):
        proj = lax.dot_general(mine[row], weights[core], contract, preferred_element_type=F32)
        proj = proj + lax.dot_general(theirs[row], weights[1 - core], contract, preferred_element_type=F32)
        out[row] = (proj * gate[row]).astype(BF16)


def finish(pos, mixed, other, gain, bias, weights, gate):
    slab, rows, width = other.shape
    outs = weights.shape[-1]
    whole = lambda *shape: pl.BlockSpec(shape, lambda s, pos: (0,) * len(shape))
    return pl.pallas_call(
        finish_kernel,
        out_shape=jax.ShapeDtypeStruct((rows, width, outs), BF16),
        grid_spec=pltpu.PrefetchScalarGridSpec(
            num_scalar_prefetch=1,
            grid=(1,),
            in_specs=[
                whole(slab, rows, width),
                whole(slab, rows, width),
                whole(2, slab, width),
                whole(2, slab, width),
                whole(2, slab, outs),
                whole(rows, width, outs),
            ],
            out_specs=whole(rows, width, outs),
        ),
        compiler_params=params(),
        cost_estimate=pl.CostEstimate(
            flops=2 * rows * width * 2 * slab * outs,
            bytes_accessed=8 * slab * rows * width + 6 * rows * width * outs,
            transcendentals=rows * width,
        ),
    )(pos, mixed, other, gain, bias, weights, gate)


def shards(
    pair,
    ln_gain,
    ln_bias,
    w_a_gate,
    w_a_proj,
    w_b_gate,
    w_b_proj,
    w_gate,
    out_gain,
    out_bias,
    w_out,
):
    rows, tokens, _ = pair.shape
    x_count, cores = lax.axis_size("x"), lax.axis_size("core")
    pos = jnp.stack([lax.axis_index("x"), lax.axis_index("core")]).astype(jnp.int32)
    width = tokens // x_count
    own_width = width // cores
    slab = w_a_gate.shape[1]

    weights = jnp.stack([w.T for w in (w_a_gate, w_a_proj, w_b_gate, w_b_proj)])
    weights = lax.all_gather(weights, "x", axis=1, tiled=True)
    half = x_count * slab
    left_weights = weights[:2].reshape(2 * half, -1)
    right_weights = weights[2:].reshape(2 * half, -1)

    normed = norm_columns(pos, pair, ln_gain, ln_bias, width)
    left = lax.all_to_all(project(normed, left_weights), "row", split_axis=0, concat_axis=0, tiled=True)
    left = lax.all_gather(left.reshape(tokens, width), "x")
    right = lax.all_to_all(project(normed, right_weights), "row", split_axis=0, concat_axis=0, tiled=True)
    right = right.reshape(tokens, width)
    gate = output_gate(pos, normed, w_gate, own_width)

    mixed = mix(pos, left, right, rows)
    mixed = lax.all_to_all(mixed, "row", split_axis=0, concat_axis=0, tiled=True)
    other = lax.ppermute(mixed[:, rows:], "core", [(0, 1), (1, 0)])

    def by_core(array):
        array = array.reshape(x_count, cores, slab, -1)
        return jnp.swapaxes(array, 0, 1).reshape(cores, half, -1)

    gain = jnp.broadcast_to(by_core(out_gain), (cores, half, own_width))
    bias = jnp.broadcast_to(by_core(out_bias), (cores, half, own_width))
    return finish(pos, mixed, other, gain, bias, by_core(w_out), gate)


def solution(mesh):
    cores = 2
    names = ("row", "x", "core")
    fine = Mesh(mesh.devices.reshape(mesh.devices.shape[0], -1, cores), names)
    chan = ("x", "core")
    in_specs = (
        P("row", None, None),
        P(),
        P(),
        P(None, chan),
        P(None, chan),
        P(None, chan),
        P(None, chan),
        P(),
        P(),
        P(),
        P(),
    )
    return jax.shard_map(shards, mesh=fine, in_specs=in_specs, out_specs=P("row", chan, None), check_vma=False)
```

time: 483 us -> 140 us (0.29); the launches traced: 476 us -> 139 us
  waiting for transfers between devices: 283 us -> 11.9 us
  matrix products: 89.8 us -> 0 us
  blocking collectives: 40.3 us -> 92.3 us
  local copies, waits for them, and re-layouts: 34.9 us -> 5.63 us
  other arithmetic: 14.4 us -> 0.82 us
  Pallas kernels: 0 us -> 9.84 us
  starting transfers between devices: 0.09 us -> 5.41 us
    all_gather x1, waiting for transfers between devices: 159 us -> 11.9 us  [shards(): left = lax.all_gather(left.reshape(tokens, width), 'x')]
    dot_general x7 -> x0, matrix products: 89.8 us -> none  [the longest x1 75.5 us: shards(): jnp.einsum('cki,ckj->cij', left_cols, lax.all_gather(right, 'row', axis=1...]
    psum x1 -> x0, waiting for transfers between devices: 66.3 us -> none  [shards(): lax.psum(second.astype(jnp.bfloat16), 'chan').astype(jnp.float32)]
    reduce_scatter x1 -> x0, waiting for transfers between devices: 57.7 us -> none  [shards(): lax.psum_scatter(jnp.einsum('cij,co->jio', scaled, out_part, preferred_el...]
    all_to_all x1 -> x3, blocking collectives: 40.3 us -> 82.2 us  [the longest x1 30.9 us: shards(): lax.all_to_all(project(normed, left_weights), 'row', split_axis=0, concat...]
    all_to_all x2 -> x0, local copies, waits for them, and re-layouts: 17.7 us -> none  [shards(): lax.all_to_all(left, 'row', split_axis=2, concat_axis=1, tiled=True)]
    all_gather x0 -> x1, blocking collectives: none -> 10.1 us  [shards(): weights = lax.all_gather(weights, 'x', axis=1, tiled=True)]
    pallas_call x0 -> x6, Pallas kernels: none -> 9.84 us  [the longest x1 2.52 us: mix(): pl.pallas_call(mix_kernel, out_shape=jax.ShapeDtypeStruct((slices * per,...]
  transfers between devices with their start and end apart: 3 -> 2, of which waited for: 3 -> 1; matrix products, arithmetic and copies ran while one was open for 6% -> 0% of each run, Pallas kernels for 0% -> 1%
where the time goes in v1:
time: 140 us; the launch traced here: 139 us
  blocking collectives  92.3 us (66%)
  between operations  13.5 us (10%)
  waiting for transfers between devices  11.9 us (8%)
  Pallas kernels  9.84 us (7%)
  local copies, waits for them, and re-layouts  5.63 us (4%)
  starting transfers between devices  5.41 us (4%)
    all_to_all x1, blocking collectives, shards(): lax.all_to_all(project(normed, left_weights), 'row', split_axis=0, concat...  30.9 us
    all_to_all x1, blocking collectives, shards(): lax.all_to_all(mixed, 'row', split_axis=0, concat_axis=0, tiled=True)  30 us
    all_to_all x1, blocking collectives, shards(): lax.all_to_all(project(normed, right_weights), 'row', split_axis=0, conca...  21.2 us
    all_gather x1, waiting for transfers between devices, shards(): left = lax.all_gather(left.reshape(tokens, width), 'x')  11.9 us
    all_gather x1, blocking collectives, shards(): weights = lax.all_gather(weights, 'x', axis=1, tiled=True)  10.1 us
    ppermute x1, starting transfers between devices, shards(): other = lax.ppermute(mixed[:, rows:], 'core', [(0, 1), (1, 0)])  5.41 us
    unnamed x16, local copies, waits for them, and re-layouts  5.1 us
  transfers between devices with their start and end apart: 2, of which 1 were waited for; matrix products, arithmetic and copies ran while one was open for 0% of the time, Pallas kernels for 1%

profile of v1, /device:TPU:1, one launch (start us, length us, event | category | flops | bytes accessed | tf_op | source)
XLA Modules:
  0.0 139.4 jit_solution(1978431992049053480)
XLA Ops:
  6.5 0.7 pad_maximum_fusion
  7.3 10.1 %all_gather.6 = bf16[4,64,128]{2,1,0:T(8,128)(2,1)S(1)} all-gather(bf16[4,16,128]{2,1,0:T(8,128)(2,1)S(1)} %pad_maximum_fusion), channel_id=1, replica_groups=mesh['row'=64,'x'=4,'core'=2] {'x'}, dimensions={1}, use_global_device_ids=true | all-gather | bytes 81920 | tf_op jit(solution)/shard_map/all_gather | solution.py:223
  17.4 0.1 pad_add_fusion.pos
  17.5 2.2 %copy-done = bf16[16,1024,128]{2,1,0:T(8,128)(2,1)S(1)} copy-done((bf16[16,1024,128]{2,1,0:T(8,128)(2,1)S(1)}, bf16[16,1024,128]{2,1,0:T(8,128)(2,1)}, u32[]{:S(2)}) %copy-start) | copy-done | bytes 4194328
  19.7 0.7 copy-done.3
  20.3 0.7 copy-done.4
  21.0 2.1 %shard_map.109.normed = bf16[16,256,128]{2,1,0:T(8,128)(2,1)S(1)} custom-call(s32[2]{0:T(128)S(1)} %pad_add_fusion.pos, bf16[16,1024,128]{2,1,0:T(8,128)(2,1)S(1)} %copy-done, f32[1,1,128]{2,1,0:T(1,128)S(1)} %bitcast.34, f32[1,1,128]{2,1,0:T(1,128)S(1)} %bitcast.35), custom_call_target="tpu_custom_call" | custom-call | flops 4194304 | bytes 2097152 | tf_op jit(solution)/shard_map/pallas_call | solution.py:30
  23.2 0.9 shard_map.110
  24.1 30.9 %all_to_all.15 = bf16[64,16,256]{2,1,0:T(8,128)(2,1)} all-to-all(bf16[64,16,256]{2,1,0:T(8,128)(2,1)S(1)} %shard_map.110), channel_id=1, replica_groups=mesh['row'=64,'x'=4,'core'=2] {'row'}, dimensions={0} | all-to-all | bytes 1048576 | tf_op jit(solution)/shard_map/all_to_all | solution.py:229
  55.0 0.9 shard_map.111
  55.9 21.2 %all_to_all.16 = bf16[64,16,256]{2,1,0:T(8,128)(2,1)S(1)} all-to-all(bf16[64,16,256]{2,1,0:T(8,128)(2,1)S(1)} %shard_map.111), channel_id=1, replica_groups=mesh['row'=64,'x'=4,'core'=2] {'row'}, dimensions={0} | all-to-all | bytes 1048576 | tf_op jit(solution)/shard_map/all_to_all | solution.py:231
  77.2 11.9 %all-gather.2.cloned.1.call-done.left = bf16[4,1024,256]{2,1,0:T(8,128)(2,1)} async-done(((bf16[1,1024,256]{2,1,0:T(8,128)(2,1)}), bf16[4,1024,256]{2,1,0:T(8,128)(2,1)}) %all-gather.2.cloned.1.call-update) | async-done | bytes 2097168 | tf_op jit(solution)/shard_map/all_gather | solution.py:230
  89.1 1.6 %copy-done.1 = bf16[4,1024,256]{2,1,0:T(8,128)(2,1)S(1)} copy-done((bf16[4,1024,256]{2,1,0:T(8,128)(2,1)S(1)}, bf16[4,1024,256]{2,1,0:T(8,128)(2,1)}, u32[]{:S(2)}) %copy-start.1) | copy-done | bytes 2097176
  90.7 2.5 %shard_map.112 = bf16[64,32,128]{2,1,0:T(8,128)(2,1)S(1)} custom-call(s32[2]{0:T(128)S(1)} %pad_add_fusion.pos, bf16[4,1024,256]{2,1,0:T(8,128)(2,1)S(1)} %copy-done.1, bf16[1024,256]{1,0:T(8,128)(2,1)S(1)} %bitcast.30), custom_call_target="tpu_custom_call" | custom-call | flops 536870912 | bytes 3145728 | tf_op jit(solution)/shard_map/pallas_call | solution.py:130
  93.2 30.0 %all_to_all.17.own = bf16[64,32,128]{2,1,0:T(8,128)(2,1)S(1)} all-to-all(bf16[64,32,128]{2,1,0:T(8,128)(2,1)S(1)} %shard_map.112), channel_id=1, replica_groups=mesh['row'=64,'x'=4,'core'=2] {'row'}, dimensions={0} | all-to-all | bytes 1048576 | tf_op jit(solution)/shard_map/all_to_all | solution.py:236
  123.2 5.4 %collective-permute-start = (bf16[64,16,128]{2,1,0:T(8,128)(2,1)S(1)}, bf16[64,16,128]{2,1,0:T(8,128)(2,1)S(1)}, u32[]{:S(2)}, u32[]{:S(2)}) collective-permute-start(bf16[64,16,128]{2,1,0:T(8,128)(2,1)S(1)} %slice.14), channel_id=1, source_target_pairs={{0,1},{1,0},{2,3},{3,2},{4,5},{5,4},{6,7},{7,6},{8,9},{9,8},{10,11... | collective-permute-start | bytes 786440 | tf_op jit(solution)/shard_map/ppermute | solution.py:237
  128.7 0.1 reshape.36
  128.8 0.1 broadcast_in_dim.14
  128.8 0.1 reshape.37
  128.9 0.1 broadcast_in_dim.16
  129.1 1.1 shard_map.113.gate
  130.1 0.1 broadcast_in_dim.15.gain
  130.2 0.1 broadcast_in_dim.17.bias
  130.3 2.3 %shard_map.114 = bf16[16,128,128]{2,1,0:T(8,128)(2,1)} custom-call(s32[2]{0:T(128)S(1)} %pad_add_fusion.pos, bf16[64,32,128]{2,1,0:T(8,128)(2,1)S(1)} %all_to_all.17.own, bf16[64,16,128]{2,1,0:T(8,128)(2,1)S(1)} %collective-permute-done.other, f32[2,64,128]{2,1,0:T(8,128)S(1)} %broadcast_in_dim.15.gain, f32[2,64,128]{2,1,0:T(8,128)S(1)} %broadcast_in_dim.17.bias, ...), custom_call_target="tpu_custom_call" | custom-call | flops 67108864 | bytes 2621440 | tf_op jit(solution)/shard_map/pallas_call | solution.py:177
  (20 shorter events, 0.1 us)
Async XLA Ops:
  6.5 82.6 %all-gather.2.cloned.1.call-start = ((), (), s32[]{:S(2)}) async-start(), calls=%async_computation.3 | async-start | bytes 2621440 | tf_op jit(solution)/shard_map/all_gather | solution.py:230
  17.5 2.2 %copy-start = (bf16[16,1024,128]{2,1,0:T(8,128)(2,1)S(1)}, bf16[16,1024,128]{2,1,0:T(8,128)(2,1)}, u32[]{:S(2)}) copy-start(bf16[16,1024,128]{2,1,0:T(8,128)(2,1)} %pair.1) | copy-start | bytes 12582916
  19.7 0.7 copy-start.3
  20.3 0.7 copy-start.4
  55.0 73.7 %copy-start.6 = (f32[128]{0:T(128)S(1)}, f32[128]{0:T(128)}, u32[]{:S(2)}) copy-start(f32[128]{0:T(128)} %param.19) | copy-start | bytes 1540
  55.0 73.9 %copy-start.7 = (f32[128]{0:T(128)S(1)}, f32[128]{0:T(128)}, u32[]{:S(2)}) copy-start(f32[128]{0:T(128)} %param.20) | copy-start | bytes 1540
  55.0 74.0 %copy-start.5 = (bf16[128,128]{1,0:T(8,128)(2,1)S(1)}, bf16[128,128]{1,0:T(8,128)(2,1)}, u32[]{:S(2)}) copy-start(bf16[128,128]{1,0:T(8,128)(2,1)} %param.21) | copy-start | bytes 98308
  55.0 74.0 %copy-start.2 = (bf16[128,128]{1,0:T(8,128)(2,1)S(1)}, bf16[128,128]{1,0:T(8,128)(2,1)}, u32[]{:S(2)}) copy-start(bf16[128,128]{1,0:T(8,128)(2,1)} %weights.1) | copy-start | bytes 98308
  89.1 1.6 %copy-start.1 = (bf16[4,1024,256]{2,1,0:T(8,128)(2,1)S(1)}, bf16[4,1024,256]{2,1,0:T(8,128)(2,1)}, u32[]{:S(2)}) copy-start(bf16[4,1024,256]{2,1,0:T(8,128)(2,1)} %all-gather.2.cloned.1.call-done.left) | copy-start | bytes 6291460
  123.2 6.9 %collective-permute-start = (bf16[64,16,128]{2,1,0:T(8,128)(2,1)S(1)}, bf16[64,16,128]{2,1,0:T(8,128)(2,1)S(1)}, u32[]{:S(2)}, u32[]{:S(2)}) collective-permute-start(bf16[64,16,128]{2,1,0:T(8,128)(2,1)S(1)} %slice.14), channel_id=1, source_target_pairs={{0,1},{1,0},{2,3},{3,2},{4,5},{5,4},{6,7},{7,6},{8,9},{9,8},{10,11... | collective-permute-start | bytes 786440 | tf_op jit(solution)/shard_map/ppermute | solution.py:237
Sparse Core Ops, SparseCore 0:
  55.1 33.8 all-gather.1

commit v2 on v0

v2 whole, which is shorter than its diff:
```python
import jax
import jax.numpy as jnp
from jax import lax
from jax.experimental import pallas as pl
from jax.experimental.pallas import tpu as pltpu
from jax.sharding import Mesh
from jax.sharding import PartitionSpec as P

F32 = jnp.float32
BF16 = jnp.bfloat16
VMEM_LIMIT = 32 * 1024 * 1024
LARGE_LIMIT = 57 * 1024 * 1024
EPS = 1e-05
LANES = 128
SIDE = (0, 1, 1, 0)
NEXT = ((0, 1), (1, 0), (2, 3), (3, 2))
PAIRS = ((0, 3), (1, 2))
SWAP = ((0, 1), (1, 0))


def params(limit=VMEM_LIMIT):
    return pltpu.CompilerParams(vmem_limit_bytes=limit)


def whole(*shape):
    return pl.BlockSpec(shape, lambda s, pos: (0,) * len(shape))


def norm_kernel(pos, pair, gain, bias, out, held, sems):
    rows = pair.shape[0] // 2
    copies = []
    for part in range(4):
        row, side = part // 2 * rows, part % 2
        at = pl.multiple_of(pos[side] * LANES, LANES)
        copies.append(
            pltpu.make_async_copy(pair.at[pl.ds(row, rows), pl.ds(at, LANES), :], held.at[part], sems.at[part])
        )
    for copy in copies:
        copy.start()
    for part, copy in enumerate(copies):
        copy.wait()
        row, side = part // 2 * rows, part % 2
        values = held[part].astype(F32)
        mean = jnp.mean(values, axis=-1, keepdims=True)
        centred = values - mean
        var = jnp.mean(centred * centred, axis=-1, keepdims=True)
        normed = centred * lax.rsqrt(var + EPS) * gain[...] + bias[...]
        out[row : row + rows, side * LANES : (side + 1) * LANES, :] = normed.astype(BF16)


def norm_columns(pos, pair, gain, bias):
    rows, _, chans = pair.shape
    return pl.pallas_call(
        norm_kernel,
        out_shape=jax.ShapeDtypeStruct((rows, 2 * LANES, chans), BF16),
        grid_spec=pltpu.PrefetchScalarGridSpec(
            num_scalar_prefetch=1,
            grid=(1,),
            in_specs=[pl.BlockSpec(memory_space=pltpu.HBM), whole(1, 1, chans), whole(1, 1, chans)],
            out_specs=whole(rows, 2 * LANES, chans),
            scratch_shapes=[pltpu.VMEM((4, rows // 2, LANES, chans), BF16), pltpu.SemaphoreType.DMA((4,))],
        ),
        compiler_params=params(LARGE_LIMIT),
        cost_estimate=pl.CostEstimate(
            flops=16 * rows * LANES * chans, bytes_accessed=8 * rows * LANES * chans, transcendentals=2 * rows * LANES
        ),
    )(pos, pair, gain.reshape(1, 1, chans), bias.reshape(1, 1, chans))


def project_kernel(pos, normed, own, core, near, far, out, held):
    for place, part in enumerate((own, core, near, far)):
        held[0, pos[4 + place]] = part[0]
        held[1, pos[4 + place]] = part[1]
    rows, width, chans = normed.shape
    slab = held.shape[1] * held.shape[2]
    flat = normed[...].reshape(rows * width, chans)
    weights = held[...].reshape(2 * slab, chans)
    both = lax.dot_general(weights, flat, (((1,), (1,)), ((), ())), preferred_element_type=F32)
    value = jax.nn.sigmoid(both[:slab]) * both[slab:]
    parts = [value[:, k * width : (k + 1) * width] for k in range(rows)]
    out[...] = jnp.swapaxes(jnp.stack(parts, axis=0), 0, 1).astype(BF16)


def project(pos, normed, weights, which):
    rows, width, chans = normed.shape
    small = weights[0].shape[1]
    slab = 4 * small
    part = pl.BlockSpec((2, small, chans), lambda s, pos: (which, 0, 0))
    return pl.pallas_call(
        project_kernel,
        out_shape=jax.ShapeDtypeStruct((slab, rows, width), BF16),
        grid_spec=pltpu.PrefetchScalarGridSpec(
            num_scalar_prefetch=1,
            grid=(width // LANES,),
            in_specs=[pl.BlockSpec((rows, LANES, chans), lambda s, pos: (0, s, 0)), part, part, part, part],
            out_specs=pl.BlockSpec((slab, rows, LANES), lambda s, pos: (0, 0, s)),
            scratch_shapes=[pltpu.VMEM((2, 4, small, chans), BF16)],
        ),
        compiler_params=params(),
        cost_estimate=pl.CostEstimate(
            flops=4 * rows * width * slab * chans,
            bytes_accessed=2 * rows * width * (slab + chans),
            transcendentals=rows * width * slab,
        ),
    )(pos, normed, *weights)


def gate_kernel(pos, normed, weights, out):
    rows, width, chans = normed.shape
    flat = normed[...].reshape(rows * width, chans)
    got = jnp.dot(flat, weights[...], preferred_element_type=F32)
    out[...] = jax.nn.sigmoid(got).reshape(rows, width, chans)


def output_gate(pos, normed, weights):
    rows, _, chans = normed.shape
    step = rows // 2
    return pl.pallas_call(
        gate_kernel,
        out_shape=jax.ShapeDtypeStruct((rows, LANES, chans), F32),
        grid_spec=pltpu.PrefetchScalarGridSpec(
            num_scalar_prefetch=1,
            grid=(2,),
            in_specs=[pl.BlockSpec((step, LANES, chans), lambda s, pos: (s, pos[2], 0)), whole(chans, chans)],
            out_specs=pl.BlockSpec((step, LANES, chans), lambda s, pos: (s, 0, 0)),
        ),
        compiler_params=params(),
        cost_estimate=pl.CostEstimate(
            flops=2 * rows * LANES * chans * chans,
            bytes_accessed=6 * rows * LANES * chans,
            transcendentals=rows * LANES * chans,
        ),
    )(pos, normed, weights)


def mix_kernel(pos, right, own, core, near, far, out):
    per = LANES // out.shape[2]
    for place, left in enumerate((own, core, near, far)):
        mixed = lax.dot_general(left[...], right[...], (((0,), (0,)), ((), ())), preferred_element_type=F32)
        mixed = mixed.astype(BF16)
        for side in range(2):
            at = pos[8 + 2 * place + side] * per
            for half in range(2):
                block = mixed[side * LANES : (side + 1) * LANES, half * LANES : (half + 1) * LANES]
                out[pl.ds(at, per), half] = block.reshape(per, out.shape[2], LANES)


def mix(pos, right, lefts, rows):
    depth, width = right.shape
    tokens = 4 * width
    return pl.pallas_call(
        mix_kernel,
        out_shape=jax.ShapeDtypeStruct((tokens // rows, 2, rows, LANES), BF16),
        grid_spec=pltpu.PrefetchScalarGridSpec(
            num_scalar_prefetch=1,
            grid=(1,),
            in_specs=[whole(depth, width)] * 5,
            out_specs=whole(tokens // rows, 2, rows, LANES),
        ),
        compiler_params=params(),
        cost_estimate=pl.CostEstimate(
            flops=2 * depth * tokens * width, bytes_accessed=2 * (5 * depth * width + tokens * width), transcendentals=0
        ),
    )(pos, right, *lefts)


def finish_kernel(mixed, gain, bias, weights, gate, out):
    chans, rows, _ = mixed.shape
    values = mixed[...].astype(F32)
    values = values - (jnp.sum(values, axis=0) / chans)[None]
    scale = lax.rsqrt(jnp.sum(values * values, axis=0) / chans + EPS)
    scaled = jnp.swapaxes(values * scale[None], 0, 1)
    scaled = (scaled * gain[...][None] + bias[...][None]).astype(BF16)
    for row in range(rows):
        proj = lax.dot_general(
            scaled[row], weights[...], (((0,), (0,)), ((), ())), preferred_element_type=F32
        )
        out[row] = (proj * gate[row]).astype(BF16)


def finish(mixed, gain, bias, weights, gate):
    chans, rows, width = mixed.shape
    return pl.pallas_call(
        finish_kernel,
        out_shape=jax.ShapeDtypeStruct((rows, width, weights.shape[1]), BF16),
        compiler_params=params(),
        cost_estimate=pl.CostEstimate(
            flops=2 * rows * width * chans * chans, bytes_accessed=8 * chans * rows * width, transcendentals=rows * width
        ),
    )(mixed, gain, bias, weights, gate)


def positions(x, core):
    a = x // 2
    b = jnp.where(a == 0, x, 3 - x)
    slot = 2 * (x % 2) + core
    blocks = []
    for other_b, other_core in ((b, core), (b, 1 - core), (1 - b, core), (1 - b, 1 - core)):
        blocks += [2 * other_b + other_core, 2 * (3 - other_b) + other_core]
    slots = [slot, 2 * (x % 2) + 1 - core, 2 * (1 - x % 2) + core, 2 * (1 - x % 2) + 1 - core]
    return jnp.stack([blocks[0], blocks[1], a, a] + slots + blocks).astype(jnp.int32)


def shards(
    pair,
    ln_gain,
    ln_bias,
    w_a_gate,
    w_a_proj,
    w_b_gate,
    w_b_proj,
    w_gate,
    out_gain,
    out_bias,
    w_out,
):
    rows, tokens, chans = pair.shape
    depth = lax.axis_size("row")
    pos = positions(lax.axis_index("x"), lax.axis_index("core"))

    own = jnp.stack([w.T for w in (w_a_gate, w_a_proj, w_b_gate, w_b_proj)])
    diagonal = [(2 * f + c, 2 * t + 1 - c) for f, t in NEXT for c in range(2)]
    weights = [
        own,
        lax.ppermute(own, "core", SWAP),
        lax.ppermute(own, "x", NEXT),
        lax.ppermute(own, ("x", "core"), diagonal),
    ]
    normed = norm_columns(pos, pair, ln_gain, ln_bias)

    def spread(operand):
        return lax.all_to_all(operand, "row", split_axis=0, concat_axis=0, tiled=True).reshape(tokens, -1)

    left = spread(project(pos, normed, weights, 0))
    right = project(pos, normed, weights, 1)
    left, right = lax.optimization_barrier((left, right))
    near = lax.ppermute(left, "x", NEXT)
    core = lax.ppermute(left, "core", SWAP)
    right = spread(right)
    near, normed, out_gain, out_bias, w_out, right = lax.optimization_barrier(
        (near, normed, out_gain, out_bias, w_out, right)
    )
    far = lax.ppermute(near, "core", SWAP)

    def in_order(array):
        return jnp.swapaxes(array.reshape(2, depth, -1), 0, 1).reshape(2 * depth, -1)

    gate = output_gate(pos, normed, w_gate)
    gain = jnp.broadcast_to(in_order(out_gain), (2 * depth, LANES))
    bias = jnp.broadcast_to(in_order(out_bias), (2 * depth, LANES))
    out_weights = in_order(w_out)
    right, gate, gain, bias, out_weights = lax.optimization_barrier((right, gate, gain, bias, out_weights))

    mixed = mix(pos, right, (left, core, near, far), rows).reshape(2 * depth, rows, LANES)
    groups = [[4 * row + x for row in range(depth) for x in pair_of] for pair_of in PAIRS]
    mixed = lax.all_to_all(
        mixed, ("row", "x"), split_axis=0, concat_axis=0, tiled=True, axis_index_groups=groups
    )

    return finish(mixed, gain, bias, out_weights, gate)


def solution(mesh):
    fine = Mesh(mesh.devices.reshape(mesh.devices.shape[0], -1, 2), ("row", "x", "core"))
    chan = ("x", "core")
    in_specs = (
        P("row", None, None),
        P(),
        P(),
        P(None, chan),
        P(None, chan),
        P(None, chan),
        P(None, chan),
        P(),
        P(),
        P(),
        P(),
    )
    return jax.shard_map(shards, mesh=fine, in_specs=in_specs, out_specs=P("row", chan, None), check_vma=False)
```

time: 483 us -> 120 us (0.25)
  waiting for transfers between devices: 283 us -> 24.2 us
  matrix products: 89.8 us -> 0 us
  starting transfers between devices: 0.09 us -> 44.4 us
  local copies, waits for them, and re-layouts: 34.9 us -> 3.96 us
  Pallas kernels: 0 us -> 14.2 us
  other arithmetic: 14.4 us -> 0.74 us
  between operations: 13.7 us -> 0.26 us
  blocking collectives: 40.3 us -> 29.7 us
    all_gather x1 -> x0, waiting for transfers between devices: 159 us -> none  [shards(): lax.all_gather(right, 'row', axis=1, tiled=True)]
    dot_general x7 -> x0, matrix products: 89.8 us -> none  [the longest x1 75.5 us: shards(): jnp.einsum('cki,ckj->cij', left_cols, lax.all_gather(right, 'row', axis=1...]
    psum x1 -> x0, waiting for transfers between devices: 66.3 us -> none  [shards(): lax.psum(second.astype(jnp.bfloat16), 'chan').astype(jnp.float32)]
    reduce_scatter x1 -> x0, waiting for transfers between devices: 57.7 us -> none  [shards(): lax.psum_scatter(jnp.einsum('cij,co->jio', scaled, out_part, preferred_el...]
    ppermute x0 -> x6, starting transfers between devices: none -> 27.1 us  [the longest x1 8.77 us: shards(): lax.ppermute(own, 'core', SWAP)]
    all_to_all x2 -> x0, local copies, waits for them, and re-layouts: 17.7 us -> none  [shards(): lax.all_to_all(left, 'row', split_axis=2, concat_axis=1, tiled=True)]
    all_to_all x0 -> x2, starting transfers between devices: none -> 17.3 us  [spread(): lax.all_to_all(operand, 'row', split_axis=0, concat_axis=0, tiled=True)]
    all_to_all x0 -> x2, waiting for transfers between devices: none -> 17.2 us  [spread(): lax.all_to_all(operand, 'row', split_axis=0, concat_axis=0, tiled=True)]
  transfers between devices with their start and end apart: 3 -> 8, of which waited for: 3 -> 3; matrix products, arithmetic and copies ran while one was open for 6% -> 1% of each run, Pallas kernels for 0% -> 7%
where the time goes in v2:
time: 120 us; the launch traced here: 117 us
  starting transfers between devices  44.4 us (37%)
  blocking collectives  29.7 us (25%)
  waiting for transfers between devices  24.2 us (20%)
  Pallas kernels  14.2 us (12%)
  local copies, waits for them, and re-layouts  3.96 us (3%)
    all_to_all x1, blocking collectives, shards(): lax.all_to_all(mixed, ('row', 'x'), split_axis=0, concat_axis=0, tiled=Tr...  29.7 us
    all_to_all x2, starting transfers between devices, spread(): lax.all_to_all(operand, 'row', split_axis=0, concat_axis=0, tiled=True)  17.3 us
    all_to_all x2, waiting for transfers between devices, spread(): lax.all_to_all(operand, 'row', split_axis=0, concat_axis=0, tiled=True)  17.2 us
    ppermute x1, starting transfers between devices, shards(): lax.ppermute(own, 'core', SWAP)  8.77 us
    ppermute x1, waiting for transfers between devices, shards(): near = lax.ppermute(left, 'x', NEXT)  6.95 us
    ppermute x1, starting transfers between devices, shards(): far = lax.ppermute(near, 'core', SWAP)  6.06 us
    pallas_call x1, Pallas kernels, norm_columns(): pl.pallas_call(norm_kernel, out_shape=jax.ShapeDtypeStruct((rows, 2 * LAN...  4.87 us
    pallas_call x2, Pallas kernels, project(): pl.pallas_call(project_kernel, out_shape=jax.ShapeDtypeStruct((slab, rows...  4.14 us
  transfers between devices with their start and end apart: 8, of which 3 were waited for; matrix products, arithmetic and copies ran while one was open for 1% of the time, Pallas kernels for 7%

profile of v2, /device:TPU:1, one launch (start us, length us, event | category | flops | bytes accessed | tf_op | source)
XLA Modules:
  0.0 117.4 jit_solution(5382895797159570414)
XLA Ops:
  0.0 0.7 pad_maximum_fusion.own
  0.7 8.8 %collective-permute-start = (bf16[4,16,128]{2,1,0:T(8,128)(2,1)S(1)}, bf16[4,16,128]{2,1,0:T(8,128)(2,1)S(1)}, u32[]{:S(2)}, u32[]{:S(2)}) collective-permute-start(bf16[4,16,128]{2,1,0:T(8,128)(2,1)S(1)} %pad_maximum_fusion.own), channel_id=1, source_target_pairs={{0,1},{1,0},{2,3},{3,2},{4,5},{5,4},{6,7},{7,6},{8,9},{9,8},{10,11... | collective-permute-start | bytes 49160 | tf_op jit(solution)/shard_map/ppermute | solution.py:225
  9.5 1.9 %collective-permute-start.1 = (bf16[4,16,128]{2,1,0:T(8,128)(2,1)S(1)}, bf16[4,16,128]{2,1,0:T(8,128)(2,1)S(1)}, u32[]{:S(2)}, u32[]{:S(2)}) collective-permute-start(bf16[4,16,128]{2,1,0:T(8,128)(2,1)S(1)} %pad_maximum_fusion.own), channel_id=1, source_target_pairs={{0,2},{2,0},{4,6},{6,4},{1,3},{3,1},{5,7},{7,5},{8,10},{10,8},{12,... | collective-permute-start | bytes 49160 | tf_op jit(solution)/shard_map/ppermute | solution.py:226
  11.5 3.5 %collective-permute-start.2 = (bf16[4,16,128]{2,1,0:T(8,128)(2,1)S(1)}, bf16[4,16,128]{2,1,0:T(8,128)(2,1)S(1)}, u32[]{:S(2)}, u32[]{:S(2)}) collective-permute-start(bf16[4,16,128]{2,1,0:T(8,128)(2,1)S(1)} %pad_maximum_fusion.own), channel_id=1, source_target_pairs={{0,3},{1,2},{2,1},{3,0},{4,7},{5,6},{6,5},{7,4},{8,11},{9,10},{10,... | collective-permute-start | bytes 49160 | tf_op jit(solution)/shard_map/ppermute | solution.py:227
  15.0 0.7 stack.73.pos
  15.7 4.9 %shard_map.109.normed = bf16[16,256,128]{2,1,0:T(8,128)(2,1)} custom-call(s32[16]{0:T(128)} %stack.73.pos, bf16[16,1024,128]{2,1,0:T(8,128)(2,1)} %pair.1, f32[1,1,128]{2,1,0:T(1,128)} %bitcast.53, f32[1,1,128]{2,1,0:T(1,128)} %bitcast.54), custom_call_target="tpu_custom_call" | custom-call | flops 4194304 | bytes 2097152 | tf_op jit(solution)/shard_map/pallas_call | solution.py:53
  20.7 1.2 %copy-done = bf16[16,256,128]{2,1,0:T(8,128)(2,1)S(1)} copy-done((bf16[16,256,128]{2,1,0:T(8,128)(2,1)S(1)}, bf16[16,256,128]{2,1,0:T(8,128)(2,1)}, u32[]{:S(2)}) %copy-start) | copy-done | bytes 1048600
  21.9 2.1 %shard_map.110 = bf16[64,16,256]{2,1,0:T(8,128)(2,1)} custom-call(s32[16]{0:T(128)S(1)} %copy-done.4, bf16[16,256,128]{2,1,0:T(8,128)(2,1)S(1)} %copy-done, bf16[4,16,128]{2,1,0:T(8,128)(2,1)S(1)} %pad_maximum_fusion.own, bf16[4,16,128]{2,1,0:T(8,128)(2,1)S(1)} %collective-permute-done.core, bf16[4,16,128]{2,1,0:T(8,128)(2,1)S(1)} %collective-permute-done.1.near, ...), custom_call_target="tpu_custom_call" | custom-call | flops 134217728 | bytes 1572864 | tf_op jit(solution)/shard_map/pallas_call | solution.py:89
  24.0 10.9 %all-to-all-start = ((bf16[64,16,256]{2,1,0:T(8,128)(2,1)}), bf16[64,16,256]{2,1,0:T(8,128)(2,1)S(1)}, u32[]{:S(2)}, u32[]{:S(2)}) async-start(bf16[64,16,256]{2,1,0:T(8,128)(2,1)} %shard_map.110), calls=%async_computation | async-start | bytes 1048576 | tf_op jit(solution)/shard_map/all_to_all | solution.py:232
  34.9 1.2 %copy-done.1 = bf16[16,256,128]{2,1,0:T(8,128)(2,1)S(1)} copy-done((bf16[16,256,128]{2,1,0:T(8,128)(2,1)S(1)}, bf16[16,256,128]{2,1,0:T(8,128)(2,1)}, u32[]{:S(2)}) %copy-start.1) | copy-done | bytes 1048600
  36.1 2.1 %shard_map.111 = bf16[64,16,256]{2,1,0:T(8,128)(2,1)} custom-call(s32[16]{0:T(128)S(1)} %copy-done.4, bf16[16,256,128]{2,1,0:T(8,128)(2,1)S(1)} %copy-done.1, bf16[4,16,128]{2,1,0:T(8,128)(2,1)S(1)} %pad_maximum_fusion.own, bf16[4,16,128]{2,1,0:T(8,128)(2,1)S(1)} %collective-permute-done.core, bf16[4,16,128]{2,1,0:T(8,128)(2,1)S(1)} %collective-permute-done.1.near, ...), custom_call_target="tpu_custom_call" | custom-call | flops 134217728 | bytes 1572864 | tf_op jit(solution)/shard_map/pallas_call | solution.py:89
  38.2 14.6 %all-to-all-done = bf16[64,16,256]{2,1,0:T(8,128)(2,1)S(1)} async-done(((bf16[64,16,256]{2,1,0:T(8,128)(2,1)}), bf16[64,16,256]{2,1,0:T(8,128)(2,1)S(1)}, u32[]{:S(2)}, u32[]{:S(2)}) %all-to-all-start) | async-done | bytes 524320 | tf_op jit(solution)/shard_map/all_to_all | solution.py:232
  52.8 6.3 %all-to-all-start.1 = ((bf16[64,16,256]{2,1,0:T(8,128)(2,1)}), bf16[64,16,256]{2,1,0:T(8,128)(2,1)S(1)}, u32[]{:S(2)}, u32[]{:S(2)}) async-start(bf16[64,16,256]{2,1,0:T(8,128)(2,1)} %shard_map.111), calls=%async_computation.1 | async-start | bytes 1048576 | tf_op jit(solution)/shard_map/all_to_all | solution.py:232
  59.1 3.1 %collective-permute-start.3 = (bf16[1024,256]{1,0:T(8,128)(2,1)S(1)}, bf16[1024,256]{1,0:T(8,128)(2,1)S(1)}, u32[]{:S(2)}, u32[]{:S(2)}) collective-permute-start(bf16[1024,256]{1,0:T(8,128)(2,1)S(1)} %bitcast.40), channel_id=1, source_target_pairs={{0,2},{2,0},{4,6},{6,4},{1,3},{3,1},{5,7},{7,5},{8,10},{10,8},{12,... | collective-permute-start | bytes 1572872 | tf_op jit(solution)/shard_map/ppermute | solution.py:237
  62.2 3.7 %collective-permute-start.4 = (bf16[1024,256]{1,0:T(8,128)(2,1)S(1)}, bf16[1024,256]{1,0:T(8,128)(2,1)S(1)}, u32[]{:S(2)}, u32[]{:S(2)}) collective-permute-start(bf16[1024,256]{1,0:T(8,128)(2,1)S(1)} %bitcast.41), channel_id=1, source_target_pairs={{0,1},{1,0},{2,3},{3,2},{4,5},{5,4},{6,7},{7,6},{8,9},{9,8},{10,11... | collective-permute-start | bytes 1572872 | tf_op jit(solution)/shard_map/ppermute | solution.py:238
  66.0 6.9 %collective-permute-done.3.near = bf16[1024,256]{1,0:T(8,128)(2,1)S(1)} collective-permute-done((bf16[1024,256]{1,0:T(8,128)(2,1)S(1)}, bf16[1024,256]{1,0:T(8,128)(2,1)S(1)}, u32[]{:S(2)}, u32[]{:S(2)}) %collective-permute-start.3) | collective-permute-done | bytes 524320 | tf_op jit(solution)/shard_map/ppermute | solution.py:237
  72.9 2.6 %all-to-all-done.1 = bf16[64,16,256]{2,1,0:T(8,128)(2,1)S(1)} async-done(((bf16[64,16,256]{2,1,0:T(8,128)(2,1)}), bf16[64,16,256]{2,1,0:T(8,128)(2,1)S(1)}, u32[]{:S(2)}, u32[]{:S(2)}) %all-to-all-start.1) | async-done | bytes 524320 | tf_op jit(solution)/shard_map/all_to_all | solution.py:232
  75.5 6.1 %collective-permute-start.5 = (bf16[1024,256]{1,0:T(8,128)(2,1)S(1)}, bf16[1024,256]{1,0:T(8,128)(2,1)}, u32[]{:S(2)}, u32[]{:S(2)}) collective-permute-start(bf16[1024,256]{1,0:T(8,128)(2,1)S(1)} %collective-permute-done.3.near), channel_id=1, source_target_pairs={{0,1},{1,0},{2,3},{3,2},{4,5},{5,4},{6,7},{7,6},{8,9},{9,8},{10,11... | collective-permute-start | bytes 1572872 | tf_op jit(solution)/shard_map/ppermute | solution.py:243
  81.8 0.1 broadcast_in_dim.14
  82.1 0.1 broadcast_in_dim.16
  82.3 1.1 shard_map.112.gate
  83.6 2.3 %shard_map.113 = bf16[64,2,16,128]{3,2,1,0:T(8,128)(2,1)S(1)} custom-call(s32[16]{0:T(128)S(1)} %copy-done.4, bf16[1024,256]{1,0:T(8,128)(2,1)S(1)} %bitcast.43, bf16[1024,256]{1,0:T(8,128)(2,1)S(1)} %bitcast.42, bf16[1024,256]{1,0:T(8,128)(2,1)S(1)} %collective-permute-done.4.core, bf16[1024,256]{1,0:T(8,128)(2,1)S(1)} %collective-permute-done.3.near, ...), custom_call_target="tpu_custom_call" | custom-call | flops 536870912 | bytes 3145728 | tf_op jit(solution)/shard_map/pallas_call | solution.py:151
  85.9 29.7 %all_to_all.15.mixed = bf16[128,16,128]{2,1,0:T(8,128)(2,1)S(1)} all-to-all(bf16[128,16,128]{2,1,0:T(8,128)(2,1)S(1)} %bitcast.44), channel_id=1, replica_groups={{0,6,8,14,16,22,24,30,32,38,40,46,48,54,56,62,64,70,72,78,80,86,88,94,9..., dimensions={0} | all-to-all | bytes 1048576 | tf_op jit(solution)/shard_map/all_to_all | solution.py:256
  115.6 1.8 %shard_map.114 = bf16[16,128,128]{2,1,0:T(8,128)(2,1)} custom-call(bf16[128,16,128]{2,1,0:T(8,128)(2,1)S(1)} %all_to_all.15.mixed, f32[128,128]{1,0:T(8,128)S(1)} %broadcast_in_dim.15.gain, f32[128,128]{1,0:T(8,128)S(1)} %broadcast_in_dim.17.bias, bf16[128,128]{1,0:T(8,128)(2,1)S(1)} %bitcast.45, f32[16,128,128]{2,1,0:T(8,128)S(1)} %shard_map.112.gate), custom_call_target="tpu_custom_call" | custom-call | flops 67108864 | bytes 2097152 | tf_op jit(solution)/shard_map/pallas_call | solution.py:183
  (26 shorter events, 0.6 us)
Async XLA Ops:
  0.7 19.9 %collective-permute-start = (bf16[4,16,128]{2,1,0:T(8,128)(2,1)S(1)}, bf16[4,16,128]{2,1,0:T(8,128)(2,1)S(1)}, u32[]{:S(2)}, u32[]{:S(2)}) collective-permute-start(bf16[4,16,128]{2,1,0:T(8,128)(2,1)S(1)} %pad_maximum_fusion.own), channel_id=1, source_target_pairs={{0,1},{1,0},{2,3},{3,2},{4,5},{5,4},{6,7},{7,6},{8,9},{9,8},{10,11... | collective-permute-start | bytes 49160 | tf_op jit(solution)/shard_map/ppermute | solution.py:225
  9.5 11.1 %collective-permute-start.1 = (bf16[4,16,128]{2,1,0:T(8,128)(2,1)S(1)}, bf16[4,16,128]{2,1,0:T(8,128)(2,1)S(1)}, u32[]{:S(2)}, u32[]{:S(2)}) collective-permute-start(bf16[4,16,128]{2,1,0:T(8,128)(2,1)S(1)} %pad_maximum_fusion.own), channel_id=1, source_target_pairs={{0,2},{2,0},{4,6},{6,4},{1,3},{3,1},{5,7},{7,5},{8,10},{10,8},{12,... | collective-permute-start | bytes 49160 | tf_op jit(solution)/shard_map/ppermute | solution.py:226
  11.5 9.2 %collective-permute-start.2 = (bf16[4,16,128]{2,1,0:T(8,128)(2,1)S(1)}, bf16[4,16,128]{2,1,0:T(8,128)(2,1)S(1)}, u32[]{:S(2)}, u32[]{:S(2)}) collective-permute-start(bf16[4,16,128]{2,1,0:T(8,128)(2,1)S(1)} %pad_maximum_fusion.own), channel_id=1, source_target_pairs={{0,3},{1,2},{2,1},{3,0},{4,7},{5,6},{6,5},{7,4},{8,11},{9,10},{10,... | collective-permute-start | bytes 49160 | tf_op jit(solution)/shard_map/ppermute | solution.py:227
  15.7 4.9 %copy-start.4 = (s32[16]{0:T(128)S(1)}, s32[16]{0:T(128)}, u32[]{:S(2)}) copy-start(s32[16]{0:T(128)} %stack.73.pos) | copy-start | bytes 196
  15.7 65.9 %copy-start.6 = (f32[128]{0:T(128)S(1)}, f32[128]{0:T(128)}, u32[]{:S(2)}) copy-start(f32[128]{0:T(128)} %param.19) | copy-start | bytes 1540
  15.7 66.2 %copy-start.7 = (f32[128]{0:T(128)S(1)}, f32[128]{0:T(128)}, u32[]{:S(2)}) copy-start(f32[128]{0:T(128)} %param.20) | copy-start | bytes 1540
  15.7 66.5 %copy-start.5 = (bf16[128,128]{1,0:T(8,128)(2,1)S(1)}, bf16[128,128]{1,0:T(8,128)(2,1)}, u32[]{:S(2)}) copy-start(bf16[128,128]{1,0:T(8,128)(2,1)} %param.21) | copy-start | bytes 98308
  15.7 66.6 %copy-start.3 = (bf16[128,128]{1,0:T(8,128)(2,1)S(1)}, bf16[128,128]{1,0:T(8,128)(2,1)}, u32[]{:S(2)}) copy-start(bf16[128,128]{1,0:T(8,128)(2,1)} %weights.1) | copy-start | bytes 98308
  20.7 1.2 %copy-start = (bf16[16,256,128]{2,1,0:T(8,128)(2,1)S(1)}, bf16[16,256,128]{2,1,0:T(8,128)(2,1)}, u32[]{:S(2)}) copy-start(bf16[16,256,128]{2,1,0:T(8,128)(2,1)} %shard_map.109.normed) | copy-start | bytes 3145732
  21.9 60.4 %copy-start.2 = (bf16[16,256,128]{2,1,0:T(8,128)(2,1)S(1)}, bf16[16,256,128]{2,1,0:T(8,128)(2,1)}, u32[]{:S(2)}) copy-start(bf16[16,256,128]{2,1,0:T(8,128)(2,1)} %shard_map.109.normed) | copy-start | bytes 3145732
  24.0 28.8 %all-to-all-start = ((bf16[64,16,256]{2,1,0:T(8,128)(2,1)}), bf16[64,16,256]{2,1,0:T(8,128)(2,1)S(1)}, u32[]{:S(2)}, u32[]{:S(2)}) async-start(bf16[64,16,256]{2,1,0:T(8,128)(2,1)} %shard_map.110), calls=%async_computation | async-start | bytes 1048576 | tf_op jit(solution)/shard_map/all_to_all | solution.py:232
  34.9 1.2 %copy-start.1 = (bf16[16,256,128]{2,1,0:T(8,128)(2,1)S(1)}, bf16[16,256,128]{2,1,0:T(8,128)(2,1)}, u32[]{:S(2)}) copy-start(bf16[16,256,128]{2,1,0:T(8,128)(2,1)} %shard_map.109.normed) | copy-start | bytes 3145732
  52.8 22.7 %all-to-all-start.1 = ((bf16[64,16,256]{2,1,0:T(8,128)(2,1)}), bf16[64,16,256]{2,1,0:T(8,128)(2,1)S(1)}, u32[]{:S(2)}, u32[]{:S(2)}) async-start(bf16[64,16,256]{2,1,0:T(8,128)(2,1)} %shard_map.111), calls=%async_computation.1 | async-start | bytes 1048576 | tf_op jit(solution)/shard_map/all_to_all | solution.py:232
  59.1 13.8 %collective-permute-start.3 = (bf16[1024,256]{1,0:T(8,128)(2,1)S(1)}, bf16[1024,256]{1,0:T(8,128)(2,1)S(1)}, u32[]{:S(2)}, u32[]{:S(2)}) collective-permute-start(bf16[1024,256]{1,0:T(8,128)(2,1)S(1)} %bitcast.40), channel_id=1, source_target_pairs={{0,2},{2,0},{4,6},{6,4},{1,3},{3,1},{5,7},{7,5},{8,10},{10,8},{12,... | collective-permute-start | bytes 1572872 | tf_op jit(solution)/shard_map/ppermute | solution.py:237
  62.2 21.3 %collective-permute-start.4 = (bf16[1024,256]{1,0:T(8,128)(2,1)S(1)}, bf16[1024,256]{1,0:T(8,128)(2,1)S(1)}, u32[]{:S(2)}, u32[]{:S(2)}) collective-permute-start(bf16[1024,256]{1,0:T(8,128)(2,1)S(1)} %bitcast.41), channel_id=1, source_target_pairs={{0,1},{1,0},{2,3},{3,2},{4,5},{5,4},{6,7},{7,6},{8,9},{9,8},{10,11... | collective-permute-start | bytes 1572872 | tf_op jit(solution)/shard_map/ppermute | solution.py:238
  75.5 8.1 %collective-permute-start.5 = (bf16[1024,256]{1,0:T(8,128)(2,1)S(1)}, bf16[1024,256]{1,0:T(8,128)(2,1)}, u32[]{:S(2)}, u32[]{:S(2)}) collective-permute-start(bf16[1024,256]{1,0:T(8,128)(2,1)S(1)} %collective-permute-done.3.near), channel_id=1, source_target_pairs={{0,1},{1,0},{2,3},{3,2},{4,5},{5,4},{6,7},{7,6},{8,9},{9,8},{10,11... | collective-permute-start | bytes 1572872 | tf_op jit(solution)/shard_map/ppermute | solution.py:243

commit v3 on v0

v3 whole, which is shorter than its diff:
```python
import jax
import jax.numpy as jnp
from jax import lax
from jax.experimental import pallas as pl
from jax.experimental.pallas import tpu as pltpu
from jax.sharding import Mesh
from jax.sharding import PartitionSpec as P

F32 = jnp.float32
BF16 = jnp.bfloat16
VMEM_LIMIT = 32 * 1024 * 1024
LARGE_LIMIT = 50 * 1024 * 1024
EPS = 1e-05
LANES = 128
SWAP = ((0, 1), (1, 0))
OVER_FIRST = (((0,), (0,)), ((), ()))
OVER_LAST = (((1,), (1,)), ((), ()))


def params(limit=VMEM_LIMIT):
    return pltpu.CompilerParams(vmem_limit_bytes=limit)


def whole(*shape):
    return pl.BlockSpec(shape, lambda s, pos: (0,) * len(shape))


def normalise(values, gain, bias):
    chans = values.shape[-1]
    share = jnp.full((chans, chans), 1.0 / chans, BF16)
    mean = jnp.dot(values, share, preferred_element_type=F32)
    centred = values.astype(F32) - mean
    square = centred * centred
    high = square.astype(BF16)
    low = (square - high.astype(F32)).astype(BF16)
    var = jnp.dot(high, share, preferred_element_type=F32) + jnp.dot(low, share, preferred_element_type=F32)
    return (centred * lax.rsqrt(var + EPS) * gain + bias).astype(BF16)


def front_kernel(pos, pair, scale, mine, theirs, out, own, weights):
    step, core = pl.program_id(0), pos[1]
    weights[:, core] = mine[...]
    weights[:, 1 - core] = theirs[...]
    rows, width, chans = pair.shape
    slab = 2 * mine.shape[1]
    normed = normalise(pair[...].reshape(rows * width, chans), scale[0:1], scale[1:2])

    @pl.when(step == pos[0])
    def _():
        own[...] = normed.reshape(rows, width, chans)

    got = lax.dot_general(
        weights[...].reshape(4 * slab, chans), normed, OVER_LAST, preferred_element_type=F32
    )

    def gated(at):
        value = jax.nn.sigmoid(got[at : at + slab]) * got[at + slab : at + 2 * slab]
        parts = [value[:, k * width : (k + 1) * width] for k in range(rows)]
        return jnp.swapaxes(jnp.stack(parts, axis=0), 0, 1).astype(BF16)

    left, right = gated(0), gated(2 * slab)
    out[pl.ds(step // 2 * slab, slab), step % 2] = left
    out[:slab, 2 + step] = right
    out[slab:, 2 + step] = right


def front(pos, pair, scale, mine, theirs):
    rows, tokens, chans = pair.shape
    steps = tokens // (2 * LANES)
    slab = 2 * mine.shape[1]
    return pl.pallas_call(
        front_kernel,
        out_shape=(
            jax.ShapeDtypeStruct((2 * slab, 2 + steps, rows, LANES), BF16),
            jax.ShapeDtypeStruct((rows, LANES, chans), BF16),
        ),
        grid_spec=pltpu.PrefetchScalarGridSpec(
            num_scalar_prefetch=1,
            grid=(steps,),
            in_specs=[
                pl.BlockSpec((rows, LANES, chans), lambda s, pos: (0, 2 * s + pos[1], 0)),
                whole(2, chans),
                whole(*mine.shape),
                whole(*theirs.shape),
            ],
            out_specs=(whole(2 * slab, 2 + steps, rows, LANES), whole(rows, LANES, chans)),
            scratch_shapes=[pltpu.VMEM((4, 2) + mine.shape[1:], BF16)],
        ),
        compiler_params=params(LARGE_LIMIT),
        cost_estimate=pl.CostEstimate(
            flops=14 * steps * rows * LANES * chans * chans,
            bytes_accessed=4 * steps * rows * LANES * chans,
            transcendentals=steps * rows * LANES * chans,
        ),
    )(pos, pair, scale, mine, theirs)


def gate_kernel(normed, weights, out):
    rows, width, chans = normed.shape
    flat = normed[...].reshape(rows * width, chans)
    got = jnp.dot(flat, weights[...], preferred_element_type=F32)
    out[...] = jax.nn.sigmoid(got).reshape(rows, width, chans)


def output_gate(normed, weights):
    rows, width, chans = normed.shape
    return pl.pallas_call(
        gate_kernel,
        out_shape=jax.ShapeDtypeStruct((rows, width, chans), F32),
        compiler_params=params(),
        cost_estimate=pl.CostEstimate(
            flops=2 * rows * width * chans * chans,
            bytes_accessed=6 * rows * width * chans,
            transcendentals=rows * width * chans,
        ),
    )(normed, weights)


def mix_kernel(pos, got, other, out):
    core = pos[1]
    sources, parts, rows, _ = got.shape
    per = LANES // rows

    def block(ref, at):
        return ref[:, at].reshape(sources * rows, LANES)

    right = jnp.concatenate([block(got, at) for at in range(2, parts)], axis=1)
    for ref, first in ((got, core), (other, 1 - core)):
        left = jnp.concatenate([block(ref, 0), block(ref, 1)], axis=1)
        mixed = lax.dot_general(left, right, OVER_FIRST, preferred_element_type=F32).astype(BF16)
        for side in range(2):
            for at in range(parts - 2):
                piece = mixed[side * LANES : (side + 1) * LANES, at * LANES : (at + 1) * LANES]
                out[pl.ds((2 * side + first) * per, per), at] = piece.reshape(per, rows, LANES)


def mix(pos, got, other):
    sources, parts, rows, _ = got.shape
    depth = sources * rows
    return pl.pallas_call(
        mix_kernel,
        out_shape=jax.ShapeDtypeStruct((4 * LANES // rows, parts - 2, rows, LANES), BF16),
        grid_spec=pltpu.PrefetchScalarGridSpec(
            num_scalar_prefetch=1,
            grid=(1,),
            in_specs=[whole(*got.shape), whole(*other.shape)],
            out_specs=whole(4 * LANES // rows, parts - 2, rows, LANES),
        ),
        compiler_params=params(),
        cost_estimate=pl.CostEstimate(
            flops=8 * depth * LANES * (parts - 2) * LANES, bytes_accessed=2 * depth * LANES * 12, transcendentals=0
        ),
    )(pos, got, other)


def finish_kernel(mixed, gain, bias, weights, gate, out):
    chans, rows, _ = mixed.shape
    values = mixed[...].astype(F32)
    values = values - (jnp.sum(values, axis=0) / chans)[None]
    scale = lax.rsqrt(jnp.sum(values * values, axis=0) / chans + EPS)
    scaled = jnp.swapaxes(values * scale[None], 0, 1)
    scaled = (scaled * gain[...][None] + bias[...][None]).astype(BF16)
    for row in range(rows):
        proj = lax.dot_general(scaled[row], weights[...], OVER_FIRST, preferred_element_type=F32)
        out[row] = (proj * gate[row]).astype(BF16)


def finish(mixed, gain, bias, weights, gate):
    chans, rows, width = mixed.shape
    return pl.pallas_call(
        finish_kernel,
        out_shape=jax.ShapeDtypeStruct((rows, width, weights.shape[1]), BF16),
        compiler_params=params(),
        cost_estimate=pl.CostEstimate(
            flops=2 * rows * width * chans * chans, bytes_accessed=8 * chans * rows * width, transcendentals=rows * width
        ),
    )(mixed, gain, bias, weights, gate)


def shards(
    pair,
    ln_gain,
    ln_bias,
    w_a_gate,
    w_a_proj,
    w_b_gate,
    w_b_proj,
    w_gate,
    out_gain,
    out_bias,
    w_out,
):
    rows = pair.shape[0]
    depth, x_count = lax.axis_size("row"), lax.axis_size("x")
    half = depth // 2
    pos = jnp.stack([lax.axis_index("x"), lax.axis_index("core")]).astype(jnp.int32)

    mine = jnp.stack([w.T for w in (w_a_gate, w_a_proj, w_b_gate, w_b_proj)])
    theirs = lax.ppermute(mine, "core", SWAP)
    messages, normed = front(pos, pair, jnp.stack([ln_gain, ln_bias]), mine, theirs)
    shape = messages.shape
    got = lax.all_to_all(
        messages.reshape(shape[0], -1, LANES), "row", split_axis=0, concat_axis=0, tiled=True
    ).reshape(shape)
    got, normed, w_gate, out_gain, out_bias, w_out = lax.optimization_barrier(
        (got, normed, w_gate, out_gain, out_bias, w_out)
    )
    other = lax.ppermute(got[:, :2], "core", SWAP)

    def in_order(array):
        return jnp.swapaxes(array.reshape(x_count, half, -1), 0, 1).reshape(x_count * half, -1)

    gate = output_gate(normed, w_gate)
    gain = jnp.broadcast_to(in_order(out_gain), (x_count * half, LANES))
    bias = jnp.broadcast_to(in_order(out_bias), (x_count * half, LANES))
    out_weights = in_order(w_out)
    got, gate, gain, bias, out_weights = lax.optimization_barrier((got, gate, gain, bias, out_weights))

    mixed = mix(pos, got, other).reshape(half * x_count, rows, LANES)
    groups = [[x_count * (part * half + at) + x for at in range(half) for x in range(x_count)] for part in range(2)]
    mixed = lax.all_to_all(
        mixed, ("row", "x"), split_axis=0, concat_axis=0, tiled=True, axis_index_groups=groups
    )
    return finish(mixed, gain, bias, out_weights, gate)


def solution(mesh):
    fine = Mesh(mesh.devices.reshape(mesh.devices.shape[0], -1, 2), ("row", "x", "core"))
    chan = ("x", "core")
    in_specs = (
        P("row", None, None),
        P(),
        P(),
        P(None, chan),
        P(None, chan),
        P(None, chan),
        P(None, chan),
        P(),
        P(),
        P(),
        P(),
    )
    return jax.shard_map(shards, mesh=fine, in_specs=in_specs, out_specs=P("row", chan, None), check_vma=False)
```

time: 483 us -> 107 us (0.22); the launches traced: 476 us -> 105 us
  waiting for transfers between devices: 283 us -> 0.5 us
  matrix products: 89.8 us -> 0 us
  blocking collectives: 40.3 us -> 78.8 us
  local copies, waits for them, and re-layouts: 34.9 us -> 0.79 us
  between operations: 13.7 us -> 0.12 us
  starting transfers between devices: 0.09 us -> 13.6 us
  other arithmetic: 14.4 us -> 1.5 us
  Pallas kernels: 0 us -> 10.1 us
    all_gather x1 -> x0, waiting for transfers between devices: 159 us -> none  [shards(): lax.all_gather(right, 'row', axis=1, tiled=True)]
    dot_general x7 -> x0, matrix products: 89.8 us -> none  [the longest x1 75.5 us: shards(): jnp.einsum('cki,ckj->cij', left_cols, lax.all_gather(right, 'row', axis=1...]
    psum x1 -> x0, waiting for transfers between devices: 66.3 us -> none  [shards(): lax.psum(second.astype(jnp.bfloat16), 'chan').astype(jnp.float32)]
    reduce_scatter x1 -> x0, waiting for transfers between devices: 57.7 us -> none  [shards(): lax.psum_scatter(jnp.einsum('cij,co->jio', scaled, out_part, preferred_el...]
    all_to_all x1 -> x2, blocking collectives: 40.3 us -> 78.8 us  [the longest x1 50.3 us: shards(): lax.all_to_all(messages.reshape(shape[0], -1, LANES), 'row', split_axis=0...]
    all_to_all x2 -> x0, local copies, waits for them, and re-layouts: 17.7 us -> none  [shards(): lax.all_to_all(left, 'row', split_axis=2, concat_axis=1, tiled=True)]
    ppermute x0 -> x2, starting transfers between devices: none -> 13.6 us  [the longest x1 8.77 us: shards(): theirs = lax.ppermute(mine, 'core', SWAP)]
    unnamed x28 -> x8, local copies, waits for them, and re-layouts: 11.3 us -> 0.03 us
  transfers between devices with their start and end apart: 3 -> 2, of which waited for: 3 -> 2; matrix products, arithmetic and copies ran while one was open for 6% -> 1% of each run, Pallas kernels for 0% -> 0%
where the time goes in v3:
time: 107 us; the launch traced here: 105 us
  blocking collectives  78.8 us (74%)
  starting transfers between devices  13.6 us (13%)
  Pallas kernels  10.1 us (9%)
  other arithmetic  1.5 us (1%)
    all_to_all x1, blocking collectives, shards(): lax.all_to_all(messages.reshape(shape[0], -1, LANES), 'row', split_axis=0...  50.3 us
    all_to_all x1, blocking collectives, shards(): lax.all_to_all(mixed, ('row', 'x'), split_axis=0, concat_axis=0, tiled=Tr...  28.5 us
    ppermute x1, starting transfers between devices, shards(): theirs = lax.ppermute(mine, 'core', SWAP)  8.77 us
    pallas_call x1, Pallas kernels, front(): pl.pallas_call(front_kernel, out_shape=(jax.ShapeDtypeStruct((2 * slab, 2...  6.76 us
    ppermute x1, starting transfers between devices, shards(): other = lax.ppermute(got[:, :2], 'core', SWAP)  4.82 us
  transfers between devices with their start and end apart: 2, of which 2 were waited for; matrix products, arithmetic and copies ran while one was open for 1% of the time, Pallas kernels for 0%

profile of v3, /device:TPU:1, one launch (start us, length us, event | category | flops | bytes accessed | tf_op | source)
XLA Modules:
  0.0 105.3 jit_solution(9603671960838085900)
XLA Ops:
  0.0 0.7 pad_maximum_fusion.mine
  0.7 8.8 %collective-permute-start = (bf16[4,16,128]{2,1,0:T(8,128)(2,1)S(1)}, bf16[4,16,128]{2,1,0:T(8,128)(2,1)S(1)}, u32[]{:S(2)}, u32[]{:S(2)}) collective-permute-start(bf16[4,16,128]{2,1,0:T(8,128)(2,1)S(1)} %pad_maximum_fusion.mine), channel_id=1, source_target_pairs={{0,1},{1,0},{2,3},{3,2},{4,5},{5,4},{6,7},{7,6},{8,9},{9,8},{10,11... | collective-permute-start | bytes 49160 | tf_op jit(solution)/shard_map/ppermute | solution.py:199
  9.5 0.7 pad_maximum_fusion.1.scale
  10.2 0.1 pad_add_fusion.pos
  10.3 0.1 collective-permute-done.theirs
  10.3 6.8 %shard_map.109 = (bf16[64,6,16,128]{3,2,1,0:T(8,128)(2,1)S(1)}, bf16[16,128,128]{2,1,0:T(8,128)(2,1)S(1)}) custom-call(s32[2]{0:T(128)S(1)} %pad_add_fusion.pos, bf16[16,1024,128]{2,1,0:T(8,128)(2,1)} %pair.1, f32[2,128]{1,0:T(2,128)S(1)} %pad_maximum_fusion.1.scale, bf16[4,16,128]{2,1,0:T(8,128)(2,1)S(1)} %pad_maximum_fusion.mine, ...), custom_call_target="tpu_custom_call" | custom-call | flops 1879048192 | bytes 4194304 | tf_op jit(solution)/shard_map/pallas_call | solution.py:71
  17.1 0.0 copy-start.2
  17.1 0.0 copy-start.1
  17.1 0.0 copy-start
  17.2 50.3 %all_to_all.10 = bf16[64,96,128]{2,1,0:T(8,128)(2,1)S(1)} all-to-all(bf16[64,96,128]{2,1,0:T(8,128)(2,1)S(1)} %bitcast.32), channel_id=1, replica_groups=mesh['row'=64,'x'=4,'core'=2] {'row'}, dimensions={0} | all-to-all | bytes 3145728 | tf_op jit(solution)/shard_map/all_to_all | solution.py:202
  67.5 4.8 %collective-permute-start.1 = (bf16[64,2,16,128]{3,2,1,0:T(8,128)(2,1)S(1)}, bf16[64,2,16,128]{3,2,1,0:T(8,128)(2,1)S(1)}, u32[]{:S(2)}, u32[]{:S(2)}) collective-permute-start(bf16[64,2,16,128]{3,2,1,0:T(8,128)(2,1)S(1)} %slice.3), channel_id=1, source_target_pairs={{0,1},{1,0},{2,3},{3,2},{4,5},{5,4},{6,7},{7,6},{8,9},{9,8},{10,11... | collective-permute-start | bytes 1572872 | tf_op jit(solution)/shard_map/ppermute | solution.py:208
  72.3 0.1 reshape.27
  72.4 0.1 reshape.28
  72.5 0.1 copy.16
  72.6 0.1 broadcast_in_dim.16
  72.7 0.1 copy.15
  72.8 0.1 broadcast_in_dim.14
  72.9 0.3 shard_map.110.gate
  73.2 0.1 broadcast_in_dim.15.gain
  73.3 0.1 broadcast_in_dim.17.bias
  73.4 0.4 collective-permute-done.1.other
  73.8 1.3 %shard_map.111 = bf16[32,4,16,128]{3,2,1,0:T(8,128)(2,1)S(1)} custom-call(s32[2]{0:T(128)S(1)} %pad_add_fusion.pos, bf16[64,6,16,128]{3,2,1,0:T(8,128)(2,1)S(1)} %bitcast.30, bf16[64,2,16,128]{3,2,1,0:T(8,128)(2,1)S(1)} %collective-permute-done.1.other), custom_call_target="tpu_custom_call" | custom-call | flops 536870912 | bytes 3145728 | tf_op jit(solution)/shard_map/pallas_call | solution.py:140
  75.1 28.5 %all_to_all.11.mixed = bf16[128,16,128]{2,1,0:T(8,128)(2,1)S(1)} all-to-all(bf16[128,16,128]{2,1,0:T(8,128)(2,1)S(1)} %bitcast.31), channel_id=1, replica_groups={{0,2,4,6,8,10,12,14,16,18,20,22,24,26,28,30,32,34,36,38,40,42,44,46,48,..., dimensions={0} | all-to-all | bytes 1048576 | tf_op jit(solution)/shard_map/all_to_all | solution.py:221
  103.6 1.8 %shard_map.112 = bf16[16,128,128]{2,1,0:T(8,128)(2,1)} custom-call(bf16[128,16,128]{2,1,0:T(8,128)(2,1)S(1)} %all_to_all.11.mixed, f32[128,128]{1,0:T(8,128)S(1)} %broadcast_in_dim.15.gain, f32[128,128]{1,0:T(8,128)S(1)} %broadcast_in_dim.17.bias, bf16[128,128]{1,0:T(8,128)(2,1)S(1)} %bitcast.33, f32[16,128,128]{2,1,0:T(8,128)S(1)} %shard_map.110.gate), custom_call_target="tpu_custom_call" | custom-call | flops 67108864 | bytes 2097152 | tf_op jit(solution)/shard_map/pallas_call | solution.py:170
  (7 shorter events, 0.1 us)
Async XLA Ops:
  0.7 9.6 %collective-permute-start = (bf16[4,16,128]{2,1,0:T(8,128)(2,1)S(1)}, bf16[4,16,128]{2,1,0:T(8,128)(2,1)S(1)}, u32[]{:S(2)}, u32[]{:S(2)}) collective-permute-start(bf16[4,16,128]{2,1,0:T(8,128)(2,1)S(1)} %pad_maximum_fusion.mine), channel_id=1, source_target_pairs={{0,1},{1,0},{2,3},{3,2},{4,5},{5,4},{6,7},{7,6},{8,9},{9,8},{10,11... | collective-permute-start | bytes 49160 | tf_op jit(solution)/shard_map/ppermute | solution.py:199
  17.1 55.2 %copy-start.2 = (f32[128]{0:T(128)S(1)}, f32[128]{0:T(128)}, u32[]{:S(2)}) copy-start(f32[128]{0:T(128)} %param.19) | copy-start | bytes 1540
  17.1 55.3 %copy-start.3 = (f32[128]{0:T(128)S(1)}, f32[128]{0:T(128)}, u32[]{:S(2)}) copy-start(f32[128]{0:T(128)} %param.20) | copy-start | bytes 1540
  17.1 55.7 %copy-start.1 = (bf16[128,128]{1,0:T(8,128)(2,1)S(1)}, bf16[128,128]{1,0:T(8,128)(2,1)}, u32[]{:S(2)}) copy-start(bf16[128,128]{1,0:T(8,128)(2,1)} %param.21) | copy-start | bytes 98308
  17.1 55.8 %copy-start = (bf16[128,128]{1,0:T(8,128)(2,1)S(1)}, bf16[128,128]{1,0:T(8,128)(2,1)}, u32[]{:S(2)}) copy-start(bf16[128,128]{1,0:T(8,128)(2,1)} %weights) | copy-start | bytes 98308
  67.5 6.3 %collective-permute-start.1 = (bf16[64,2,16,128]{3,2,1,0:T(8,128)(2,1)S(1)}, bf16[64,2,16,128]{3,2,1,0:T(8,128)(2,1)S(1)}, u32[]{:S(2)}, u32[]{:S(2)}) collective-permute-start(bf16[64,2,16,128]{3,2,1,0:T(8,128)(2,1)S(1)} %slice.3), channel_id=1, source_target_pairs={{0,1},{1,0},{2,3},{3,2},{4,5},{5,4},{6,7},{7,6},{8,9},{9,8},{10,11... | collective-permute-start | bytes 1572872 | tf_op jit(solution)/shard_map/ppermute | solution.py:208

commit v4 on v3

v4 whole, which is shorter than its diff:
```python
import jax
import jax.numpy as jnp
from jax import lax
from jax.experimental import pallas as pl
from jax.experimental.pallas import tpu as pltpu
from jax.sharding import Mesh
from jax.sharding import PartitionSpec as P

F32 = jnp.float32
BF16 = jnp.bfloat16
VMEM_LIMIT = 32 * 1024 * 1024
LARGE_LIMIT = 50 * 1024 * 1024
EPS = 1e-05
LANES = 128
SWAP = ((0, 1), (1, 0))
OVER_FIRST = (((0,), (0,)), ((), ()))


def params(limit=VMEM_LIMIT):
    return pltpu.CompilerParams(vmem_limit_bytes=limit)


def in_vmem(count):
    return [pl.BlockSpec(memory_space=pltpu.VMEM)] * count


def normalise(values, gain, bias):
    values = values.T.astype(F32)
    centred = values - jnp.mean(values, axis=0, keepdims=True)
    var = jnp.mean(centred * centred, axis=0, keepdims=True)
    return (centred * lax.rsqrt(var + EPS) * gain + bias).astype(BF16)


def front_kernel(pair, scale, mine, theirs, out, own, weights, held, sems):
    core, x = lax.axis_index("core"), lax.axis_index("x")
    steps, rows, _, chans = held.shape
    copies = []
    for step in range(steps):
        at = pl.multiple_of((2 * step + core) * LANES, LANES)
        copies.append(pltpu.make_async_copy(pair.at[:, pl.ds(at, LANES), :], held.at[step], sems.at[step]))
    for copy in copies:
        copy.start()
    weights[:, core] = mine[...]
    weights[:, 1 - core] = theirs[...]
    slab = 2 * mine.shape[1]
    both = weights[...].reshape(4 * slab, chans)
    columns = scale[...].T
    for step in range(steps):
        copies[step].wait()
        normed = normalise(held[step].reshape(rows * LANES, chans), columns[:, 0:1], columns[:, 1:2])

        @pl.when(step == x)
        def _():
            own[...] = normed

        got = jnp.dot(both, normed, preferred_element_type=F32)

        def gated(first):
            value = jax.nn.sigmoid(got[first : first + slab]) * got[first + slab : first + 2 * slab]
            parts = [value[:, k * LANES : (k + 1) * LANES] for k in range(rows)]
            return jnp.swapaxes(jnp.stack(parts, axis=0), 0, 1).astype(BF16)

        left, right = gated(0), gated(2 * slab)
        half = step // 2 * slab
        out[half : half + slab, step % 2] = left
        out[:slab, 2 + step] = right
        out[slab:, 2 + step] = right


def front(pair, scale, mine, theirs):
    rows, tokens, chans = pair.shape
    steps = tokens // (2 * LANES)
    slab = 2 * mine.shape[1]
    return pl.pallas_call(
        front_kernel,
        out_shape=(
            jax.ShapeDtypeStruct((2 * slab, 2 + steps, rows, LANES), BF16),
            jax.ShapeDtypeStruct((chans, rows * LANES), BF16),
        ),
        in_specs=[pl.BlockSpec(memory_space=pltpu.HBM)] + in_vmem(3),
        out_specs=tuple(in_vmem(2)),
        scratch_shapes=[
            pltpu.VMEM((4, 2) + mine.shape[1:], BF16),
            pltpu.VMEM((steps, rows, LANES, chans), BF16),
            pltpu.SemaphoreType.DMA((steps,)),
        ],
        compiler_params=params(LARGE_LIMIT),
        cost_estimate=pl.CostEstimate(
            flops=14 * steps * rows * LANES * chans * chans,
            bytes_accessed=4 * steps * rows * LANES * chans,
            transcendentals=steps * rows * LANES * chans,
        ),
    )(pair, scale, mine, theirs)


def gate_kernel(normed, weights, out):
    got = lax.dot_general(normed[...], weights[...], OVER_FIRST, preferred_element_type=F32)
    out[...] = jax.nn.sigmoid(got).reshape(out.shape)


def output_gate(normed, weights):
    chans, pairs = normed.shape
    rows = pairs // LANES
    return pl.pallas_call(
        gate_kernel,
        out_shape=jax.ShapeDtypeStruct((rows, LANES, chans), F32),
        in_specs=in_vmem(2),
        out_specs=in_vmem(1)[0],
        compiler_params=params(),
        cost_estimate=pl.CostEstimate(
            flops=2 * pairs * chans * chans, bytes_accessed=6 * pairs * chans, transcendentals=pairs * chans
        ),
    )(normed, weights)


def mix_kernel(got, other, out):
    core = lax.axis_index("core")
    sources, parts, rows, _ = got.shape
    per = LANES // rows

    def block(ref, at):
        return ref[:, at].reshape(sources * rows, LANES)

    right = jnp.concatenate([block(got, at) for at in range(2, parts)], axis=1)
    for ref, first in ((got, core), (other, 1 - core)):
        left = jnp.concatenate([block(ref, 0), block(ref, 1)], axis=1)
        mixed = lax.dot_general(left, right, OVER_FIRST, preferred_element_type=F32).astype(BF16)
        for side in range(2):
            for at in range(parts - 2):
                piece = mixed[side * LANES : (side + 1) * LANES, at * LANES : (at + 1) * LANES]
                out[at, pl.ds((2 * side + first) * per, per)] = piece.reshape(per, rows, LANES)


def mix(got, other):
    sources, parts, rows, _ = got.shape
    depth = sources * rows
    return pl.pallas_call(
        mix_kernel,
        out_shape=jax.ShapeDtypeStruct((parts - 2, 4 * LANES // rows, rows, LANES), BF16),
        in_specs=in_vmem(2),
        out_specs=in_vmem(1)[0],
        compiler_params=params(),
        cost_estimate=pl.CostEstimate(
            flops=8 * depth * LANES * (parts - 2) * LANES, bytes_accessed=2 * depth * LANES * 12, transcendentals=0
        ),
    )(got, other)


def finish_kernel(mixed, gain, bias, weights, gate, out, held, sems):
    chans, rows, width = mixed.shape
    values = mixed[...].astype(F32)
    values = values - (jnp.sum(values, axis=0) / chans)[None]
    scale = lax.rsqrt(jnp.sum(values * values, axis=0) / chans + EPS)
    scaled = jnp.swapaxes(values * scale[None], 0, 1)
    scaled = (scaled * gain[...][None] + bias[...][None]).astype(BF16)
    count = held.shape[0]
    step = rows // count
    copies = []
    for piece in range(count):
        at = piece * step
        wide = jnp.concatenate([scaled[at + row] for row in range(step)], axis=1)
        proj = lax.dot_general(wide, weights[...], OVER_FIRST, preferred_element_type=F32)
        held[piece] = (proj.reshape(step, width, -1) * gate[at : at + step]).astype(BF16)
        copies.append(pltpu.make_async_copy(held.at[piece], out.at[pl.ds(at, step)], sems.at[piece]))
        copies[-1].start()
    for copy in copies:
        copy.wait()


def finish(mixed, gain, bias, weights, gate):
    chans, rows, width = mixed.shape
    outs = weights.shape[1]
    return pl.pallas_call(
        finish_kernel,
        out_shape=jax.ShapeDtypeStruct((rows, width, outs), BF16),
        in_specs=in_vmem(5),
        out_specs=pl.BlockSpec(memory_space=pltpu.HBM),
        scratch_shapes=[pltpu.VMEM((2, rows // 2, width, outs), BF16), pltpu.SemaphoreType.DMA((2,))],
        compiler_params=params(),
        cost_estimate=pl.CostEstimate(
            flops=2 * rows * width * chans * chans, bytes_accessed=8 * chans * rows * width, transcendentals=rows * width
        ),
    )(mixed, gain, bias, weights, gate)


def shards(
    pair,
    ln_gain,
    ln_bias,
    w_a_gate,
    w_a_proj,
    w_b_gate,
    w_b_proj,
    w_gate,
    out_gain,
    out_bias,
    w_out,
):
    rows, _, chans = pair.shape
    depth, x_count = lax.axis_size("row"), lax.axis_size("x")
    half = depth // 2

    mine = jnp.stack([w.T for w in (w_a_gate, w_a_proj, w_b_gate, w_b_proj)])
    theirs = lax.ppermute(mine, "core", SWAP)
    messages, normed = front(pair, jnp.stack([ln_gain, ln_bias]), mine, theirs)
    shape = messages.shape
    got = lax.all_to_all(
        messages.reshape(shape[0], -1, LANES), "row", split_axis=0, concat_axis=0, tiled=True
    ).reshape(shape)
    got, normed, w_gate, out_gain, out_bias = lax.optimization_barrier((got, normed, w_gate, out_gain, out_bias))
    other = lax.ppermute(got[:, :2], "core", SWAP)
    gate = output_gate(normed, w_gate)
    gain = jnp.broadcast_to(out_gain[:, None], (chans, LANES))
    bias = jnp.broadcast_to(out_bias[:, None], (chans, LANES))
    got, gate, gain, bias = lax.optimization_barrier((got, gate, gain, bias))

    mixed = mix(got, other).reshape(x_count * half, rows, LANES)
    groups = [[x_count * (part * half + at) + x for x in range(x_count) for at in range(half)] for part in range(2)]
    mixed = lax.all_to_all(
        mixed, ("row", "x"), split_axis=0, concat_axis=0, tiled=True, axis_index_groups=groups
    )
    return finish(mixed, gain, bias, w_out, gate)


def solution(mesh):
    fine = Mesh(mesh.devices.reshape(mesh.devices.shape[0], -1, 2), ("row", "x", "core"))
    chan = ("x", "core")
    in_specs = (
        P("row", None, None),
        P(),
        P(),
        P(None, chan),
        P(None, chan),
        P(None, chan),
        P(None, chan),
        P(),
        P(),
        P(),
        P(),
    )
    return jax.shard_map(shards, mesh=fine, in_specs=in_specs, out_specs=P("row", chan, None), check_vma=False)
```

time: 107 us -> 105 us (0.981)
  Pallas kernels: 10.1 us -> 7.05 us
  blocking collectives: 78.8 us -> 80.8 us
    pallas_call x1, Pallas kernels: 6.76 us -> 4.3 us  [front(): pl.pallas_call(front_kernel, out_shape=(jax.ShapeDtypeStruct((2 * slab, 2...]
    all_to_all x1, blocking collectives: 28.5 us -> 30.6 us  [shards(): lax.all_to_all(mixed, ('row', 'x'), split_axis=0, concat_axis=0, tiled=Tr...]
where the time goes in v4:
time: 105 us; the launch traced here: 104 us
  blocking collectives  80.8 us (77%)
  starting transfers between devices  13.6 us (13%)
  Pallas kernels  7.05 us (7%)
  other arithmetic  1.42 us (1%)
  waiting for transfers between devices  1.11 us (1%)
    all_to_all x1, blocking collectives, shards(): lax.all_to_all(messages.reshape(shape[0], -1, LANES), 'row', split_axis=0...  50.1 us
    all_to_all x1, blocking collectives, shards(): lax.all_to_all(mixed, ('row', 'x'), split_axis=0, concat_axis=0, tiled=Tr...  30.6 us
    ppermute x1, starting transfers between devices, shards(): theirs = lax.ppermute(mine, 'core', SWAP)  8.77 us
    ppermute x1, starting transfers between devices, shards(): other = lax.ppermute(got[:, :2], 'core', SWAP)  4.82 us
    pallas_call x1, Pallas kernels, front(): pl.pallas_call(front_kernel, out_shape=(jax.ShapeDtypeStruct((2 * slab, 2...  4.3 us
  transfers between devices with their start and end apart: 2, of which 2 were waited for; matrix products, arithmetic and copies ran while one was open for 1% of the time, Pallas kernels for 0%

profile of v4, /device:TPU:1, one launch (start us, length us, event | category | flops | bytes accessed | tf_op | source)
XLA Modules:
  0.0 104.2 jit_solution(8987497290895949262)
XLA Ops:
  0.0 0.7 pad_maximum_fusion.mine
  0.7 8.8 %collective-permute-start = (bf16[4,16,128]{2,1,0:T(8,128)(2,1)S(1)}, bf16[4,16,128]{2,1,0:T(8,128)(2,1)S(1)}, u32[]{:S(2)}, u32[]{:S(2)}) collective-permute-start(bf16[4,16,128]{2,1,0:T(8,128)(2,1)S(1)} %pad_maximum_fusion.mine), channel_id=1, source_target_pairs={{0,1},{1,0},{2,3},{3,2},{4,5},{5,4},{6,7},{7,6},{8,9},{9,8},{10,11... | collective-permute-start | bytes 49160 | tf_op jit(solution)/shard_map/ppermute | solution.py:204
  9.5 0.7 pad_maximum_fusion.1.scale
  10.2 0.1 collective-permute-done.theirs
  10.3 4.3 %shard_map.109 = (bf16[64,6,16,128]{3,2,1,0:T(8,128)(2,1)S(1)}, bf16[128,2048]{1,0:T(8,128)(2,1)S(1)}) custom-call(bf16[16,1024,128]{2,1,0:T(8,128)(2,1)} %pair.1, f32[2,128]{1,0:T(2,128)S(1)} %pad_maximum_fusion.1.scale, bf16[4,16,128]{2,1,0:T(8,128)(2,1)S(1)} %pad_maximum_fusion.mine, bf16[4,16,128]{2,1,0:T(8,128)(2,1)S(1)} %collective-permute-done.theirs), custom_call_target="tpu_custom_call" | custom-call | flops 1879048192 | bytes 4194304 | tf_op jit(solution)/shard_map/pallas_call | solution.py:74
  14.7 0.0 copy-start.1
  14.7 50.1 %all_to_all.10 = bf16[64,96,128]{2,1,0:T(8,128)(2,1)S(1)} all-to-all(bf16[64,96,128]{2,1,0:T(8,128)(2,1)S(1)} %bitcast.20), channel_id=1, replica_groups=mesh['row'=64,'x'=4,'core'=2] {'row'}, dimensions={0} | all-to-all | bytes 3145728 | tf_op jit(solution)/shard_map/all_to_all | solution.py:207
  64.8 0.0 copy-start.2
  64.8 0.0 copy-start.3
  64.9 4.8 %collective-permute-start.1 = (bf16[64,2,16,128]{3,2,1,0:T(8,128)(2,1)S(1)}, bf16[64,2,16,128]{3,2,1,0:T(8,128)(2,1)S(1)}, u32[]{:S(2)}, u32[]{:S(2)}) collective-permute-start(bf16[64,2,16,128]{3,2,1,0:T(8,128)(2,1)S(1)} %slice.3), channel_id=1, source_target_pairs={{0,1},{1,0},{2,3},{3,2},{4,5},{5,4},{6,7},{7,6},{8,9},{9,8},{10,11... | collective-permute-start | bytes 1572872 | tf_op jit(solution)/shard_map/ppermute | solution.py:211
  69.7 0.0 copy-done.1
  69.7 0.3 shard_map.110.gate
  70.0 0.0 copy-done.2
  70.1 0.1 broadcast_in_dim.4.gain
  70.1 0.0 copy-done.3
  70.1 0.1 broadcast_in_dim.5.bias
  70.2 0.0 copy-start
  70.2 1.0 collective-permute-done.1.other
  71.2 0.7 shard_map.111
  71.9 30.6 %all_to_all.11.mixed = bf16[128,16,128]{2,1,0:T(8,128)(2,1)S(1)} all-to-all(bf16[128,16,128]{2,1,0:T(8,128)(2,1)S(1)} %bitcast.19), channel_id=1, replica_groups={{0,8,16,24,32,40,48,56,64,72,80,88,96,104,112,120,128,136,144,152,160,1..., dimensions={0} | all-to-all | bytes 1048576 | tf_op jit(solution)/shard_map/all_to_all | solution.py:219
  102.6 0.0 copy-done
  102.6 1.7 %shard_map.112 = bf16[16,128,128]{2,1,0:T(8,128)(2,1)} custom-call(bf16[128,16,128]{2,1,0:T(8,128)(2,1)S(1)} %all_to_all.11.mixed, f32[128,128]{1,0:T(8,128)S(1)} %broadcast_in_dim.4.gain, f32[128,128]{1,0:T(8,128)S(1)} %broadcast_in_dim.5.bias, bf16[128,128]{1,0:T(8,128)(2,1)S(1)} %copy-done, f32[16,128,128]{2,1,0:T(8,128)S(1)} %shard_map.110.gate), custom_call_target="tpu_custom_call" | custom-call | flops 67108864 | bytes 2097152 | tf_op jit(solution)/shard_map/pallas_call | solution.py:173
  (1 shorter events, 0.0 us)
Async XLA Ops:
  0.7 9.6 %collective-permute-start = (bf16[4,16,128]{2,1,0:T(8,128)(2,1)S(1)}, bf16[4,16,128]{2,1,0:T(8,128)(2,1)S(1)}, u32[]{:S(2)}, u32[]{:S(2)}) collective-permute-start(bf16[4,16,128]{2,1,0:T(8,128)(2,1)S(1)} %pad_maximum_fusion.mine), channel_id=1, source_target_pairs={{0,1},{1,0},{2,3},{3,2},{4,5},{5,4},{6,7},{7,6},{8,9},{9,8},{10,11... | collective-permute-start | bytes 49160 | tf_op jit(solution)/shard_map/ppermute | solution.py:204
  14.7 55.0 %copy-start.1 = (bf16[128,128]{1,0:T(8,128)(2,1)S(1)}, bf16[128,128]{1,0:T(8,128)(2,1)}, u32[]{:S(2)}) copy-start(bf16[128,128]{1,0:T(8,128)(2,1)} %weights.1) | copy-start | bytes 98308
  64.8 5.2 %copy-start.2 = (f32[128]{0:T(128)S(1)}, f32[128]{0:T(128)}, u32[]{:S(2)}) copy-start(f32[128]{0:T(128)} %param.19) | copy-start | bytes 1540
  64.8 5.3 %copy-start.3 = (f32[128]{0:T(128)S(1)}, f32[128]{0:T(128)}, u32[]{:S(2)}) copy-start(f32[128]{0:T(128)} %param.20) | copy-start | bytes 1540
  64.9 6.3 %collective-permute-start.1 = (bf16[64,2,16,128]{3,2,1,0:T(8,128)(2,1)S(1)}, bf16[64,2,16,128]{3,2,1,0:T(8,128)(2,1)S(1)}, u32[]{:S(2)}, u32[]{:S(2)}) collective-permute-start(bf16[64,2,16,128]{3,2,1,0:T(8,128)(2,1)S(1)} %slice.3), channel_id=1, source_target_pairs={{0,1},{1,0},{2,3},{3,2},{4,5},{5,4},{6,7},{7,6},{8,9},{9,8},{10,11... | collective-permute-start | bytes 1572872 | tf_op jit(solution)/shard_map/ppermute | solution.py:211
  70.2 32.4 %copy-start = (bf16[128,128]{1,0:T(8,128)(2,1)S(1)}, bf16[128,128]{1,0:T(8,128)(2,1)}, u32[]{:S(2)}) copy-start(bf16[128,128]{1,0:T(8,128)(2,1)} %weights.2) | copy-start | bytes 98308

commit v5 on v4

--- a/solution.py
+++ b/solution.py
@@ -60,11 +60,8 @@
             parts = [value[:, k * LANES : (k + 1) * LANES] for k in range(rows)]
             return jnp.swapaxes(jnp.stack(parts, axis=0), 0, 1).astype(BF16)
 
-        left, right = gated(0), gated(2 * slab)
-        half = step // 2 * slab
-        out[half : half + slab, step % 2] = left
-        out[:slab, 2 + step] = right
-        out[slab:, 2 + step] = right
+        out[:, step] = gated(0)
+        out[:, steps + step] = gated(2 * slab)
 
 
 def front(pair, scale, mine, theirs):
@@ -74,7 +71,7 @@
     return pl.pallas_call(
         front_kernel,
         out_shape=(
-            jax.ShapeDtypeStruct((2 * slab, 2 + steps, rows, LANES), BF16),
+            jax.ShapeDtypeStruct((slab, 2 * steps, rows, LANES), BF16),
             jax.ShapeDtypeStruct((chans, rows * LANES), BF16),
         ),
         in_specs=[pl.BlockSpec(memory_space=pltpu.HBM)] + in_vmem(3),
@@ -116,39 +113,42 @@
 def mix_kernel(got, other, out):
     core = lax.axis_index("core")
     sources, parts, rows, _ = got.shape
+    blocks = parts // 2
     per = LANES // rows
 
-    def block(ref, at):
-        return ref[:, at].reshape(sources * rows, LANES)
-
-    right = jnp.concatenate([block(got, at) for at in range(2, parts)], axis=1)
+    def joined(ref, first):
+        return jnp.concatenate(
+            [ref[:, first + at].reshape(sources * rows, LANES) for at in range(blocks)], axis=1
+        )
+
+    right = joined(got, blocks)
     for ref, first in ((got, core), (other, 1 - core)):
-        left = jnp.concatenate([block(ref, 0), block(ref, 1)], axis=1)
-        mixed = lax.dot_general(left, right, OVER_FIRST, preferred_element_type=F32).astype(BF16)
-        for side in range(2):
-            for at in range(parts - 2):
+        mixed = lax.dot_general(joined(ref, 0), right, OVER_FIRST, preferred_element_type=F32).astype(BF16)
+        for side in range(blocks):
+            for at in range(blocks):
                 piece = mixed[side * LANES : (side + 1) * LANES, at * LANES : (at + 1) * LANES]
                 out[at, pl.ds((2 * side + first) * per, per)] = piece.reshape(per, rows, LANES)
 
 
 def mix(got, other):
     sources, parts, rows, _ = got.shape
-    depth = sources * rows
+    depth, width = sources * rows, parts // 2 * LANES
     return pl.pallas_call(
         mix_kernel,
-        out_shape=jax.ShapeDtypeStruct((parts - 2, 4 * LANES // rows, rows, LANES), BF16),
+        out_shape=jax.ShapeDtypeStruct((parts // 2, 2 * width // rows, rows, LANES), BF16),
         in_specs=in_vmem(2),
         out_specs=in_vmem(1)[0],
         compiler_params=params(),
         cost_estimate=pl.CostEstimate(
-            flops=8 * depth * LANES * (parts - 2) * LANES, bytes_accessed=2 * depth * LANES * 12, transcendentals=0
+            flops=4 * depth * width * width, bytes_accessed=2 * (3 * depth * width + 2 * width * width), transcendentals=0
         ),
     )(got, other)
 
 
 def finish_kernel(mixed, gain, bias, weights, gate, out, held, sems):
-    chans, rows, width = mixed.shape
-    values = mixed[...].astype(F32)
+    groups, _, each, rows, width = mixed.shape
+    chans = groups * each
+    values = (mixed[:, 0].astype(F32) + mixed[:, 1].astype(F32)).reshape(chans, rows, width)
     values = values - (jnp.sum(values, axis=0) / chans)[None]
     scale = lax.rsqrt(jnp.sum(values * values, axis=0) / chans + EPS)
     scaled = jnp.swapaxes(values * scale[None], 0, 1)
@@ -168,17 +168,17 @@
 
 
 def finish(mixed, gain, bias, weights, gate):
-    chans, rows, width = mixed.shape
-    outs = weights.shape[1]
+    groups, _, each, rows, width = mixed.shape
+    chans, outs = weights.shape
     return pl.pallas_call(
         finish_kernel,
         out_shape=jax.ShapeDtypeStruct((rows, width, outs), BF16),
         in_specs=in_vmem(5),
         out_specs=pl.BlockSpec(memory_space=pltpu.HBM),
-        scratch_shapes=[pltpu.VMEM((2, rows // 2, width, outs), BF16), pltpu.SemaphoreType.DMA((2,))],
+        scratch_shapes=[pltpu.VMEM((4, rows // 4, width, outs), BF16), pltpu.SemaphoreType.DMA((4,))],
         compiler_params=params(),
         cost_estimate=pl.CostEstimate(
-            flops=2 * rows * width * chans * chans, bytes_accessed=8 * chans * rows * width, transcendentals=rows * width
+            flops=2 * rows * width * chans * chans, bytes_accessed=10 * chans * rows * width, transcendentals=rows * width
         ),
     )(mixed, gain, bias, weights, gate)
 
@@ -204,22 +204,23 @@
     theirs = lax.ppermute(mine, "core", SWAP)
     messages, normed = front(pair, jnp.stack([ln_gain, ln_bias]), mine, theirs)
     shape = messages.shape
+    halves = [[part * half + at for at in range(half)] for part in range(2)]
     got = lax.all_to_all(
-        messages.reshape(shape[0], -1, LANES), "row", split_axis=0, concat_axis=0, tiled=True
+        messages.reshape(half, -1, LANES), "row", split_axis=0, concat_axis=0, tiled=True, axis_index_groups=halves
     ).reshape(shape)
     got, normed, w_gate, out_gain, out_bias = lax.optimization_barrier((got, normed, w_gate, out_gain, out_bias))
-    other = lax.ppermute(got[:, :2], "core", SWAP)
+    other = lax.ppermute(got[:, : shape[1] // 2], "core", SWAP)
     gate = output_gate(normed, w_gate)
     gain = jnp.broadcast_to(out_gain[:, None], (chans, LANES))
     bias = jnp.broadcast_to(out_bias[:, None], (chans, LANES))
     got, gate, gain, bias = lax.optimization_barrier((got, gate, gain, bias))
 
-    mixed = mix(got, other).reshape(x_count * half, rows, LANES)
-    groups = [[x_count * (part * half + at) + x for x in range(x_count) for at in range(half)] for part in range(2)]
+    mixed = mix(got, other).reshape(x_count * depth, rows, LANES)
+    group = [x_count * row + x for x in range(x_count) for row in range(depth)]
     mixed = lax.all_to_all(
-        mixed, ("row", "x"), split_axis=0, concat_axis=0, tiled=True, axis_index_groups=groups
+        mixed, ("row", "x"), split_axis=0, concat_axis=0, tiled=True, axis_index_groups=[group]
     )
-    return finish(mixed, gain, bias, w_out, gate)
+    return finish(mixed.reshape(x_count, 2, half, rows, LANES), gain, bias, w_out, gate)
 
 
 def solution(mesh):

time: 105 us -> 104 us (level)
  blocking collectives: 80.8 us -> 78.5 us
  starting transfers between devices: 13.6 us -> 14.9 us
    all_to_all x1, blocking collectives: 50.1 us -> 33 us  [shards(): lax.all_to_all(messages.reshape(half, -1, LANES), 'row', split_axis=0, co...]
    all_to_all x1, blocking collectives: 30.6 us -> 45.5 us  [shards(): lax.all_to_all(mixed, ('row', 'x'), split_axis=0, concat_axis=0, tiled=Tr...]
    ppermute x1, starting transfers between devices: 4.82 us -> 6.11 us  [shards(): other = lax.ppermute(got[:, :shape[1] // 2], 'core', SWAP)]
where the time goes in v5:
time: 104 us; the launch traced here: 103 us
  blocking collectives  78.5 us (75%)
  starting transfers between devices  14.9 us (14%)
  Pallas kernels  7.09 us (7%)
  other arithmetic  1.42 us (1%)
  waiting for transfers between devices  1.1 us (1%)
    all_to_all x1, blocking collectives, shards(): lax.all_to_all(mixed, ('row', 'x'), split_axis=0, concat_axis=0, tiled=Tr...  45.5 us
    all_to_all x1, blocking collectives, shards(): lax.all_to_all(messages.reshape(half, -1, LANES), 'row', split_axis=0, co...  33 us
    ppermute x1, starting transfers between devices, shards(): theirs = lax.ppermute(mine, 'core', SWAP)  8.77 us
    ppermute x1, starting transfers between devices, shards(): other = lax.ppermute(got[:, :shape[1] // 2], 'core', SWAP)  6.11 us
    pallas_call x1, Pallas kernels, front(): pl.pallas_call(front_kernel, out_shape=(jax.ShapeDtypeStruct((slab, 2 * s...  4.31 us
  transfers between devices with their start and end apart: 2, of which 2 were waited for; matrix products, arithmetic and copies ran while one was open for 1% of the time, Pallas kernels for 0%

profile of v5, /device:TPU:1, one launch (start us, length us, event | category | flops | bytes accessed | tf_op | source)
XLA Modules:
  0.0 103.3 jit_solution(12902630747052731228)
XLA Ops:
  0.0 0.7 pad_maximum_fusion.mine
  0.7 8.8 %collective-permute-start = (bf16[4,16,128]{2,1,0:T(8,128)(2,1)S(1)}, bf16[4,16,128]{2,1,0:T(8,128)(2,1)S(1)}, u32[]{:S(2)}, u32[]{:S(2)}) collective-permute-start(bf16[4,16,128]{2,1,0:T(8,128)(2,1)S(1)} %pad_maximum_fusion.mine), channel_id=1, source_target_pairs={{0,1},{1,0},{2,3},{3,2},{4,5},{5,4},{6,7},{7,6},{8,9},{9,8},{10,11... | collective-permute-start | bytes 49160 | tf_op jit(solution)/shard_map/ppermute | solution.py:204
  9.5 0.7 pad_maximum_fusion.1.scale
  10.2 0.0 copy-start.1
  10.2 0.0 copy-start.2
  10.2 0.0 copy-start.3
  10.2 0.1 collective-permute-done.theirs
  10.3 4.3 %shard_map.109 = (bf16[32,8,16,128]{3,2,1,0:T(8,128)(2,1)S(1)}, bf16[128,2048]{1,0:T(8,128)(2,1)S(1)}) custom-call(bf16[16,1024,128]{2,1,0:T(8,128)(2,1)} %pair.1, f32[2,128]{1,0:T(2,128)S(1)} %pad_maximum_fusion.1.scale, bf16[4,16,128]{2,1,0:T(8,128)(2,1)S(1)} %pad_maximum_fusion.mine, bf16[4,16,128]{2,1,0:T(8,128)(2,1)S(1)} %collective-permute-done.theirs), custom_call_target="tpu_custom_call" | custom-call | flops 1879048192 | bytes 4194304 | tf_op jit(solution)/shard_map/pallas_call | solution.py:71
  14.7 33.0 %all_to_all.10 = bf16[32,128,128]{2,1,0:T(8,128)(2,1)S(1)} all-to-all(bf16[32,128,128]{2,1,0:T(8,128)(2,1)S(1)} %bitcast.22), channel_id=1, replica_groups={{0,8,16,24,32,40,48,56,64,72,80,88,96,104,112,120,128,136,144,152,160,1..., dimensions={0} | all-to-all | bytes 2097152 | tf_op jit(solution)/shard_map/all_to_all | solution.py:208
  47.6 0.0 copy-start
  47.7 6.1 %collective-permute-start.1 = (bf16[32,4,16,128]{3,2,1,0:T(8,128)(2,1)S(1)}, bf16[32,4,16,128]{3,2,1,0:T(8,128)(2,1)S(1)}, u32[]{:S(2)}, u32[]{:S(2)}) collective-permute-start(bf16[32,4,16,128]{3,2,1,0:T(8,128)(2,1)S(1)} %slice.3), channel_id=1, source_target_pairs={{0,1},{1,0},{2,3},{3,2},{4,5},{5,4},{6,7},{7,6},{8,9},{9,8},{10,11... | collective-permute-start | bytes 1572872 | tf_op jit(solution)/shard_map/ppermute | solution.py:212
  53.8 0.0 copy-done.1
  53.8 0.3 shard_map.110.gate
  54.2 0.0 copy-done.2
  54.2 0.1 broadcast_in_dim.4.gain
  54.3 0.0 copy-done.3
  54.3 0.1 broadcast_in_dim.5.bias
  54.3 1.0 collective-permute-done.1.other
  55.3 0.7 shard_map.111
  56.1 45.5 %all_to_all.11 = bf16[256,16,128]{2,1,0:T(8,128)(2,1)S(1)} all-to-all(bf16[256,16,128]{2,1,0:T(8,128)(2,1)S(1)} %bitcast.21), channel_id=1, replica_groups={{0,8,16,24,32,40,48,56,64,72,80,88,96,104,112,120,128,136,144,152,160,1..., dimensions={0} | all-to-all | bytes 2097152 | tf_op jit(solution)/shard_map/all_to_all | solution.py:220
  101.6 0.0 copy-done
  101.6 1.7 %shard_map.112 = bf16[16,128,128]{2,1,0:T(8,128)(2,1)} custom-call(bf16[4,2,32,16,128]{4,3,2,1,0:T(8,128)(2,1)S(1)} %bitcast.20, f32[128,128]{1,0:T(8,128)S(1)} %broadcast_in_dim.4.gain, f32[128,128]{1,0:T(8,128)S(1)} %broadcast_in_dim.5.bias, bf16[128,128]{1,0:T(8,128)(2,1)S(1)} %copy-done, f32[16,128,128]{2,1,0:T(8,128)S(1)} %shard_map.110.gate), custom_call_target="tpu_custom_call" | custom-call | flops 67108864 | bytes 2621440 | tf_op jit(solution)/shard_map/pallas_call | solution.py:173
  (1 shorter events, 0.0 us)
Async XLA Ops:
  0.7 9.6 %collective-permute-start = (bf16[4,16,128]{2,1,0:T(8,128)(2,1)S(1)}, bf16[4,16,128]{2,1,0:T(8,128)(2,1)S(1)}, u32[]{:S(2)}, u32[]{:S(2)}) collective-permute-start(bf16[4,16,128]{2,1,0:T(8,128)(2,1)S(1)} %pad_maximum_fusion.mine), channel_id=1, source_target_pairs={{0,1},{1,0},{2,3},{3,2},{4,5},{5,4},{6,7},{7,6},{8,9},{9,8},{10,11... | collective-permute-start | bytes 49160 | tf_op jit(solution)/shard_map/ppermute | solution.py:204
  10.2 43.6 %copy-start.1 = (bf16[128,128]{1,0:T(8,128)(2,1)S(1)}, bf16[128,128]{1,0:T(8,128)(2,1)}, u32[]{:S(2)}) copy-start(bf16[128,128]{1,0:T(8,128)(2,1)} %weights.1) | copy-start | bytes 98308
  10.2 44.0 %copy-start.2 = (f32[128]{0:T(128)S(1)}, f32[128]{0:T(128)}, u32[]{:S(2)}) copy-start(f32[128]{0:T(128)} %param.19) | copy-start | bytes 1540
  10.2 44.0 %copy-start.3 = (f32[128]{0:T(128)S(1)}, f32[128]{0:T(128)}, u32[]{:S(2)}) copy-start(f32[128]{0:T(128)} %param.20) | copy-start | bytes 1540
  47.6 54.0 %copy-start = (bf16[128,128]{1,0:T(8,128)(2,1)S(1)}, bf16[128,128]{1,0:T(8,128)(2,1)}, u32[]{:S(2)}) copy-start(bf16[128,128]{1,0:T(8,128)(2,1)} %weights.2) | copy-start | bytes 98308
  47.7 7.6 %collective-permute-start.1 = (bf16[32,4,16,128]{3,2,1,0:T(8,128)(2,1)S(1)}, bf16[32,4,16,128]{3,2,1,0:T(8,128)(2,1)S(1)}, u32[]{:S(2)}, u32[]{:S(2)}) collective-permute-start(bf16[32,4,16,128]{3,2,1,0:T(8,128)(2,1)S(1)} %slice.3), channel_id=1, source_target_pairs={{0,1},{1,0},{2,3},{3,2},{4,5},{5,4},{6,7},{7,6},{8,9},{9,8},{10,11... | collective-permute-start | bytes 1572872 | tf_op jit(solution)/shard_map/ppermute | solution.py:212

commit v6 on v5

--- a/solution.py
+++ b/solution.py
@@ -127,7 +127,7 @@
         for side in range(blocks):
             for at in range(blocks):
                 piece = mixed[side * LANES : (side + 1) * LANES, at * LANES : (at + 1) * LANES]
-                out[at, pl.ds((2 * side + first) * per, per)] = piece.reshape(per, rows, LANES)
+                out[:, 2 * side + first, at] = piece.reshape(per, rows, LANES)
 
 
 def mix(got, other):
@@ -135,7 +135,7 @@
     depth, width = sources * rows, parts // 2 * LANES
     return pl.pallas_call(
         mix_kernel,
-        out_shape=jax.ShapeDtypeStruct((parts // 2, 2 * width // rows, rows, LANES), BF16),
+        out_shape=jax.ShapeDtypeStruct((LANES // rows, parts, parts // 2, rows, LANES), BF16),
         in_specs=in_vmem(2),
         out_specs=in_vmem(1)[0],
         compiler_params=params(),
@@ -204,23 +204,35 @@
     theirs = lax.ppermute(mine, "core", SWAP)
     messages, normed = front(pair, jnp.stack([ln_gain, ln_bias]), mine, theirs)
     shape = messages.shape
-    halves = [[part * half + at for at in range(half)] for part in range(2)]
+    per = LANES // rows
+    z_count = depth // per
+    halves = [
+        [z * per + y for y in range(per) for z in range(part * z_count // 2, (part + 1) * z_count // 2)]
+        for part in range(2)
+    ]
     got = lax.all_to_all(
         messages.reshape(half, -1, LANES), "row", split_axis=0, concat_axis=0, tiled=True, axis_index_groups=halves
     ).reshape(shape)
-    got, normed, w_gate, out_gain, out_bias = lax.optimization_barrier((got, normed, w_gate, out_gain, out_bias))
+    got, normed, w_gate, out_gain, out_bias, w_out = lax.optimization_barrier(
+        (got, normed, w_gate, out_gain, out_bias, w_out)
+    )
     other = lax.ppermute(got[:, : shape[1] // 2], "core", SWAP)
     gate = output_gate(normed, w_gate)
-    gain = jnp.broadcast_to(out_gain[:, None], (chans, LANES))
-    bias = jnp.broadcast_to(out_bias[:, None], (chans, LANES))
-    got, gate, gain, bias = lax.optimization_barrier((got, gate, gain, bias))
-
-    mixed = mix(got, other).reshape(x_count * depth, rows, LANES)
-    group = [x_count * row + x for x in range(x_count) for row in range(depth)]
+
+    def in_order(array):
+        return jnp.swapaxes(array.reshape(x_count, half, -1), 0, 1).reshape(chans, -1)
+
+    gain = jnp.broadcast_to(in_order(out_gain), (chans, LANES))
+    bias = jnp.broadcast_to(in_order(out_bias), (chans, LANES))
+    got, gate, gain, bias, out_weights = lax.optimization_barrier((got, gate, gain, bias, in_order(w_out)))
+
+    mixed = mix(got, other).reshape(depth * x_count, rows, LANES)
+    group = [x_count * (z * per + y) + x for y in range(per) for z in range(z_count) for x in range(x_count)]
     mixed = lax.all_to_all(
         mixed, ("row", "x"), split_axis=0, concat_axis=0, tiled=True, axis_index_groups=[group]
     )
-    return finish(mixed.reshape(x_count, 2, half, rows, LANES), gain, bias, w_out, gate)
+    mixed = mixed.reshape(per, 2, z_count // 2 * x_count, rows, LANES)
+    return finish(mixed, gain, bias, out_weights, gate)
 
 
 def solution(mesh):

time: 104 us -> 103 us (level)
  starting transfers between devices: 14.9 us -> 12.6 us
  blocking collectives: 78.5 us -> 79.6 us
    ppermute x1, starting transfers between devices: 6.11 us -> 3.86 us  [shards(): other = lax.ppermute(got[:, :shape[1] // 2], 'core', SWAP)]
    all_to_all x1, blocking collectives: 33 us -> 34.1 us  [shards(): lax.all_to_all(messages.reshape(half, -1, LANES), 'row', split_axis=0, co...]
where the time goes in v6:
time: 103 us; the launch traced here: 102 us
  blocking collectives  79.6 us (77%)
  starting transfers between devices  12.6 us (12%)
  Pallas kernels  7.09 us (7%)
  other arithmetic  1.42 us (1%)
    all_to_all x1, blocking collectives, shards(): lax.all_to_all(mixed, ('row', 'x'), split_axis=0, concat_axis=0, tiled=Tr...  45.5 us
    all_to_all x1, blocking collectives, shards(): lax.all_to_all(messages.reshape(half, -1, LANES), 'row', split_axis=0, co...  34.1 us
    ppermute x1, starting transfers between devices, shards(): theirs = lax.ppermute(mine, 'core', SWAP)  8.77 us
    pallas_call x1, Pallas kernels, front(): pl.pallas_call(front_kernel, out_shape=(jax.ShapeDtypeStruct((slab, 2 * s...  4.31 us
    ppermute x1, starting transfers between devices, shards(): other = lax.ppermute(got[:, :shape[1] // 2], 'core', SWAP)  3.86 us
  transfers between devices with their start and end apart: 2, of which 2 were waited for; matrix products, arithmetic and copies ran while one was open for 1% of the time, Pallas kernels for 0%

profile of v6, /device:TPU:1, one launch (start us, length us, event | category | flops | bytes accessed | tf_op | source)
XLA Modules:
  0.0 102.1 jit_solution(17689602968792646230)
XLA Ops:
  0.0 0.7 pad_maximum_fusion.mine
  0.7 8.8 %collective-permute-start = (bf16[4,16,128]{2,1,0:T(8,128)(2,1)S(1)}, bf16[4,16,128]{2,1,0:T(8,128)(2,1)S(1)}, u32[]{:S(2)}, u32[]{:S(2)}) collective-permute-start(bf16[4,16,128]{2,1,0:T(8,128)(2,1)S(1)} %pad_maximum_fusion.mine), channel_id=1, source_target_pairs={{0,1},{1,0},{2,3},{3,2},{4,5},{5,4},{6,7},{7,6},{8,9},{9,8},{10,11... | collective-permute-start | bytes 49160 | tf_op jit(solution)/shard_map/ppermute | solution.py:204
  9.5 0.7 pad_maximum_fusion.1.scale
  10.2 0.0 copy-start.1
  10.2 0.0 copy-start
  10.2 0.1 collective-permute-done.theirs
  10.3 4.3 %shard_map.109 = (bf16[32,8,16,128]{3,2,1,0:T(8,128)(2,1)S(1)}, bf16[128,2048]{1,0:T(8,128)(2,1)S(1)}) custom-call(bf16[16,1024,128]{2,1,0:T(8,128)(2,1)} %pair.1, f32[2,128]{1,0:T(2,128)S(1)} %pad_maximum_fusion.1.scale, bf16[4,16,128]{2,1,0:T(8,128)(2,1)S(1)} %pad_maximum_fusion.mine, bf16[4,16,128]{2,1,0:T(8,128)(2,1)S(1)} %collective-permute-done.theirs), custom_call_target="tpu_custom_call" | custom-call | flops 1879048192 | bytes 4194304 | tf_op jit(solution)/shard_map/pallas_call | solution.py:71
  14.7 34.1 %all_to_all.10 = bf16[32,128,128]{2,1,0:T(8,128)(2,1)S(1)} all-to-all(bf16[32,128,128]{2,1,0:T(8,128)(2,1)S(1)} %bitcast.32), channel_id=1, replica_groups={{0,64,128,192,8,72,136,200,16,80,144,208,24,88,152,216,32,96,160,224,40..., dimensions={0} | all-to-all | bytes 2097152 | tf_op jit(solution)/shard_map/all_to_all | solution.py:213
  48.8 3.9 %collective-permute-start.1 = (bf16[32,4,16,128]{3,2,1,0:T(8,128)(2,1)S(1)}, bf16[32,4,16,128]{3,2,1,0:T(8,128)(2,1)S(1)}, u32[]{:S(2)}, u32[]{:S(2)}) collective-permute-start(bf16[32,4,16,128]{3,2,1,0:T(8,128)(2,1)S(1)} %slice.3), channel_id=1, source_target_pairs={{0,1},{1,0},{2,3},{3,2},{4,5},{5,4},{6,7},{7,6},{8,9},{9,8},{10,11... | collective-permute-start | bytes 1572872 | tf_op jit(solution)/shard_map/ppermute | solution.py:219
  52.7 0.0 copy-done.2
  52.7 0.1 reshape.30
  52.8 0.1 reshape.31
  52.8 0.1 copy.16
  52.9 0.1 broadcast_in_dim.16
  53.0 0.1 copy.15
  53.1 0.1 broadcast_in_dim.14
  53.2 0.0 copy-done.1
  53.3 0.3 shard_map.110.gate
  53.6 0.1 broadcast_in_dim.15.gain
  53.7 0.1 broadcast_in_dim.17.bias
  53.8 0.4 collective-permute-done.1.other
  54.2 0.7 shard_map.111
  54.9 45.5 %all_to_all.11 = bf16[256,16,128]{2,1,0:T(8,128)(2,1)S(1)} all-to-all(bf16[256,16,128]{2,1,0:T(8,128)(2,1)S(1)} %bitcast.31), channel_id=1, replica_groups={{0,2,4,6,64,66,68,70,128,130,132,134,192,194,196,198,256,258,260,262,32..., dimensions={0} | all-to-all | bytes 2097152 | tf_op jit(solution)/shard_map/all_to_all | solution.py:231
  100.4 1.7 %shard_map.112 = bf16[16,128,128]{2,1,0:T(8,128)(2,1)} custom-call(bf16[8,2,16,16,128]{4,3,2,1,0:T(8,128)(2,1)S(1)} %bitcast.30, f32[128,128]{1,0:T(8,128)S(1)} %broadcast_in_dim.15.gain, f32[128,128]{1,0:T(8,128)S(1)} %broadcast_in_dim.17.bias, bf16[128,128]{1,0:T(8,128)(2,1)S(1)} %bitcast.33, f32[16,128,128]{2,1,0:T(8,128)S(1)} %shard_map.110.gate), custom_call_target="tpu_custom_call" | custom-call | flops 67108864 | bytes 2621440 | tf_op jit(solution)/shard_map/pallas_call | solution.py:173
  (6 shorter events, 0.1 us)
Async XLA Ops:
  0.7 9.6 %collective-permute-start = (bf16[4,16,128]{2,1,0:T(8,128)(2,1)S(1)}, bf16[4,16,128]{2,1,0:T(8,128)(2,1)S(1)}, u32[]{:S(2)}, u32[]{:S(2)}) collective-permute-start(bf16[4,16,128]{2,1,0:T(8,128)(2,1)S(1)} %pad_maximum_fusion.mine), channel_id=1, source_target_pairs={{0,1},{1,0},{2,3},{3,2},{4,5},{5,4},{6,7},{7,6},{8,9},{9,8},{10,11... | collective-permute-start | bytes 49160 | tf_op jit(solution)/shard_map/ppermute | solution.py:204
  10.2 42.5 %copy-start.2 = (f32[128]{0:T(128)S(1)}, f32[128]{0:T(128)}, u32[]{:S(2)}) copy-start(f32[128]{0:T(128)} %param.19) | copy-start | bytes 1540
  10.2 42.6 %copy-start.3 = (f32[128]{0:T(128)S(1)}, f32[128]{0:T(128)}, u32[]{:S(2)}) copy-start(f32[128]{0:T(128)} %param.20) | copy-start | bytes 1540
  10.2 43.0 %copy-start.1 = (bf16[128,128]{1,0:T(8,128)(2,1)S(1)}, bf16[128,128]{1,0:T(8,128)(2,1)}, u32[]{:S(2)}) copy-start(bf16[128,128]{1,0:T(8,128)(2,1)} %param.21) | copy-start | bytes 98308
  10.2 43.1 %copy-start = (bf16[128,128]{1,0:T(8,128)(2,1)S(1)}, bf16[128,128]{1,0:T(8,128)(2,1)}, u32[]{:S(2)}) copy-start(bf16[128,128]{1,0:T(8,128)(2,1)} %weights) | copy-start | bytes 98308
  48.8 5.4 %collective-permute-start.1 = (bf16[32,4,16,128]{3,2,1,0:T(8,128)(2,1)S(1)}, bf16[32,4,16,128]{3,2,1,0:T(8,128)(2,1)S(1)}, u32[]{:S(2)}, u32[]{:S(2)}) collective-permute-start(bf16[32,4,16,128]{3,2,1,0:T(8,128)(2,1)S(1)} %slice.3), channel_id=1, source_target_pairs={{0,1},{1,0},{2,3},{3,2},{4,5},{5,4},{6,7},{7,6},{8,9},{9,8},{10,11... | collective-permute-start | bytes 1572872 | tf_op jit(solution)/shard_map/ppermute | solution.py:219

commit v7 on v6

--- a/solution.py
+++ b/solution.py
@@ -24,15 +24,8 @@
     return [pl.BlockSpec(memory_space=pltpu.VMEM)] * count
 
 
-def normalise(values, gain, bias):
-    values = values.T.astype(F32)
-    centred = values - jnp.mean(values, axis=0, keepdims=True)
-    var = jnp.mean(centred * centred, axis=0, keepdims=True)
-    return (centred * lax.rsqrt(var + EPS) * gain + bias).astype(BF16)
-
-
-def front_kernel(pair, scale, mine, theirs, out, own, weights, held, sems):
-    core, x = lax.axis_index("core"), lax.axis_index("x")
+def measure_kernel(pair, values, stats, held, sems):
+    core = lax.axis_index("core")
     steps, rows, _, chans = held.shape
     copies = []
     for step in range(steps):
@@ -40,14 +33,50 @@
         copies.append(pltpu.make_async_copy(pair.at[:, pl.ds(at, LANES), :], held.at[step], sems.at[step]))
     for copy in copies:
         copy.start()
+    for step in range(steps):
+        copies[step].wait()
+        block = held[step].reshape(rows * LANES, chans).T
+        values[step] = block
+        block = block.astype(F32)
+        mean = jnp.mean(block, axis=0, keepdims=True)
+        centred = block - mean
+        var = jnp.mean(centred * centred, axis=0, keepdims=True)
+        stats[step, 0:1] = mean
+        stats[step, 1:2] = lax.rsqrt(var + EPS)
+
+
+def measure_columns(pair):
+    rows, tokens, chans = pair.shape
+    steps = tokens // (2 * LANES)
+    return pl.pallas_call(
+        measure_kernel,
+        out_shape=(
+            jax.ShapeDtypeStruct((steps, chans, rows * LANES), BF16),
+            jax.ShapeDtypeStruct((steps, 2, rows * LANES), F32),
+        ),
+        in_specs=[pl.BlockSpec(memory_space=pltpu.HBM)],
+        out_specs=tuple(in_vmem(2)),
+        scratch_shapes=[pltpu.VMEM((steps, rows, LANES, chans), BF16), pltpu.SemaphoreType.DMA((steps,))],
+        compiler_params=params(LARGE_LIMIT),
+        cost_estimate=pl.CostEstimate(
+            flops=6 * steps * rows * LANES * chans,
+            bytes_accessed=4 * steps * rows * LANES * chans,
+            transcendentals=steps * rows * LANES,
+        ),
+    )(pair)
+
+
+def project_kernel(values, stats, gain, bias, mine, theirs, out, own, weights):
+    core, x = lax.axis_index("core"), lax.axis_index("x")
     weights[:, core] = mine[...]
     weights[:, 1 - core] = theirs[...]
+    steps, chans, pairs = values.shape
     slab = 2 * mine.shape[1]
     both = weights[...].reshape(4 * slab, chans)
-    columns = scale[...].T
+    gains, biases = gain[...].T, bias[...].T
     for step in range(steps):
-        copies[step].wait()
-        normed = normalise(held[step].reshape(rows * LANES, chans), columns[:, 0:1], columns[:, 1:2])
+        normed = (values[step].astype(F32) - stats[step, 0:1]) * stats[step, 1:2]
+        normed = (normed * gains + biases).astype(BF16)
 
         @pl.when(step == x)
         def _():
@@ -57,37 +86,32 @@
 
         def gated(first):
             value = jax.nn.sigmoid(got[first : first + slab]) * got[first + slab : first + 2 * slab]
-            parts = [value[:, k * LANES : (k + 1) * LANES] for k in range(rows)]
+            parts = [value[:, at : at + LANES] for at in range(0, pairs, LANES)]
             return jnp.swapaxes(jnp.stack(parts, axis=0), 0, 1).astype(BF16)
 
         out[:, step] = gated(0)
         out[:, steps + step] = gated(2 * slab)
 
 
-def front(pair, scale, mine, theirs):
-    rows, tokens, chans = pair.shape
-    steps = tokens // (2 * LANES)
+def project(values, stats, gain, bias, mine, theirs):
+    steps, chans, pairs = values.shape
     slab = 2 * mine.shape[1]
     return pl.pallas_call(
-        front_kernel,
+        project_kernel,
         out_shape=(
-            jax.ShapeDtypeStruct((slab, 2 * steps, rows, LANES), BF16),
-            jax.ShapeDtypeStruct((chans, rows * LANES), BF16),
-        ),
-        in_specs=[pl.BlockSpec(memory_space=pltpu.HBM)] + in_vmem(3),
+            jax.ShapeDtypeStruct((slab, 2 * steps, pairs // LANES, LANES), BF16),
+            jax.ShapeDtypeStruct((chans, pairs), BF16),
+        ),
+        in_specs=in_vmem(6),
         out_specs=tuple(in_vmem(2)),
-        scratch_shapes=[
-            pltpu.VMEM((4, 2) + mine.shape[1:], BF16),
-            pltpu.VMEM((steps, rows, LANES, chans), BF16),
-            pltpu.SemaphoreType.DMA((steps,)),
-        ],
-        compiler_params=params(LARGE_LIMIT),
-        cost_estimate=pl.CostEstimate(
-            flops=14 * steps * rows * LANES * chans * chans,
-            bytes_accessed=4 * steps * rows * LANES * chans,
-            transcendentals=steps * rows * LANES * chans,
-        ),
-    )(pair, scale, mine, theirs)
+        scratch_shapes=[pltpu.VMEM((4, 2) + mine.shape[1:], BF16)],
+        compiler_params=params(),
+        cost_estimate=pl.CostEstimate(
+            flops=8 * steps * pairs * slab * chans,
+            bytes_accessed=4 * steps * pairs * chans,
+            transcendentals=2 * steps * pairs * slab,
+        ),
+    )(values, stats, gain.reshape(1, chans), bias.reshape(1, chans), mine, theirs)
 
 
 def gate_kernel(normed, weights, out):
@@ -110,39 +134,57 @@
     )(normed, weights)
 
 
-def mix_kernel(got, other, out):
-    core = lax.axis_index("core")
+def mix_rows(got, left, first, out):
     sources, parts, rows, _ = got.shape
     blocks = parts // 2
-    per = LANES // rows
-
-    def joined(ref, first):
+
+    def joined(ref, start):
         return jnp.concatenate(
-            [ref[:, first + at].reshape(sources * rows, LANES) for at in range(blocks)], axis=1
+            [ref[:, start + at].reshape(sources * rows, LANES) for at in range(blocks)], axis=1
         )
 
-    right = joined(got, blocks)
-    for ref, first in ((got, core), (other, 1 - core)):
-        mixed = lax.dot_general(joined(ref, 0), right, OVER_FIRST, preferred_element_type=F32).astype(BF16)
-        for side in range(blocks):
-            for at in range(blocks):
-                piece = mixed[side * LANES : (side + 1) * LANES, at * LANES : (at + 1) * LANES]
-                out[:, 2 * side + first, at] = piece.reshape(per, rows, LANES)
+    mixed = lax.dot_general(joined(left, 0), joined(got, blocks), OVER_FIRST, preferred_element_type=F32)
+    mixed = mixed.astype(BF16)
+    for side in range(blocks):
+        for at in range(blocks):
+            piece = mixed[side * LANES : (side + 1) * LANES, at * LANES : (at + 1) * LANES]
+            out[:, 2 * side + first, at] = piece.reshape(LANES // rows, rows, LANES)
+
+
+def mix_own_kernel(got, out):
+    mix_rows(got, got, 0, out)
+
+
+def mix_other_kernel(got, other, begun, out):
+    core = lax.axis_index("core")
+    for side in range(got.shape[1] // 2):
+        out[:, 2 * side + core] = begun[:, 2 * side]
+    mix_rows(got, other, 1 - core, out)
 
 
 def mix(got, other):
     sources, parts, rows, _ = got.shape
     depth, width = sources * rows, parts // 2 * LANES
-    return pl.pallas_call(
-        mix_kernel,
-        out_shape=jax.ShapeDtypeStruct((LANES // rows, parts, parts // 2, rows, LANES), BF16),
-        in_specs=in_vmem(2),
+    shape = jax.ShapeDtypeStruct((LANES // rows, parts, parts // 2, rows, LANES), BF16)
+    cost = pl.CostEstimate(
+        flops=2 * depth * width * width, bytes_accessed=2 * (2 * depth * width + width * width), transcendentals=0
+    )
+    begun = pl.pallas_call(
+        mix_own_kernel,
+        out_shape=shape,
+        in_specs=in_vmem(1),
         out_specs=in_vmem(1)[0],
         compiler_params=params(),
-        cost_estimate=pl.CostEstimate(
-            flops=4 * depth * width * width, bytes_accessed=2 * (3 * depth * width + 2 * width * width), transcendentals=0
-        ),
-    )(got, other)
+        cost_estimate=cost,
+    )(got)
+    return pl.pallas_call(
+        mix_other_kernel,
+        out_shape=shape,
+        in_specs=in_vmem(3),
+        out_specs=in_vmem(1)[0],
+        compiler_params=params(),
+        cost_estimate=cost,
+    )(got, other, begun)
 
 
 def finish_kernel(mixed, gain, bias, weights, gate, out, held, sems):
@@ -202,7 +244,8 @@
 
     mine = jnp.stack([w.T for w in (w_a_gate, w_a_proj, w_b_gate, w_b_proj)])
     theirs = lax.ppermute(mine, "core", SWAP)
-    messages, normed = front(pair, jnp.stack([ln_gain, ln_bias]), mine, theirs)
+    values, stats = measure_columns(pair)
+    messages, normed = project(values, stats, ln_gain, ln_bias, mine, theirs)
     shape = messages.shape
     per = LANES // rows
     z_count = depth // per

time: 103 us -> 103 us (level)
    pallas_call x2 -> x4, Pallas kernels: 5.04 us -> 6.05 us  [the longest x1 2.68 us: project(): pl.pallas_call(project_kernel, out_shape=(jax.ShapeDtypeStruct((slab, 2 *...]
  transfers between devices with their start and end apart: 2 -> 2, of which waited for: 2 -> 0; matrix products, arithmetic and copies ran while one was open for 1% -> 1% of each run, Pallas kernels for 0% -> 3%
where the time goes in v7:
time: 103 us; the launch traced here: 102 us
  blocking collectives  79.5 us (77%)
  starting transfers between devices  12.2 us (12%)
  Pallas kernels  8.1 us (8%)
    all_to_all x1, blocking collectives, shards(): lax.all_to_all(mixed, ('row', 'x'), split_axis=0, concat_axis=0, tiled=Tr...  44.8 us
    all_to_all x1, blocking collectives, shards(): lax.all_to_all(messages.reshape(half, -1, LANES), 'row', split_axis=0, co...  34.7 us
    ppermute x1, starting transfers between devices, shards(): theirs = lax.ppermute(mine, 'core', SWAP)  8.92 us
    ppermute x1, starting transfers between devices, shards(): other = lax.ppermute(got[:, :shape[1] // 2], 'core', SWAP)  3.3 us
    pallas_call x1, Pallas kernels, project(): pl.pallas_call(project_kernel, out_shape=(jax.ShapeDtypeStruct((slab, 2 *...  2.68 us
    pallas_call x1, Pallas kernels, measure_columns(): pl.pallas_call(measure_kernel, out_shape=(jax.ShapeDtypeStruct((steps, ch...  2.42 us
  transfers between devices with their start and end apart: 2, of which 0 were waited for; matrix products, arithmetic and copies ran while one was open for 1% of the time, Pallas kernels for 3%

profile of v7, /device:TPU:1, one launch (start us, length us, event | category | flops | bytes accessed | tf_op | source)
XLA Modules:
  0.0 101.5 jit_solution(7818084095052161598)
XLA Ops:
  0.0 0.8 pad_maximum_fusion.mine
  0.8 0.0 copy-start.3
  0.8 0.0 copy-start
  0.8 8.9 %collective-permute-start = (bf16[4,16,128]{2,1,0:T(8,128)(2,1)S(1)}, bf16[4,16,128]{2,1,0:T(8,128)(2,1)S(1)}, u32[]{:S(2)}, u32[]{:S(2)}) collective-permute-start(bf16[4,16,128]{2,1,0:T(8,128)(2,1)S(1)} %pad_maximum_fusion.mine), channel_id=1, source_target_pairs={{0,1},{1,0},{2,3},{3,2},{4,5},{5,4},{6,7},{7,6},{8,9},{9,8},{10,11... | collective-permute-start | bytes 49160 | tf_op jit(solution)/shard_map/ppermute | solution.py:246
  9.7 2.4 %shard_map.109 = (bf16[4,128,2048]{2,1,0:T(8,128)(2,1)S(1)}, f32[4,2,2048]{2,1,0:T(2,128)S(1)}) custom-call(bf16[16,1024,128]{2,1,0:T(8,128)(2,1)} %pair.1), custom_call_target="tpu_custom_call" | custom-call | flops 6291456 | bytes 4194304 | tf_op jit(solution)/shard_map/pallas_call | solution.py:51
  12.2 0.0 collective-permute-done.theirs
  12.2 0.0 copy-done.2
  12.2 2.7 %shard_map.110 = (bf16[32,8,16,128]{3,2,1,0:T(8,128)(2,1)S(1)}, bf16[128,2048]{1,0:T(8,128)(2,1)S(1)}) custom-call(bf16[4,128,2048]{2,1,0:T(8,128)(2,1)S(1)} %get-tuple-element.20.values, f32[4,2,2048]{2,1,0:T(2,128)S(1)} %get-tuple-element.21.stats, f32[1,128]{1,0:T(1,128)S(1)} %bitcast.35, f32[1,128]{1,0:T(1,128)S(1)} %bitcast.36, ...), custom_call_target="tpu_custom_call" | custom-call | flops 268435456 | bytes 4194304 | tf_op jit(solution)/shard_map/pallas_call | solution.py:99
  14.9 34.7 %all_to_all.10 = bf16[32,128,128]{2,1,0:T(8,128)(2,1)S(1)} all-to-all(bf16[32,128,128]{2,1,0:T(8,128)(2,1)S(1)} %bitcast.33), channel_id=1, replica_groups={{0,64,128,192,8,72,136,200,16,80,144,208,24,88,152,216,32,96,160,224,40..., dimensions={0} | all-to-all | bytes 2097152 | tf_op jit(solution)/shard_map/all_to_all | solution.py:256
  49.6 3.3 %collective-permute-start.1 = (bf16[32,4,16,128]{3,2,1,0:T(8,128)(2,1)S(1)}, bf16[32,4,16,128]{3,2,1,0:T(8,128)(2,1)S(1)}, u32[]{:S(2)}, u32[]{:S(2)}) collective-permute-start(bf16[32,4,16,128]{3,2,1,0:T(8,128)(2,1)S(1)} %slice.3), channel_id=1, source_target_pairs={{0,1},{1,0},{2,3},{3,2},{4,5},{5,4},{6,7},{7,6},{8,9},{9,8},{10,11... | collective-permute-start | bytes 1572872 | tf_op jit(solution)/shard_map/ppermute | solution.py:262
  52.9 0.1 reshape.38
  53.0 0.1 reshape.39
  53.1 0.1 copy.16
  53.2 0.1 broadcast_in_dim.16
  53.3 0.1 copy.15
  53.4 0.1 broadcast_in_dim.14
  53.5 0.3 shard_map.111.gate
  53.9 0.1 broadcast_in_dim.15.gain
  53.9 0.1 broadcast_in_dim.17.bias
  54.0 0.5 shard_map.112.begun
  54.5 0.0 collective-permute-done.1.other
  54.5 0.5 shard_map.113
  55.0 44.8 %all_to_all.11 = bf16[256,16,128]{2,1,0:T(8,128)(2,1)S(1)} all-to-all(bf16[256,16,128]{2,1,0:T(8,128)(2,1)S(1)} %bitcast.31), channel_id=1, replica_groups={{0,2,4,6,64,66,68,70,128,130,132,134,192,194,196,198,256,258,260,262,32..., dimensions={0} | all-to-all | bytes 2097152 | tf_op jit(solution)/shard_map/all_to_all | solution.py:274
  99.8 1.7 %shard_map.114 = bf16[16,128,128]{2,1,0:T(8,128)(2,1)} custom-call(bf16[8,2,16,16,128]{4,3,2,1,0:T(8,128)(2,1)S(1)} %bitcast.32, f32[128,128]{1,0:T(8,128)S(1)} %broadcast_in_dim.15.gain, f32[128,128]{1,0:T(8,128)S(1)} %broadcast_in_dim.17.bias, bf16[128,128]{1,0:T(8,128)(2,1)S(1)} %bitcast.34, f32[16,128,128]{2,1,0:T(8,128)S(1)} %shard_map.111.gate), custom_call_target="tpu_custom_call" | custom-call | flops 67108864 | bytes 2621440 | tf_op jit(solution)/shard_map/pallas_call | solution.py:215
  (11 shorter events, 0.1 us)
Async XLA Ops:
  0.0 12.2 %copy-start.2 = (f32[128]{0:T(128)S(1)}, f32[128]{0:T(128)}, u32[]{:S(2)}) copy-start(f32[128]{0:T(128)} %param.13) | copy-start | bytes 1540
  0.0 12.2 %copy-start.1 = (f32[128]{0:T(128)S(1)}, f32[128]{0:T(128)}, u32[]{:S(2)}) copy-start(f32[128]{0:T(128)} %param.12) | copy-start | bytes 1540
  0.8 52.1 %copy-start.4 = (f32[128]{0:T(128)S(1)}, f32[128]{0:T(128)}, u32[]{:S(2)}) copy-start(f32[128]{0:T(128)} %param.19) | copy-start | bytes 1540
  0.8 52.2 %copy-start.5 = (f32[128]{0:T(128)S(1)}, f32[128]{0:T(128)}, u32[]{:S(2)}) copy-start(f32[128]{0:T(128)} %param.20) | copy-start | bytes 1540
  0.8 52.7 %copy-start.3 = (bf16[128,128]{1,0:T(8,128)(2,1)S(1)}, bf16[128,128]{1,0:T(8,128)(2,1)}, u32[]{:S(2)}) copy-start(bf16[128,128]{1,0:T(8,128)(2,1)} %param.21) | copy-start | bytes 98308
  0.8 52.7 %copy-start = (bf16[128,128]{1,0:T(8,128)(2,1)S(1)}, bf16[128,128]{1,0:T(8,128)(2,1)}, u32[]{:S(2)}) copy-start(bf16[128,128]{1,0:T(8,128)(2,1)} %weights) | copy-start | bytes 98308
  0.8 11.4 %collective-permute-start = (bf16[4,16,128]{2,1,0:T(8,128)(2,1)S(1)}, bf16[4,16,128]{2,1,0:T(8,128)(2,1)S(1)}, u32[]{:S(2)}, u32[]{:S(2)}) collective-permute-start(bf16[4,16,128]{2,1,0:T(8,128)(2,1)S(1)} %pad_maximum_fusion.mine), channel_id=1, source_target_pairs={{0,1},{1,0},{2,3},{3,2},{4,5},{5,4},{6,7},{7,6},{8,9},{9,8},{10,11... | collective-permute-start | bytes 49160 | tf_op jit(solution)/shard_map/ppermute | solution.py:246
  49.6 4.9 %collective-permute-start.1 = (bf16[32,4,16,128]{3,2,1,0:T(8,128)(2,1)S(1)}, bf16[32,4,16,128]{3,2,1,0:T(8,128)(2,1)S(1)}, u32[]{:S(2)}, u32[]{:S(2)}) collective-permute-start(bf16[32,4,16,128]{3,2,1,0:T(8,128)(2,1)S(1)} %slice.3), channel_id=1, source_target_pairs={{0,1},{1,0},{2,3},{3,2},{4,5},{5,4},{6,7},{7,6},{8,9},{9,8},{10,11... | collective-permute-start | bytes 1572872 | tf_op jit(solution)/shard_map/ppermute | solution.py:262

commit v8 on v7

--- a/solution.py
+++ b/solution.py
@@ -66,8 +66,8 @@
     )(pair)
 
 
-def project_kernel(values, stats, gain, bias, mine, theirs, out, own, weights):
-    core, x = lax.axis_index("core"), lax.axis_index("x")
+def project_kernel(values, stats, gain, bias, mine, theirs, out, normed_out, weights):
+    core = lax.axis_index("core")
     weights[:, core] = mine[...]
     weights[:, 1 - core] = theirs[...]
     steps, chans, pairs = values.shape
@@ -77,11 +77,7 @@
     for step in range(steps):
         normed = (values[step].astype(F32) - stats[step, 0:1]) * stats[step, 1:2]
         normed = (normed * gains + biases).astype(BF16)
-
-        @pl.when(step == x)
-        def _():
-            own[...] = normed
-
+        normed_out[step] = normed
         got = jnp.dot(both, normed, preferred_element_type=F32)
 
         def gated(first):
@@ -100,7 +96,7 @@
         project_kernel,
         out_shape=(
             jax.ShapeDtypeStruct((slab, 2 * steps, pairs // LANES, LANES), BF16),
-            jax.ShapeDtypeStruct((chans, pairs), BF16),
+            jax.ShapeDtypeStruct((steps, chans, pairs), BF16),
         ),
         in_specs=in_vmem(6),
         out_specs=tuple(in_vmem(2)),
@@ -115,12 +111,12 @@
 
 
 def gate_kernel(normed, weights, out):
-    got = lax.dot_general(normed[...], weights[...], OVER_FIRST, preferred_element_type=F32)
+    got = lax.dot_general(normed[lax.axis_index("x")], weights[...], OVER_FIRST, preferred_element_type=F32)
     out[...] = jax.nn.sigmoid(got).reshape(out.shape)
 
 
 def output_gate(normed, weights):
-    chans, pairs = normed.shape
+    _, chans, pairs = normed.shape
     rows = pairs // LANES
     return pl.pallas_call(
         gate_kernel,
@@ -217,7 +213,7 @@
         out_shape=jax.ShapeDtypeStruct((rows, width, outs), BF16),
         in_specs=in_vmem(5),
         out_specs=pl.BlockSpec(memory_space=pltpu.HBM),
-        scratch_shapes=[pltpu.VMEM((4, rows // 4, width, outs), BF16), pltpu.SemaphoreType.DMA((4,))],
+        scratch_shapes=[pltpu.VMEM((2, rows // 2, width, outs), BF16), pltpu.SemaphoreType.DMA((2,))],
         compiler_params=params(),
         cost_estimate=pl.CostEstimate(
             flops=2 * rows * width * chans * chans, bytes_accessed=10 * chans * rows * width, transcendentals=rows * width

time: 103 us -> 104 us (level)
  transfers between devices with their start and end apart: 2 -> 2, of which waited for: 0 -> 1; matrix products, arithmetic and copies ran while one was open for 1% -> 1% of each run, Pallas kernels for 3% -> 3%
where the time goes in v8:
time: 104 us; the launch traced here: 103 us
  blocking collectives  79.6 us (77%)
  starting transfers between devices  12.2 us (12%)
  Pallas kernels  8.25 us (8%)
  local copies, waits for them, and re-layouts  1.6 us (2%)
    all_to_all x1, blocking collectives, shards(): lax.all_to_all(mixed, ('row', 'x'), split_axis=0, concat_axis=0, tiled=Tr...  44.8 us
    all_to_all x1, blocking collectives, shards(): lax.all_to_all(messages.reshape(half, -1, LANES), 'row', split_axis=0, co...  34.8 us
    ppermute x1, starting transfers between devices, shards(): theirs = lax.ppermute(mine, 'core', SWAP)  8.92 us
    ppermute x1, starting transfers between devices, shards(): other = lax.ppermute(got[:, :shape[1] // 2], 'core', SWAP)  3.27 us
    pallas_call x1, Pallas kernels, measure_columns(): pl.pallas_call(measure_kernel, out_shape=(jax.ShapeDtypeStruct((steps, ch...  2.42 us
  transfers between devices with their start and end apart: 2, of which 1 were waited for; matrix products, arithmetic and copies ran while one was open for 1% of the time, Pallas kernels for 3%

profile of v8, /device:TPU:1, one launch (start us, length us, event | category | flops | bytes accessed | tf_op | source)
XLA Modules:
  0.0 102.7 jit_solution(6698457410970324698)
XLA Ops:
  0.0 0.7 pad_maximum_fusion.mine
  0.8 8.9 %collective-permute-start = (bf16[4,16,128]{2,1,0:T(8,128)(2,1)S(1)}, bf16[4,16,128]{2,1,0:T(8,128)(2,1)S(1)}, u32[]{:S(2)}, u32[]{:S(2)}) collective-permute-start(bf16[4,16,128]{2,1,0:T(8,128)(2,1)S(1)} %pad_maximum_fusion.mine), channel_id=1, source_target_pairs={{0,1},{1,0},{2,3},{3,2},{4,5},{5,4},{6,7},{7,6},{8,9},{9,8},{10,11... | collective-permute-start | bytes 49160 | tf_op jit(solution)/shard_map/ppermute | solution.py:242
  9.7 2.4 %shard_map.109 = (bf16[4,128,2048]{2,1,0:T(8,128)(2,1)S(1)}, f32[4,2,2048]{2,1,0:T(2,128)S(1)}) custom-call(bf16[16,1024,128]{2,1,0:T(8,128)(2,1)} %pair.1), custom_call_target="tpu_custom_call" | custom-call | flops 6291456 | bytes 4194304 | tf_op jit(solution)/shard_map/pallas_call | solution.py:51
  12.1 1.8 %shard_map.110 = (bf16[32,8,16,128]{3,2,1,0:T(8,128)(2,1)S(1)}, bf16[4,128,2048]{2,1,0:T(8,128)(2,1)S(1)}) custom-call(bf16[4,128,2048]{2,1,0:T(8,128)(2,1)S(1)} %get-tuple-element.20.values, f32[4,2,2048]{2,1,0:T(2,128)S(1)} %get-tuple-element.21.stats, f32[1,128]{1,0:T(1,128)S(1)} %bitcast.35, f32[1,128]{1,0:T(1,128)S(1)} %bitcast.36, ...), custom_call_target="tpu_custom_call" | custom-call | flops 268435456 | bytes 4194304 | tf_op jit(solution)/shard_map/pallas_call | solution.py:95
  14.0 0.0 copy-start.4
  14.0 0.0 copy-start.3
  14.0 0.0 copy-start
  14.0 34.8 %all_to_all.10 = bf16[32,128,128]{2,1,0:T(8,128)(2,1)S(1)} all-to-all(bf16[32,128,128]{2,1,0:T(8,128)(2,1)S(1)} %bitcast.33), channel_id=1, replica_groups={{0,64,128,192,8,72,136,200,16,80,144,208,24,88,152,216,32,96,160,224,40..., dimensions={0} | all-to-all | bytes 2097152 | tf_op jit(solution)/shard_map/all_to_all | solution.py:252
  48.8 0.8 slice.3
  49.7 3.3 %collective-permute-start.1 = (bf16[32,4,16,128]{3,2,1,0:T(8,128)(2,1)}, bf16[32,4,16,128]{3,2,1,0:T(8,128)(2,1)}, u32[]{:S(2)}, u32[]{:S(2)}) collective-permute-start(bf16[32,4,16,128]{3,2,1,0:T(8,128)(2,1)} %slice.3), channel_id=1, source_target_pairs={{0,1},{1,0},{2,3},{3,2},{4,5},{5,4},{6,7},{7,6},{8,9},{9,8},{10,11... | collective-permute-start | bytes 1572872 | tf_op jit(solution)/shard_map/ppermute | solution.py:258
  53.0 0.1 reshape.38
  53.1 0.1 reshape.39
  53.1 0.1 copy.16
  53.2 0.1 broadcast_in_dim.16
  53.3 0.1 copy.15
  53.4 0.1 broadcast_in_dim.14
  53.6 0.4 shard_map.111.gate
  53.9 0.1 broadcast_in_dim.15.gain
  54.0 0.1 broadcast_in_dim.17.bias
  54.1 0.5 shard_map.112.begun
  54.6 0.2 collective-permute-done.1.other
  54.8 1.5 %shard_map.113 = bf16[8,8,4,16,128]{4,3,2,1,0:T(8,128)(2,1)S(1)} custom-call(bf16[32,8,16,128]{3,2,1,0:T(8,128)(2,1)S(1)} %bitcast.30, bf16[32,4,16,128]{3,2,1,0:T(8,128)(2,1)} %collective-permute-done.1.other, bf16[8,8,4,16,128]{4,3,2,1,0:T(8,128)(2,1)S(1)} %shard_map.112.begun), custom_call_target="tpu_custom_call" | custom-call | flops 268435456 | bytes 1572864 | tf_op jit(solution)/shard_map/pallas_call | solution.py:176
  56.3 44.8 %all_to_all.11 = bf16[256,16,128]{2,1,0:T(8,128)(2,1)S(1)} all-to-all(bf16[256,16,128]{2,1,0:T(8,128)(2,1)S(1)} %bitcast.31), channel_id=1, replica_groups={{0,2,4,6,64,66,68,70,128,130,132,134,192,194,196,198,256,258,260,262,32..., dimensions={0} | all-to-all | bytes 2097152 | tf_op jit(solution)/shard_map/all_to_all | solution.py:270
  101.1 1.7 %shard_map.114 = bf16[16,128,128]{2,1,0:T(8,128)(2,1)} custom-call(bf16[8,2,16,16,128]{4,3,2,1,0:T(8,128)(2,1)S(1)} %bitcast.32, f32[128,128]{1,0:T(8,128)S(1)} %broadcast_in_dim.15.gain, f32[128,128]{1,0:T(8,128)S(1)} %broadcast_in_dim.17.bias, bf16[128,128]{1,0:T(8,128)(2,1)S(1)} %bitcast.34, f32[16,128,128]{2,1,0:T(8,128)S(1)} %shard_map.111.gate), custom_call_target="tpu_custom_call" | custom-call | flops 67108864 | bytes 2621440 | tf_op jit(solution)/shard_map/pallas_call | solution.py:211
  (11 shorter events, 0.0 us)
Async XLA Ops:
  0.7 11.4 %copy-start.1 = (f32[128]{0:T(128)S(1)}, f32[128]{0:T(128)}, u32[]{:S(2)}) copy-start(f32[128]{0:T(128)} %param.12) | copy-start | bytes 1540
  0.7 11.4 %copy-start.2 = (f32[128]{0:T(128)S(1)}, f32[128]{0:T(128)}, u32[]{:S(2)}) copy-start(f32[128]{0:T(128)} %param.13) | copy-start | bytes 1540
  0.8 11.4 %collective-permute-start = (bf16[4,16,128]{2,1,0:T(8,128)(2,1)S(1)}, bf16[4,16,128]{2,1,0:T(8,128)(2,1)S(1)}, u32[]{:S(2)}, u32[]{:S(2)}) collective-permute-start(bf16[4,16,128]{2,1,0:T(8,128)(2,1)S(1)} %pad_maximum_fusion.mine), channel_id=1, source_target_pairs={{0,1},{1,0},{2,3},{3,2},{4,5},{5,4},{6,7},{7,6},{8,9},{9,8},{10,11... | collective-permute-start | bytes 49160 | tf_op jit(solution)/shard_map/ppermute | solution.py:242
  14.0 39.0 %copy-start.4 = (f32[128]{0:T(128)S(1)}, f32[128]{0:T(128)}, u32[]{:S(2)}) copy-start(f32[128]{0:T(128)} %param.19) | copy-start | bytes 1540
  14.0 39.1 %copy-start.5 = (f32[128]{0:T(128)S(1)}, f32[128]{0:T(128)}, u32[]{:S(2)}) copy-start(f32[128]{0:T(128)} %param.20) | copy-start | bytes 1540
  14.0 39.5 %copy-start.3 = (bf16[128,128]{1,0:T(8,128)(2,1)S(1)}, bf16[128,128]{1,0:T(8,128)(2,1)}, u32[]{:S(2)}) copy-start(bf16[128,128]{1,0:T(8,128)(2,1)} %param.21) | copy-start | bytes 98308
  14.0 39.6 %copy-start = (bf16[128,128]{1,0:T(8,128)(2,1)S(1)}, bf16[128,128]{1,0:T(8,128)(2,1)}, u32[]{:S(2)}) copy-start(bf16[128,128]{1,0:T(8,128)(2,1)} %weights) | copy-start | bytes 98308
  49.7 5.1 %collective-permute-start.1 = (bf16[32,4,16,128]{3,2,1,0:T(8,128)(2,1)}, bf16[32,4,16,128]{3,2,1,0:T(8,128)(2,1)}, u32[]{:S(2)}, u32[]{:S(2)}) collective-permute-start(bf16[32,4,16,128]{3,2,1,0:T(8,128)(2,1)} %slice.3), channel_id=1, source_target_pairs={{0,1},{1,0},{2,3},{3,2},{4,5},{5,4},{6,7},{7,6},{8,9},{9,8},{10,11... | collective-permute-start | bytes 1572872 | tf_op jit(solution)/shard_map/ppermute | solution.py:258

commit v9 on v7

--- a/solution.py
+++ b/solution.py
@@ -66,7 +66,7 @@
     )(pair)
 
 
-def project_kernel(values, stats, gain, bias, mine, theirs, out, own, weights):
+def project_kernel(values, stats, gain, bias, mine, theirs, out, own, weights, held):
     core, x = lax.axis_index("core"), lax.axis_index("x")
     weights[:, core] = mine[...]
     weights[:, 1 - core] = theirs[...]
@@ -77,11 +77,7 @@
     for step in range(steps):
         normed = (values[step].astype(F32) - stats[step, 0:1]) * stats[step, 1:2]
         normed = (normed * gains + biases).astype(BF16)
-
-        @pl.when(step == x)
-        def _():
-            own[...] = normed
-
+        held[step] = normed
         got = jnp.dot(both, normed, preferred_element_type=F32)
 
         def gated(first):
@@ -91,6 +87,7 @@
 
         out[:, step] = gated(0)
         out[:, steps + step] = gated(2 * slab)
+    own[...] = held[x]
 
 
 def project(values, stats, gain, bias, mine, theirs):
@@ -104,7 +101,7 @@
         ),
         in_specs=in_vmem(6),
         out_specs=tuple(in_vmem(2)),
-        scratch_shapes=[pltpu.VMEM((4, 2) + mine.shape[1:], BF16)],
+        scratch_shapes=[pltpu.VMEM((4, 2) + mine.shape[1:], BF16), pltpu.VMEM(values.shape, BF16)],
         compiler_params=params(),
         cost_estimate=pl.CostEstimate(
             flops=8 * steps * pairs * slab * chans,
@@ -217,7 +214,7 @@
         out_shape=jax.ShapeDtypeStruct((rows, width, outs), BF16),
         in_specs=in_vmem(5),
         out_specs=pl.BlockSpec(memory_space=pltpu.HBM),
-        scratch_shapes=[pltpu.VMEM((4, rows // 4, width, outs), BF16), pltpu.SemaphoreType.DMA((4,))],
+        scratch_shapes=[pltpu.VMEM((2, rows // 2, width, outs), BF16), pltpu.SemaphoreType.DMA((2,))],
         compiler_params=params(),
         cost_estimate=pl.CostEstimate(
             flops=2 * rows * width * chans * chans, bytes_accessed=10 * chans * rows * width, transcendentals=rows * width

time: 103 us -> 102 us (level)
  no operation moved by 1% of the time
where the time goes in v9:
time: 102 us; the launch traced here: 101 us
  blocking collectives  79.5 us (78%)
  starting transfers between devices  12.2 us (12%)
  Pallas kernels  7.22 us (7%)
    all_to_all x1, blocking collectives, shards(): lax.all_to_all(mixed, ('row', 'x'), split_axis=0, concat_axis=0, tiled=Tr...  44.8 us
    all_to_all x1, blocking collectives, shards(): lax.all_to_all(messages.reshape(half, -1, LANES), 'row', split_axis=0, co...  34.7 us
    ppermute x1, starting transfers between devices, shards(): theirs = lax.ppermute(mine, 'core', SWAP)  8.92 us
    ppermute x1, starting transfers between devices, shards(): other = lax.ppermute(got[:, :shape[1] // 2], 'core', SWAP)  3.3 us
    pallas_call x1, Pallas kernels, measure_columns(): pl.pallas_call(measure_kernel, out_shape=(jax.ShapeDtypeStruct((steps, ch...  2.42 us
  transfers between devices with their start and end apart: 2, of which 0 were waited for; matrix products, arithmetic and copies ran while one was open for 1% of the time, Pallas kernels for 3%

profile of v9, /device:TPU:1, one launch (start us, length us, event | category | flops | bytes accessed | tf_op | source)
XLA Modules:
  0.0 100.7 jit_solution(672221844837140693)
XLA Ops:
  0.0 0.8 pad_maximum_fusion.mine
  0.8 0.0 copy-start.3
  0.8 0.0 copy-start
  0.8 8.9 %collective-permute-start = (bf16[4,16,128]{2,1,0:T(8,128)(2,1)S(1)}, bf16[4,16,128]{2,1,0:T(8,128)(2,1)S(1)}, u32[]{:S(2)}, u32[]{:S(2)}) collective-permute-start(bf16[4,16,128]{2,1,0:T(8,128)(2,1)S(1)} %pad_maximum_fusion.mine), channel_id=1, source_target_pairs={{0,1},{1,0},{2,3},{3,2},{4,5},{5,4},{6,7},{7,6},{8,9},{9,8},{10,11... | collective-permute-start | bytes 49160 | tf_op jit(solution)/shard_map/ppermute | solution.py:243
  9.7 2.4 %shard_map.109 = (bf16[4,128,2048]{2,1,0:T(8,128)(2,1)S(1)}, f32[4,2,2048]{2,1,0:T(2,128)S(1)}) custom-call(bf16[16,1024,128]{2,1,0:T(8,128)(2,1)} %pair.1), custom_call_target="tpu_custom_call" | custom-call | flops 6291456 | bytes 4194304 | tf_op jit(solution)/shard_map/pallas_call | solution.py:51
  12.2 0.0 collective-permute-done.theirs
  12.2 0.0 copy-done.2
  12.2 1.8 %shard_map.110 = (bf16[32,8,16,128]{3,2,1,0:T(8,128)(2,1)S(1)}, bf16[128,2048]{1,0:T(8,128)(2,1)S(1)}) custom-call(bf16[4,128,2048]{2,1,0:T(8,128)(2,1)S(1)} %get-tuple-element.20.values, f32[4,2,2048]{2,1,0:T(2,128)S(1)} %get-tuple-element.21.stats, f32[1,128]{1,0:T(1,128)S(1)} %bitcast.35, f32[1,128]{1,0:T(1,128)S(1)} %bitcast.36, ...), custom_call_target="tpu_custom_call" | custom-call | flops 268435456 | bytes 4194304 | tf_op jit(solution)/shard_map/pallas_call | solution.py:96
  14.0 34.7 %all_to_all.10 = bf16[32,128,128]{2,1,0:T(8,128)(2,1)S(1)} all-to-all(bf16[32,128,128]{2,1,0:T(8,128)(2,1)S(1)} %bitcast.33), channel_id=1, replica_groups={{0,64,128,192,8,72,136,200,16,80,144,208,24,88,152,216,32,96,160,224,40..., dimensions={0} | all-to-all | bytes 2097152 | tf_op jit(solution)/shard_map/all_to_all | solution.py:253
  48.8 3.3 %collective-permute-start.1 = (bf16[32,4,16,128]{3,2,1,0:T(8,128)(2,1)S(1)}, bf16[32,4,16,128]{3,2,1,0:T(8,128)(2,1)S(1)}, u32[]{:S(2)}, u32[]{:S(2)}) collective-permute-start(bf16[32,4,16,128]{3,2,1,0:T(8,128)(2,1)S(1)} %slice.3), channel_id=1, source_target_pairs={{0,1},{1,0},{2,3},{3,2},{4,5},{5,4},{6,7},{7,6},{8,9},{9,8},{10,11... | collective-permute-start | bytes 1572872 | tf_op jit(solution)/shard_map/ppermute | solution.py:259
  52.1 0.1 reshape.38
  52.2 0.1 reshape.39
  52.2 0.1 copy.16
  52.3 0.1 broadcast_in_dim.16
  52.4 0.1 copy.15
  52.5 0.1 broadcast_in_dim.14
  52.7 0.3 shard_map.111.gate
  53.0 0.1 broadcast_in_dim.15.gain
  53.1 0.1 broadcast_in_dim.17.bias
  53.2 0.5 shard_map.112.begun
  53.7 0.0 collective-permute-done.1.other
  53.7 0.5 shard_map.113
  54.2 44.8 %all_to_all.11 = bf16[256,16,128]{2,1,0:T(8,128)(2,1)S(1)} all-to-all(bf16[256,16,128]{2,1,0:T(8,128)(2,1)S(1)} %bitcast.31), channel_id=1, replica_groups={{0,2,4,6,64,66,68,70,128,130,132,134,192,194,196,198,256,258,260,262,32..., dimensions={0} | all-to-all | bytes 2097152 | tf_op jit(solution)/shard_map/all_to_all | solution.py:271
  99.0 1.7 %shard_map.114 = bf16[16,128,128]{2,1,0:T(8,128)(2,1)} custom-call(bf16[8,2,16,16,128]{4,3,2,1,0:T(8,128)(2,1)S(1)} %bitcast.32, f32[128,128]{1,0:T(8,128)S(1)} %broadcast_in_dim.15.gain, f32[128,128]{1,0:T(8,128)S(1)} %broadcast_in_dim.17.bias, bf16[128,128]{1,0:T(8,128)(2,1)S(1)} %bitcast.34, f32[16,128,128]{2,1,0:T(8,128)S(1)} %shard_map.111.gate), custom_call_target="tpu_custom_call" | custom-call | flops 67108864 | bytes 2621440 | tf_op jit(solution)/shard_map/pallas_call | solution.py:212
  (11 shorter events, 0.1 us)
Async XLA Ops:
  0.0 12.2 %copy-start.2 = (f32[128]{0:T(128)S(1)}, f32[128]{0:T(128)}, u32[]{:S(2)}) copy-start(f32[128]{0:T(128)} %param.13) | copy-start | bytes 1540
  0.0 12.2 %copy-start.1 = (f32[128]{0:T(128)S(1)}, f32[128]{0:T(128)}, u32[]{:S(2)}) copy-start(f32[128]{0:T(128)} %param.12) | copy-start | bytes 1540
  0.8 51.3 %copy-start.4 = (f32[128]{0:T(128)S(1)}, f32[128]{0:T(128)}, u32[]{:S(2)}) copy-start(f32[128]{0:T(128)} %param.19) | copy-start | bytes 1540
  0.8 51.4 %copy-start.5 = (f32[128]{0:T(128)S(1)}, f32[128]{0:T(128)}, u32[]{:S(2)}) copy-start(f32[128]{0:T(128)} %param.20) | copy-start | bytes 1540
  0.8 51.9 %copy-start.3 = (bf16[128,128]{1,0:T(8,128)(2,1)S(1)}, bf16[128,128]{1,0:T(8,128)(2,1)}, u32[]{:S(2)}) copy-start(bf16[128,128]{1,0:T(8,128)(2,1)} %param.21) | copy-start | bytes 98308
  0.8 51.9 %copy-start = (bf16[128,128]{1,0:T(8,128)(2,1)S(1)}, bf16[128,128]{1,0:T(8,128)(2,1)}, u32[]{:S(2)}) copy-start(bf16[128,128]{1,0:T(8,128)(2,1)} %weights) | copy-start | bytes 98308
  0.8 11.4 %collective-permute-start = (bf16[4,16,128]{2,1,0:T(8,128)(2,1)S(1)}, bf16[4,16,128]{2,1,0:T(8,128)(2,1)S(1)}, u32[]{:S(2)}, u32[]{:S(2)}) collective-permute-start(bf16[4,16,128]{2,1,0:T(8,128)(2,1)S(1)} %pad_maximum_fusion.mine), channel_id=1, source_target_pairs={{0,1},{1,0},{2,3},{3,2},{4,5},{5,4},{6,7},{7,6},{8,9},{9,8},{10,11... | collective-permute-start | bytes 49160 | tf_op jit(solution)/shard_map/ppermute | solution.py:243
  48.8 4.9 %collective-permute-start.1 = (bf16[32,4,16,128]{3,2,1,0:T(8,128)(2,1)S(1)}, bf16[32,4,16,128]{3,2,1,0:T(8,128)(2,1)S(1)}, u32[]{:S(2)}, u32[]{:S(2)}) collective-permute-start(bf16[32,4,16,128]{3,2,1,0:T(8,128)(2,1)S(1)} %slice.3), channel_id=1, source_target_pairs={{0,1},{1,0},{2,3},{3,2},{4,5},{5,4},{6,7},{7,6},{8,9},{9,8},{10,11... | collective-permute-start | bytes 1572872 | tf_op jit(solution)/shard_map/ppermute | solution.py:259

commit v10 on v9

--- a/solution.py
+++ b/solution.py
@@ -185,9 +185,8 @@
 
 
 def finish_kernel(mixed, gain, bias, weights, gate, out, held, sems):
-    groups, _, each, rows, width = mixed.shape
-    chans = groups * each
-    values = (mixed[:, 0].astype(F32) + mixed[:, 1].astype(F32)).reshape(chans, rows, width)
+    _, chans, rows, width = mixed.shape
+    values = mixed[0].astype(F32) + mixed[1].astype(F32)
     values = values - (jnp.sum(values, axis=0) / chans)[None]
     scale = lax.rsqrt(jnp.sum(values * values, axis=0) / chans + EPS)
     scaled = jnp.swapaxes(values * scale[None], 0, 1)
@@ -207,7 +206,7 @@
 
 
 def finish(mixed, gain, bias, weights, gate):
-    groups, _, each, rows, width = mixed.shape
+    _, _, rows, width = mixed.shape
     chans, outs = weights.shape
     return pl.pallas_call(
         finish_kernel,
@@ -247,8 +246,7 @@
     per = LANES // rows
     z_count = depth // per
     halves = [
-        [z * per + y for y in range(per) for z in range(part * z_count // 2, (part + 1) * z_count // 2)]
-        for part in range(2)
+        [z * per + y for z in range(z_count) for y in range(part * per // 2, (part + 1) * per // 2)] for part in range(2)
     ]
     got = lax.all_to_all(
         messages.reshape(half, -1, LANES), "row", split_axis=0, concat_axis=0, tiled=True, axis_index_groups=halves
@@ -260,7 +258,8 @@
     gate = output_gate(normed, w_gate)
 
     def in_order(array):
-        return jnp.swapaxes(array.reshape(x_count, half, -1), 0, 1).reshape(chans, -1)
+        array = array.reshape(x_count, z_count, per // 2, -1)
+        return jnp.transpose(array, (2, 1, 0, 3)).reshape(chans, -1)
 
     gain = jnp.broadcast_to(in_order(out_gain), (chans, LANES))
     bias = jnp.broadcast_to(in_order(out_bias), (chans, LANES))
@@ -271,7 +270,7 @@
     mixed = lax.all_to_all(
         mixed, ("row", "x"), split_axis=0, concat_axis=0, tiled=True, axis_index_groups=[group]
     )
-    mixed = mixed.reshape(per, 2, z_count // 2 * x_count, rows, LANES)
+    mixed = mixed.reshape(2, chans, rows, LANES)
     return finish(mixed, gain, bias, out_weights, gate)
 
 

time: 102 us -> 99.7 us (0.977)
  blocking collectives: 79.5 us -> 76 us
  starting transfers between devices: 12.2 us -> 13.4 us
    all_to_all x1, blocking collectives: 44.8 us -> 41.7 us  [shards(): lax.all_to_all(mixed, ('row', 'x'), split_axis=0, concat_axis=0, tiled=Tr...]
    ppermute x1, starting transfers between devices: 3.3 us -> 4.5 us  [shards(): other = lax.ppermute(got[:, :shape[1] // 2], 'core', SWAP)]
where the time goes in v10:
time: 99.7 us; the launch traced here: 98.5 us
  blocking collectives  76 us (76%)
  starting transfers between devices  13.4 us (13%)
  Pallas kernels  7.22 us (7%)
    all_to_all x1, blocking collectives, shards(): lax.all_to_all(mixed, ('row', 'x'), split_axis=0, concat_axis=0, tiled=Tr...  41.7 us
    all_to_all x1, blocking collectives, shards(): lax.all_to_all(messages.reshape(half, -1, LANES), 'row', split_axis=0, co...  34.3 us
    ppermute x1, starting transfers between devices, shards(): theirs = lax.ppermute(mine, 'core', SWAP)  8.92 us
    ppermute x1, starting transfers between devices, shards(): other = lax.ppermute(got[:, :shape[1] // 2], 'core', SWAP)  4.5 us
    pallas_call x1, Pallas kernels, measure_columns(): pl.pallas_call(measure_kernel, out_shape=(jax.ShapeDtypeStruct((steps, ch...  2.42 us
  transfers between devices with their start and end apart: 2, of which 0 were waited for; matrix products, arithmetic and copies ran while one was open for 1% of the time, Pallas kernels for 3%

profile of v10, /device:TPU:1, one launch (start us, length us, event | category | flops | bytes accessed | tf_op | source)
XLA Modules:
  0.0 98.5 jit_solution(2750212211332951976)
XLA Ops:
  0.0 0.8 pad_maximum_fusion.mine
  0.8 0.0 copy-start.3
  0.8 0.0 copy-start
  0.8 8.9 %collective-permute-start = (bf16[4,16,128]{2,1,0:T(8,128)(2,1)S(1)}, bf16[4,16,128]{2,1,0:T(8,128)(2,1)S(1)}, u32[]{:S(2)}, u32[]{:S(2)}) collective-permute-start(bf16[4,16,128]{2,1,0:T(8,128)(2,1)S(1)} %pad_maximum_fusion.mine), channel_id=1, source_target_pairs={{0,1},{1,0},{2,3},{3,2},{4,5},{5,4},{6,7},{7,6},{8,9},{9,8},{10,11... | collective-permute-start | bytes 49160 | tf_op jit(solution)/shard_map/ppermute | solution.py:242
  9.7 2.4 %shard_map.109 = (bf16[4,128,2048]{2,1,0:T(8,128)(2,1)S(1)}, f32[4,2,2048]{2,1,0:T(2,128)S(1)}) custom-call(bf16[16,1024,128]{2,1,0:T(8,128)(2,1)} %pair.1), custom_call_target="tpu_custom_call" | custom-call | flops 6291456 | bytes 4194304 | tf_op jit(solution)/shard_map/pallas_call | solution.py:51
  12.2 0.0 collective-permute-done.theirs
  12.2 1.8 %shard_map.110 = (bf16[32,8,16,128]{3,2,1,0:T(8,128)(2,1)S(1)}, bf16[128,2048]{1,0:T(8,128)(2,1)S(1)}) custom-call(bf16[4,128,2048]{2,1,0:T(8,128)(2,1)S(1)} %get-tuple-element.20.values, f32[4,2,2048]{2,1,0:T(2,128)S(1)} %get-tuple-element.21.stats, f32[1,128]{1,0:T(1,128)S(1)} %bitcast.39, f32[1,128]{1,0:T(1,128)S(1)} %bitcast.40, ...), custom_call_target="tpu_custom_call" | custom-call | flops 268435456 | bytes 4194304 | tf_op jit(solution)/shard_map/pallas_call | solution.py:96
  14.0 34.3 %all_to_all.10 = bf16[32,128,128]{2,1,0:T(8,128)(2,1)S(1)} all-to-all(bf16[32,128,128]{2,1,0:T(8,128)(2,1)S(1)} %bitcast.37), channel_id=1, replica_groups={{0,8,16,24,64,72,80,88,128,136,144,152,192,200,208,216,256,264,272,280,..., dimensions={0} | all-to-all | bytes 2097152 | tf_op jit(solution)/shard_map/all_to_all | solution.py:251
  48.4 4.5 %collective-permute-start.1 = (bf16[32,4,16,128]{3,2,1,0:T(8,128)(2,1)S(1)}, bf16[32,4,16,128]{3,2,1,0:T(8,128)(2,1)S(1)}, u32[]{:S(2)}, u32[]{:S(2)}) collective-permute-start(bf16[32,4,16,128]{3,2,1,0:T(8,128)(2,1)S(1)} %slice.3), channel_id=1, source_target_pairs={{0,1},{1,0},{2,3},{3,2},{4,5},{5,4},{6,7},{7,6},{8,9},{9,8},{10,11... | collective-permute-start | bytes 1572872 | tf_op jit(solution)/shard_map/ppermute | solution.py:257
  52.9 0.1 reshape.38
  53.0 0.1 copy.15
  53.2 0.1 broadcast_in_dim.14
  53.3 0.0 copy-done.5
  53.3 0.1 reshape.39
  53.4 0.1 copy.16
  53.5 0.1 broadcast_in_dim.16
  53.7 0.3 shard_map.111.gate
  54.1 0.1 broadcast_in_dim.17.bias
  54.1 0.1 broadcast_in_dim.15.gain
  54.2 0.5 shard_map.112.begun
  54.7 0.0 collective-permute-done.1.other
  54.7 0.5 shard_map.113
  55.2 41.7 %all_to_all.11 = bf16[256,16,128]{2,1,0:T(8,128)(2,1)S(1)} all-to-all(bf16[256,16,128]{2,1,0:T(8,128)(2,1)S(1)} %bitcast.35), channel_id=1, replica_groups={{0,2,4,6,64,66,68,70,128,130,132,134,192,194,196,198,256,258,260,262,32..., dimensions={0} | all-to-all | bytes 2097152 | tf_op jit(solution)/shard_map/all_to_all | solution.py:270
  96.9 1.7 %shard_map.114 = bf16[16,128,128]{2,1,0:T(8,128)(2,1)} custom-call(bf16[2,128,16,128]{3,2,1,0:T(8,128)(2,1)S(1)} %bitcast.36, f32[128,128]{1,0:T(8,128)S(1)} %broadcast_in_dim.15.gain, f32[128,128]{1,0:T(8,128)S(1)} %broadcast_in_dim.17.bias, bf16[128,128]{1,0:T(8,128)(2,1)S(1)} %bitcast.38, f32[16,128,128]{2,1,0:T(8,128)S(1)} %shard_map.111.gate), custom_call_target="tpu_custom_call" | custom-call | flops 67108864 | bytes 2621440 | tf_op jit(solution)/shard_map/pallas_call | solution.py:211
  (11 shorter events, 0.1 us)
Async XLA Ops:
  0.0 12.2 %copy-start.2 = (f32[128]{0:T(128)S(1)}, f32[128]{0:T(128)}, u32[]{:S(2)}) copy-start(f32[128]{0:T(128)} %param.13) | copy-start | bytes 1540
  0.0 12.2 %copy-start.1 = (f32[128]{0:T(128)S(1)}, f32[128]{0:T(128)}, u32[]{:S(2)}) copy-start(f32[128]{0:T(128)} %param.12) | copy-start | bytes 1540
  0.8 52.2 %copy-start.4 = (f32[128]{0:T(128)S(1)}, f32[128]{0:T(128)}, u32[]{:S(2)}) copy-start(f32[128]{0:T(128)} %param.19) | copy-start | bytes 1540
  0.8 52.5 %copy-start.5 = (f32[128]{0:T(128)S(1)}, f32[128]{0:T(128)}, u32[]{:S(2)}) copy-start(f32[128]{0:T(128)} %param.20) | copy-start | bytes 1540
  0.8 52.9 %copy-start.3 = (bf16[128,128]{1,0:T(8,128)(2,1)S(1)}, bf16[128,128]{1,0:T(8,128)(2,1)}, u32[]{:S(2)}) copy-start(bf16[128,128]{1,0:T(8,128)(2,1)} %param.21) | copy-start | bytes 98308
  0.8 52.9 %copy-start = (bf16[128,128]{1,0:T(8,128)(2,1)S(1)}, bf16[128,128]{1,0:T(8,128)(2,1)}, u32[]{:S(2)}) copy-start(bf16[128,128]{1,0:T(8,128)(2,1)} %weights) | copy-start | bytes 98308
  0.8 11.4 %collective-permute-start = (bf16[4,16,128]{2,1,0:T(8,128)(2,1)S(1)}, bf16[4,16,128]{2,1,0:T(8,128)(2,1)S(1)}, u32[]{:S(2)}, u32[]{:S(2)}) collective-permute-start(bf16[4,16,128]{2,1,0:T(8,128)(2,1)S(1)} %pad_maximum_fusion.mine), channel_id=1, source_target_pairs={{0,1},{1,0},{2,3},{3,2},{4,5},{5,4},{6,7},{7,6},{8,9},{9,8},{10,11... | collective-permute-start | bytes 49160 | tf_op jit(solution)/shard_map/ppermute | solution.py:242
  48.4 6.3 %collective-permute-start.1 = (bf16[32,4,16,128]{3,2,1,0:T(8,128)(2,1)S(1)}, bf16[32,4,16,128]{3,2,1,0:T(8,128)(2,1)S(1)}, u32[]{:S(2)}, u32[]{:S(2)}) collective-permute-start(bf16[32,4,16,128]{3,2,1,0:T(8,128)(2,1)S(1)} %slice.3), channel_id=1, source_target_pairs={{0,1},{1,0},{2,3},{3,2},{4,5},{5,4},{6,7},{7,6},{8,9},{9,8},{10,11... | collective-permute-start | bytes 1572872 | tf_op jit(solution)/shard_map/ppermute | solution.py:257

commit v11 on v10

--- a/solution.py
+++ b/solution.py
@@ -131,7 +131,11 @@
     )(normed, weights)
 
 
-def mix_rows(got, left, first, out):
+def mirrored(at, size, flip):
+    return at + flip * (size - 1 - 2 * at)
+
+
+def mix_rows(got, left, store):
     sources, parts, rows, _ = got.shape
     blocks = parts // 2
 
@@ -144,31 +148,42 @@
     mixed = mixed.astype(BF16)
     for side in range(blocks):
         for at in range(blocks):
-            piece = mixed[side * LANES : (side + 1) * LANES, at * LANES : (at + 1) * LANES]
-            out[:, 2 * side + first, at] = piece.reshape(LANES // rows, rows, LANES)
+            for y in range(LANES // rows):
+                row = side * LANES + y * rows
+                store(side, at, y, mixed[row : row + rows, at * LANES : (at + 1) * LANES])
 
 
 def mix_own_kernel(got, out):
-    mix_rows(got, got, 0, out)
+    def store(side, at, y, piece):
+        out[y, side, at] = piece
+
+    mix_rows(got, got, store)
 
 
 def mix_other_kernel(got, other, begun, out):
     core = lax.axis_index("core")
-    for side in range(got.shape[1] // 2):
-        out[:, 2 * side + core] = begun[:, 2 * side]
-    mix_rows(got, other, 1 - core, out)
+    per, z_count, x_count = out.shape[:3]
+
+    def store_at(z, x, y, piece):
+        out[mirrored(y, per, core), mirrored(z, z_count, core), mirrored(x, x_count, core)] = piece
+
+    for y in range(per):
+        for side in range(begun.shape[1]):
+            for at in range(x_count):
+                store_at(2 * side + core, at, y, begun[y, side, at])
+    mix_rows(got, other, lambda side, at, y, piece: store_at(2 * side + 1 - core, at, y, piece))
 
 
 def mix(got, other):
     sources, parts, rows, _ = got.shape
     depth, width = sources * rows, parts // 2 * LANES
-    shape = jax.ShapeDtypeStruct((LANES // rows, parts, parts // 2, rows, LANES), BF16)
+    per, blocks = LANES // rows, parts // 2
     cost = pl.CostEstimate(
         flops=2 * depth * width * width, bytes_accessed=2 * (2 * depth * width + width * width), transcendentals=0
     )
     begun = pl.pallas_call(
         mix_own_kernel,
-        out_shape=shape,
+        out_shape=jax.ShapeDtypeStruct((per, blocks, blocks, rows, LANES), BF16),
         in_specs=in_vmem(1),
         out_specs=in_vmem(1)[0],
         compiler_params=params(),
@@ -176,7 +191,7 @@
     )(got)
     return pl.pallas_call(
         mix_other_kernel,
-        out_shape=shape,
+        out_shape=jax.ShapeDtypeStruct((per, parts, blocks, rows, LANES), BF16),
         in_specs=in_vmem(3),
         out_specs=in_vmem(1)[0],
         compiler_params=params(),
@@ -185,8 +200,10 @@
 
 
 def finish_kernel(mixed, gain, bias, weights, gate, out, held, sems):
+    core = lax.axis_index("core")
     _, chans, rows, width = mixed.shape
-    values = mixed[0].astype(F32) + mixed[1].astype(F32)
+    places = [mirrored(at, chans, core) for at in range(chans)]
+    values = jnp.stack([mixed[0, at].astype(F32) + mixed[1, at].astype(F32) for at in places], axis=0)
     values = values - (jnp.sum(values, axis=0) / chans)[None]
     scale = lax.rsqrt(jnp.sum(values * values, axis=0) / chans + EPS)
     scaled = jnp.swapaxes(values * scale[None], 0, 1)
@@ -267,8 +284,9 @@
 
     mixed = mix(got, other).reshape(depth * x_count, rows, LANES)
     group = [x_count * (z * per + y) + x for y in range(per) for z in range(z_count) for x in range(x_count)]
+    groups = [[2 * at for at in group], [2 * at + 1 for at in group[::-1]]]
     mixed = lax.all_to_all(
-        mixed, ("row", "x"), split_axis=0, concat_axis=0, tiled=True, axis_index_groups=[group]
+        mixed, ("row", "x", "core"), split_axis=0, concat_axis=0, tiled=True, axis_index_groups=groups
     )
     mixed = mixed.reshape(2, chans, rows, LANES)
     return finish(mixed, gain, bias, out_weights, gate)

time: 99.7 us -> 98.6 us (0.989)
  no operation moved by 1% of the time
where the time goes in v11:
time: 98.6 us; the launch traced here: 98.1 us
  blocking collectives  75.4 us (76%)
  starting transfers between devices  13.4 us (14%)
  Pallas kernels  7.39 us (7%)
    all_to_all x1, blocking collectives, shards(): lax.all_to_all(mixed, ('row', 'x', 'core'), split_axis=0, concat_axis=0,...  41.1 us
    all_to_all x1, blocking collectives, shards(): lax.all_to_all(messages.reshape(half, -1, LANES), 'row', split_axis=0, co...  34.3 us
    ppermute x1, starting transfers between devices, shards(): theirs = lax.ppermute(mine, 'core', SWAP)  8.92 us
    ppermute x1, starting transfers between devices, shards(): other = lax.ppermute(got[:, :shape[1] // 2], 'core', SWAP)  4.5 us
    pallas_call x1, Pallas kernels, measure_columns(): pl.pallas_call(measure_kernel, out_shape=(jax.ShapeDtypeStruct((steps, ch...  2.42 us
  transfers between devices with their start and end apart: 2, of which 0 were waited for; matrix products, arithmetic and copies ran while one was open for 1% of the time, Pallas kernels for 3%

profile of v11, /device:TPU:1, one launch (start us, length us, event | category | flops | bytes accessed | tf_op | source)
XLA Modules:
  0.0 98.1 jit_solution(8365032934623984999)
XLA Ops:
  0.0 0.8 pad_maximum_fusion.mine
  0.8 0.0 copy-start.3
  0.8 0.0 copy-start
  0.8 8.9 %collective-permute-start = (bf16[4,16,128]{2,1,0:T(8,128)(2,1)S(1)}, bf16[4,16,128]{2,1,0:T(8,128)(2,1)S(1)}, u32[]{:S(2)}, u32[]{:S(2)}) collective-permute-start(bf16[4,16,128]{2,1,0:T(8,128)(2,1)S(1)} %pad_maximum_fusion.mine), channel_id=1, source_target_pairs={{0,1},{1,0},{2,3},{3,2},{4,5},{5,4},{6,7},{7,6},{8,9},{9,8},{10,11... | collective-permute-start | bytes 49160 | tf_op jit(solution)/shard_map/ppermute | solution.py:259
  9.7 2.4 %shard_map.109 = (bf16[4,128,2048]{2,1,0:T(8,128)(2,1)S(1)}, f32[4,2,2048]{2,1,0:T(2,128)S(1)}) custom-call(bf16[16,1024,128]{2,1,0:T(8,128)(2,1)} %pair.1), custom_call_target="tpu_custom_call" | custom-call | flops 6291456 | bytes 4194304 | tf_op jit(solution)/shard_map/pallas_call | solution.py:51
  12.2 0.0 collective-permute-done.theirs
  12.2 1.8 %shard_map.110 = (bf16[32,8,16,128]{3,2,1,0:T(8,128)(2,1)S(1)}, bf16[128,2048]{1,0:T(8,128)(2,1)S(1)}) custom-call(bf16[4,128,2048]{2,1,0:T(8,128)(2,1)S(1)} %get-tuple-element.20.values, f32[4,2,2048]{2,1,0:T(2,128)S(1)} %get-tuple-element.21.stats, f32[1,128]{1,0:T(1,128)S(1)} %bitcast.39, f32[1,128]{1,0:T(1,128)S(1)} %bitcast.40, ...), custom_call_target="tpu_custom_call" | custom-call | flops 268435456 | bytes 4194304 | tf_op jit(solution)/shard_map/pallas_call | solution.py:96
  14.0 34.3 %all_to_all.10 = bf16[32,128,128]{2,1,0:T(8,128)(2,1)S(1)} all-to-all(bf16[32,128,128]{2,1,0:T(8,128)(2,1)S(1)} %bitcast.37), channel_id=1, replica_groups={{0,8,16,24,64,72,80,88,128,136,144,152,192,200,208,216,256,264,272,280,..., dimensions={0} | all-to-all | bytes 2097152 | tf_op jit(solution)/shard_map/all_to_all | solution.py:268
  48.4 4.5 %collective-permute-start.1 = (bf16[32,4,16,128]{3,2,1,0:T(8,128)(2,1)S(1)}, bf16[32,4,16,128]{3,2,1,0:T(8,128)(2,1)S(1)}, u32[]{:S(2)}, u32[]{:S(2)}) collective-permute-start(bf16[32,4,16,128]{3,2,1,0:T(8,128)(2,1)S(1)} %slice.3), channel_id=1, source_target_pairs={{0,1},{1,0},{2,3},{3,2},{4,5},{5,4},{6,7},{7,6},{8,9},{9,8},{10,11... | collective-permute-start | bytes 1572872 | tf_op jit(solution)/shard_map/ppermute | solution.py:274
  52.9 0.1 reshape.38
  53.0 0.1 copy.15
  53.2 0.1 broadcast_in_dim.14
  53.3 0.0 copy-done.5
  53.3 0.1 reshape.39
  53.4 0.1 copy.16
  53.5 0.1 broadcast_in_dim.16
  53.7 0.3 shard_map.111.gate
  54.1 0.1 broadcast_in_dim.17.bias
  54.1 0.1 broadcast_in_dim.15.gain
  54.2 0.5 shard_map.112.begun
  54.7 0.0 collective-permute-done.1.other
  54.7 0.5 shard_map.113
  55.3 41.1 %all_to_all.11 = bf16[256,16,128]{2,1,0:T(8,128)(2,1)S(1)} all-to-all(bf16[256,16,128]{2,1,0:T(8,128)(2,1)S(1)} %bitcast.35), channel_id=1, replica_groups={{0,2,4,6,64,66,68,70,128,130,132,134,192,194,196,198,256,258,260,262,32..., dimensions={0} | all-to-all | bytes 2097152 | tf_op jit(solution)/shard_map/all_to_all | solution.py:288
  96.3 1.8 %shard_map.114 = bf16[16,128,128]{2,1,0:T(8,128)(2,1)} custom-call(bf16[2,128,16,128]{3,2,1,0:T(8,128)(2,1)S(1)} %bitcast.36, f32[128,128]{1,0:T(8,128)S(1)} %broadcast_in_dim.15.gain, f32[128,128]{1,0:T(8,128)S(1)} %broadcast_in_dim.17.bias, bf16[128,128]{1,0:T(8,128)(2,1)S(1)} %bitcast.38, f32[16,128,128]{2,1,0:T(8,128)S(1)} %shard_map.111.gate), custom_call_target="tpu_custom_call" | custom-call | flops 67108864 | bytes 2621440 | tf_op jit(solution)/shard_map/pallas_call | solution.py:228
  (11 shorter events, 0.1 us)
Async XLA Ops:
  0.0 12.2 %copy-start.2 = (f32[128]{0:T(128)S(1)}, f32[128]{0:T(128)}, u32[]{:S(2)}) copy-start(f32[128]{0:T(128)} %param.13) | copy-start | bytes 1540
  0.0 12.2 %copy-start.1 = (f32[128]{0:T(128)S(1)}, f32[128]{0:T(128)}, u32[]{:S(2)}) copy-start(f32[128]{0:T(128)} %param.12) | copy-start | bytes 1540
  0.8 52.2 %copy-start.4 = (f32[128]{0:T(128)S(1)}, f32[128]{0:T(128)}, u32[]{:S(2)}) copy-start(f32[128]{0:T(128)} %param.19) | copy-start | bytes 1540
  0.8 52.5 %copy-start.5 = (f32[128]{0:T(128)S(1)}, f32[128]{0:T(128)}, u32[]{:S(2)}) copy-start(f32[128]{0:T(128)} %param.20) | copy-start | bytes 1540
  0.8 52.9 %copy-start.3 = (bf16[128,128]{1,0:T(8,128)(2,1)S(1)}, bf16[128,128]{1,0:T(8,128)(2,1)}, u32[]{:S(2)}) copy-start(bf16[128,128]{1,0:T(8,128)(2,1)} %param.21) | copy-start | bytes 98308
  0.8 52.9 %copy-start = (bf16[128,128]{1,0:T(8,128)(2,1)S(1)}, bf16[128,128]{1,0:T(8,128)(2,1)}, u32[]{:S(2)}) copy-start(bf16[128,128]{1,0:T(8,128)(2,1)} %weights) | copy-start | bytes 98308
  0.8 11.4 %collective-permute-start = (bf16[4,16,128]{2,1,0:T(8,128)(2,1)S(1)}, bf16[4,16,128]{2,1,0:T(8,128)(2,1)S(1)}, u32[]{:S(2)}, u32[]{:S(2)}) collective-permute-start(bf16[4,16,128]{2,1,0:T(8,128)(2,1)S(1)} %pad_maximum_fusion.mine), channel_id=1, source_target_pairs={{0,1},{1,0},{2,3},{3,2},{4,5},{5,4},{6,7},{7,6},{8,9},{9,8},{10,11... | collective-permute-start | bytes 49160 | tf_op jit(solution)/shard_map/ppermute | solution.py:259
  48.4 6.3 %collective-permute-start.1 = (bf16[32,4,16,128]{3,2,1,0:T(8,128)(2,1)S(1)}, bf16[32,4,16,128]{3,2,1,0:T(8,128)(2,1)S(1)}, u32[]{:S(2)}, u32[]{:S(2)}) collective-permute-start(bf16[32,4,16,128]{3,2,1,0:T(8,128)(2,1)S(1)} %slice.3), channel_id=1, source_target_pairs={{0,1},{1,0},{2,3},{3,2},{4,5},{5,4},{6,7},{7,6},{8,9},{9,8},{10,11... | collective-permute-start | bytes 1572872 | tf_op jit(solution)/shard_map/ppermute | solution.py:274

commit v12 on v11

--- a/solution.py
+++ b/solution.py
@@ -22,6 +22,10 @@
 
 def in_vmem(count):
     return [pl.BlockSpec(memory_space=pltpu.VMEM)] * count
+
+
+def mirrored(at, size, flip):
+    return at + flip * (size - 1 - 2 * at)
 
 
 def measure_kernel(pair, values, stats, held, sems):
@@ -85,8 +89,11 @@
             parts = [value[:, at : at + LANES] for at in range(0, pairs, LANES)]
             return jnp.swapaxes(jnp.stack(parts, axis=0), 0, 1).astype(BF16)
 
-        out[:, step] = gated(0)
-        out[:, steps + step] = gated(2 * slab)
+        left, right = gated(0), gated(2 * slab)
+        for at in range(slab):
+            place = mirrored(at, slab, core)
+            out[place, step] = left[at]
+            out[place, steps + step] = right[at]
     own[...] = held[x]
 
 
@@ -131,20 +138,22 @@
     )(normed, weights)
 
 
-def mirrored(at, size, flip):
-    return at + flip * (size - 1 - 2 * at)
-
-
-def mix_rows(got, left, store):
+def mix_rows(got, left, backwards, store):
     sources, parts, rows, _ = got.shape
     blocks = parts // 2
 
-    def joined(ref, start):
+    def joined(ref, start, order):
         return jnp.concatenate(
-            [ref[:, start + at].reshape(sources * rows, LANES) for at in range(blocks)], axis=1
+            [jnp.concatenate([ref[source, start + at] for source in order], axis=0) for at in range(blocks)], axis=1
         )
 
-    mixed = lax.dot_general(joined(left, 0), joined(got, blocks), OVER_FIRST, preferred_element_type=F32)
+    order = range(sources)
+    mixed = lax.dot_general(
+        joined(left, 0, order[::-1] if backwards else order),
+        joined(got, blocks, order),
+        OVER_FIRST,
+        preferred_element_type=F32,
+    )
     mixed = mixed.astype(BF16)
     for side in range(blocks):
         for at in range(blocks):
@@ -157,7 +166,7 @@
     def store(side, at, y, piece):
         out[y, side, at] = piece
 
-    mix_rows(got, got, store)
+    mix_rows(got, got, False, store)
 
 
 def mix_other_kernel(got, other, begun, out):
@@ -171,7 +180,7 @@
         for side in range(begun.shape[1]):
             for at in range(x_count):
                 store_at(2 * side + core, at, y, begun[y, side, at])
-    mix_rows(got, other, lambda side, at, y, piece: store_at(2 * side + 1 - core, at, y, piece))
+    mix_rows(got, other, True, lambda side, at, y, piece: store_at(2 * side + 1 - core, at, y, piece))
 
 
 def mix(got, other):
@@ -265,8 +274,14 @@
     halves = [
         [z * per + y for z in range(z_count) for y in range(part * per // 2, (part + 1) * per // 2)] for part in range(2)
     ]
+    groups = [[2 * at for at in part] for part in halves] + [[2 * at + 1 for at in part[::-1]] for part in halves]
     got = lax.all_to_all(
-        messages.reshape(half, -1, LANES), "row", split_axis=0, concat_axis=0, tiled=True, axis_index_groups=halves
+        messages.reshape(half, -1, LANES),
+        ("row", "core"),
+        split_axis=0,
+        concat_axis=0,
+        tiled=True,
+        axis_index_groups=groups,
     ).reshape(shape)
     got, normed, w_gate, out_gain, out_bias, w_out = lax.optimization_barrier(
         (got, normed, w_gate, out_gain, out_bias, w_out)

time: 98.6 us -> 97.8 us (level)
    all_to_all x1, blocking collectives: 34.3 us -> 32.9 us  [shards(): lax.all_to_all(messages.reshape(half, -1, LANES), ('row', 'core'), split_...]
    all_to_all x1, blocking collectives: 41.1 us -> 42.2 us  [shards(): lax.all_to_all(mixed, ('row', 'x', 'core'), split_axis=0, concat_axis=0,...]
where the time goes in v12:
time: 97.8 us; the launch traced here: 97.4 us
  blocking collectives  75.1 us (77%)
  starting transfers between devices  13 us (13%)
  Pallas kernels  7.4 us (8%)
    all_to_all x1, blocking collectives, shards(): lax.all_to_all(mixed, ('row', 'x', 'core'), split_axis=0, concat_axis=0,...  42.2 us
    all_to_all x1, blocking collectives, shards(): lax.all_to_all(messages.reshape(half, -1, LANES), ('row', 'core'), split_...  32.9 us
    ppermute x1, starting transfers between devices, shards(): theirs = lax.ppermute(mine, 'core', SWAP)  8.92 us
    ppermute x1, starting transfers between devices, shards(): other = lax.ppermute(got[:, :shape[1] // 2], 'core', SWAP)  4.13 us
    pallas_call x1, Pallas kernels, measure_columns(): pl.pallas_call(measure_kernel, out_shape=(jax.ShapeDtypeStruct((steps, ch...  2.42 us
  transfers between devices with their start and end apart: 2, of which 0 were waited for; matrix products, arithmetic and copies ran while one was open for 1% of the time, Pallas kernels for 3%

profile of v12, /device:TPU:1, one launch (start us, length us, event | category | flops | bytes accessed | tf_op | source)
XLA Modules:
  0.0 97.4 jit_solution(15600042226465211567)
XLA Ops:
  0.0 0.8 pad_maximum_fusion.mine
  0.8 0.0 copy-start.3
  0.8 0.0 copy-start
  0.8 8.9 %collective-permute-start = (bf16[4,16,128]{2,1,0:T(8,128)(2,1)S(1)}, bf16[4,16,128]{2,1,0:T(8,128)(2,1)S(1)}, u32[]{:S(2)}, u32[]{:S(2)}) collective-permute-start(bf16[4,16,128]{2,1,0:T(8,128)(2,1)S(1)} %pad_maximum_fusion.mine), channel_id=1, source_target_pairs={{0,1},{1,0},{2,3},{3,2},{4,5},{5,4},{6,7},{7,6},{8,9},{9,8},{10,11... | collective-permute-start | bytes 49160 | tf_op jit(solution)/shard_map/ppermute | solution.py:268
  9.7 2.4 %shard_map.109 = (bf16[4,128,2048]{2,1,0:T(8,128)(2,1)S(1)}, f32[4,2,2048]{2,1,0:T(2,128)S(1)}) custom-call(bf16[16,1024,128]{2,1,0:T(8,128)(2,1)} %pair.1), custom_call_target="tpu_custom_call" | custom-call | flops 6291456 | bytes 4194304 | tf_op jit(solution)/shard_map/pallas_call | solution.py:55
  12.2 0.0 collective-permute-done.theirs
  12.2 1.9 %shard_map.110 = (bf16[32,8,16,128]{3,2,1,0:T(8,128)(2,1)S(1)}, bf16[128,2048]{1,0:T(8,128)(2,1)S(1)}) custom-call(bf16[4,128,2048]{2,1,0:T(8,128)(2,1)S(1)} %get-tuple-element.20.values, f32[4,2,2048]{2,1,0:T(2,128)S(1)} %get-tuple-element.21.stats, f32[1,128]{1,0:T(1,128)S(1)} %bitcast.39, f32[1,128]{1,0:T(1,128)S(1)} %bitcast.40, ...), custom_call_target="tpu_custom_call" | custom-call | flops 268435456 | bytes 4194304 | tf_op jit(solution)/shard_map/pallas_call | solution.py:103
  14.1 32.9 %all_to_all.10 = bf16[32,128,128]{2,1,0:T(8,128)(2,1)S(1)} all-to-all(bf16[32,128,128]{2,1,0:T(8,128)(2,1)S(1)} %bitcast.37), channel_id=1, replica_groups={{0,8,16,24,64,72,80,88,128,136,144,152,192,200,208,216,256,264,272,280,..., dimensions={0} | all-to-all | bytes 2097152 | tf_op jit(solution)/shard_map/all_to_all | solution.py:278
  47.0 4.1 %collective-permute-start.1 = (bf16[32,4,16,128]{3,2,1,0:T(8,128)(2,1)S(1)}, bf16[32,4,16,128]{3,2,1,0:T(8,128)(2,1)S(1)}, u32[]{:S(2)}, u32[]{:S(2)}) collective-permute-start(bf16[32,4,16,128]{3,2,1,0:T(8,128)(2,1)S(1)} %slice.3), channel_id=1, source_target_pairs={{0,1},{1,0},{2,3},{3,2},{4,5},{5,4},{6,7},{7,6},{8,9},{9,8},{10,11... | collective-permute-start | bytes 1572872 | tf_op jit(solution)/shard_map/ppermute | solution.py:289
  51.2 0.1 reshape.38
  51.3 0.1 copy.15
  51.4 0.1 broadcast_in_dim.14
  51.5 0.0 copy-done.5
  51.5 0.1 reshape.39
  51.6 0.1 copy.16
  51.8 0.1 broadcast_in_dim.16
  51.9 0.3 shard_map.111.gate
  52.3 0.1 broadcast_in_dim.17.bias
  52.3 0.1 broadcast_in_dim.15.gain
  52.4 0.5 shard_map.112.begun
  52.9 0.0 collective-permute-done.1.other
  52.9 0.5 shard_map.113
  53.5 42.2 %all_to_all.11 = bf16[256,16,128]{2,1,0:T(8,128)(2,1)S(1)} all-to-all(bf16[256,16,128]{2,1,0:T(8,128)(2,1)S(1)} %bitcast.35), channel_id=1, replica_groups={{0,2,4,6,64,66,68,70,128,130,132,134,192,194,196,198,256,258,260,262,32..., dimensions={0} | all-to-all | bytes 2097152 | tf_op jit(solution)/shard_map/all_to_all | solution.py:303
  95.7 1.8 %shard_map.114 = bf16[16,128,128]{2,1,0:T(8,128)(2,1)} custom-call(bf16[2,128,16,128]{3,2,1,0:T(8,128)(2,1)S(1)} %bitcast.36, f32[128,128]{1,0:T(8,128)S(1)} %broadcast_in_dim.15.gain, f32[128,128]{1,0:T(8,128)S(1)} %broadcast_in_dim.17.bias, bf16[128,128]{1,0:T(8,128)(2,1)S(1)} %bitcast.38, f32[16,128,128]{2,1,0:T(8,128)S(1)} %shard_map.111.gate), custom_call_target="tpu_custom_call" | custom-call | flops 67108864 | bytes 2621440 | tf_op jit(solution)/shard_map/pallas_call | solution.py:237
  (11 shorter events, 0.1 us)
Async XLA Ops:
  0.0 12.2 %copy-start.2 = (f32[128]{0:T(128)S(1)}, f32[128]{0:T(128)}, u32[]{:S(2)}) copy-start(f32[128]{0:T(128)} %param.13) | copy-start | bytes 1540
  0.0 12.2 %copy-start.1 = (f32[128]{0:T(128)S(1)}, f32[128]{0:T(128)}, u32[]{:S(2)}) copy-start(f32[128]{0:T(128)} %param.12) | copy-start | bytes 1540
  0.8 50.4 %copy-start.4 = (f32[128]{0:T(128)S(1)}, f32[128]{0:T(128)}, u32[]{:S(2)}) copy-start(f32[128]{0:T(128)} %param.19) | copy-start | bytes 1540
  0.8 50.7 %copy-start.5 = (f32[128]{0:T(128)S(1)}, f32[128]{0:T(128)}, u32[]{:S(2)}) copy-start(f32[128]{0:T(128)} %param.20) | copy-start | bytes 1540
  0.8 51.1 %copy-start.3 = (bf16[128,128]{1,0:T(8,128)(2,1)S(1)}, bf16[128,128]{1,0:T(8,128)(2,1)}, u32[]{:S(2)}) copy-start(bf16[128,128]{1,0:T(8,128)(2,1)} %param.21) | copy-start | bytes 98308
  0.8 51.1 %copy-start = (bf16[128,128]{1,0:T(8,128)(2,1)S(1)}, bf16[128,128]{1,0:T(8,128)(2,1)}, u32[]{:S(2)}) copy-start(bf16[128,128]{1,0:T(8,128)(2,1)} %weights) | copy-start | bytes 98308
  0.8 11.4 %collective-permute-start = (bf16[4,16,128]{2,1,0:T(8,128)(2,1)S(1)}, bf16[4,16,128]{2,1,0:T(8,128)(2,1)S(1)}, u32[]{:S(2)}, u32[]{:S(2)}) collective-permute-start(bf16[4,16,128]{2,1,0:T(8,128)(2,1)S(1)} %pad_maximum_fusion.mine), channel_id=1, source_target_pairs={{0,1},{1,0},{2,3},{3,2},{4,5},{5,4},{6,7},{7,6},{8,9},{9,8},{10,11... | collective-permute-start | bytes 49160 | tf_op jit(solution)/shard_map/ppermute | solution.py:268
  47.0 5.9 %collective-permute-start.1 = (bf16[32,4,16,128]{3,2,1,0:T(8,128)(2,1)S(1)}, bf16[32,4,16,128]{3,2,1,0:T(8,128)(2,1)S(1)}, u32[]{:S(2)}, u32[]{:S(2)}) collective-permute-start(bf16[32,4,16,128]{3,2,1,0:T(8,128)(2,1)S(1)} %slice.3), channel_id=1, source_target_pairs={{0,1},{1,0},{2,3},{3,2},{4,5},{5,4},{6,7},{7,6},{8,9},{9,8},{10,11... | collective-permute-start | bytes 1572872 | tf_op jit(solution)/shard_map/ppermute | solution.py:289

commit v13 on v12

--- a/solution.py
+++ b/solution.py
@@ -272,7 +272,7 @@
     per = LANES // rows
     z_count = depth // per
     halves = [
-        [z * per + y for z in range(z_count) for y in range(part * per // 2, (part + 1) * per // 2)] for part in range(2)
+        [z * per + y for y in range(part * per // 2, (part + 1) * per // 2) for z in range(z_count)] for part in range(2)
     ]
     groups = [[2 * at for at in part] for part in halves] + [[2 * at + 1 for at in part[::-1]] for part in halves]
     got = lax.all_to_all(
@@ -290,8 +290,8 @@
     gate = output_gate(normed, w_gate)
 
     def in_order(array):
-        array = array.reshape(x_count, z_count, per // 2, -1)
-        return jnp.transpose(array, (2, 1, 0, 3)).reshape(chans, -1)
+        array = array.reshape(x_count, half, -1)
+        return jnp.swapaxes(array, 0, 1).reshape(chans, -1)
 
     gain = jnp.broadcast_to(in_order(out_gain), (chans, LANES))
     bias = jnp.broadcast_to(in_order(out_bias), (chans, LANES))

time: 97.8 us -> 97.1 us (level)
  starting transfers between devices: 13 us -> 10.8 us
  blocking collectives: 75.1 us -> 76.6 us
    all_to_all x1, blocking collectives: 32.9 us -> 36 us  [shards(): lax.all_to_all(messages.reshape(half, -1, LANES), ('row', 'core'), split_...]
    ppermute x1, starting transfers between devices: 4.13 us -> 1.92 us  [shards(): other = lax.ppermute(got[:, :shape[1] // 2], 'core', SWAP)]
    all_to_all x1, blocking collectives: 42.2 us -> 40.6 us  [shards(): lax.all_to_all(mixed, ('row', 'x', 'core'), split_axis=0, concat_axis=0,...]
  transfers between devices with their start and end apart: 2 -> 2, of which waited for: 0 -> 1; matrix products, arithmetic and copies ran while one was open for 1% -> 1% of each run, Pallas kernels for 3% -> 3%
where the time goes in v13:
time: 97.1 us; the launch traced here: 96.8 us
  blocking collectives  76.6 us (79%)
  starting transfers between devices  10.8 us (11%)
  Pallas kernels  7.4 us (8%)
    all_to_all x1, blocking collectives, shards(): lax.all_to_all(mixed, ('row', 'x', 'core'), split_axis=0, concat_axis=0,...  40.6 us
    all_to_all x1, blocking collectives, shards(): lax.all_to_all(messages.reshape(half, -1, LANES), ('row', 'core'), split_...  36 us
    ppermute x1, starting transfers between devices, shards(): theirs = lax.ppermute(mine, 'core', SWAP)  8.92 us
    pallas_call x1, Pallas kernels, measure_columns(): pl.pallas_call(measure_kernel, out_shape=(jax.ShapeDtypeStruct((steps, ch...  2.42 us
  transfers between devices with their start and end apart: 2, of which 1 were waited for; matrix products, arithmetic and copies ran while one was open for 1% of the time, Pallas kernels for 3%

profile of v13, /device:TPU:1, one launch (start us, length us, event | category | flops | bytes accessed | tf_op | source)
XLA Modules:
  0.0 96.8 jit_solution(7445173380644558585)
XLA Ops:
  0.0 0.8 pad_maximum_fusion.mine
  0.8 0.0 copy-start.3
  0.8 0.0 copy-start
  0.8 8.9 %collective-permute-start = (bf16[4,16,128]{2,1,0:T(8,128)(2,1)S(1)}, bf16[4,16,128]{2,1,0:T(8,128)(2,1)S(1)}, u32[]{:S(2)}, u32[]{:S(2)}) collective-permute-start(bf16[4,16,128]{2,1,0:T(8,128)(2,1)S(1)} %pad_maximum_fusion.mine), channel_id=1, source_target_pairs={{0,1},{1,0},{2,3},{3,2},{4,5},{5,4},{6,7},{7,6},{8,9},{9,8},{10,11... | collective-permute-start | bytes 49160 | tf_op jit(solution)/shard_map/ppermute | solution.py:268
  9.7 2.4 %shard_map.109 = (bf16[4,128,2048]{2,1,0:T(8,128)(2,1)S(1)}, f32[4,2,2048]{2,1,0:T(2,128)S(1)}) custom-call(bf16[16,1024,128]{2,1,0:T(8,128)(2,1)} %pair.1), custom_call_target="tpu_custom_call" | custom-call | flops 6291456 | bytes 4194304 | tf_op jit(solution)/shard_map/pallas_call | solution.py:55
  12.2 0.0 collective-permute-done.theirs
  12.2 1.9 %shard_map.110 = (bf16[32,8,16,128]{3,2,1,0:T(8,128)(2,1)S(1)}, bf16[128,2048]{1,0:T(8,128)(2,1)S(1)}) custom-call(bf16[4,128,2048]{2,1,0:T(8,128)(2,1)S(1)} %get-tuple-element.20.values, f32[4,2,2048]{2,1,0:T(2,128)S(1)} %get-tuple-element.21.stats, f32[1,128]{1,0:T(1,128)S(1)} %bitcast.35, f32[1,128]{1,0:T(1,128)S(1)} %bitcast.36, ...), custom_call_target="tpu_custom_call" | custom-call | flops 268435456 | bytes 4194304 | tf_op jit(solution)/shard_map/pallas_call | solution.py:103
  14.1 36.0 %all_to_all.10 = bf16[32,128,128]{2,1,0:T(8,128)(2,1)S(1)} all-to-all(bf16[32,128,128]{2,1,0:T(8,128)(2,1)S(1)} %bitcast.33), channel_id=1, replica_groups={{0,64,128,192,256,320,384,448,8,72,136,200,264,328,392,456,16,80,144,20..., dimensions={0} | all-to-all | bytes 2097152 | tf_op jit(solution)/shard_map/all_to_all | solution.py:278
  50.1 1.9 %collective-permute-start.1 = (bf16[32,4,16,128]{3,2,1,0:T(8,128)(2,1)S(1)}, bf16[32,4,16,128]{3,2,1,0:T(8,128)(2,1)S(1)}, u32[]{:S(2)}, u32[]{:S(2)}) collective-permute-start(bf16[32,4,16,128]{3,2,1,0:T(8,128)(2,1)S(1)} %slice.3), channel_id=1, source_target_pairs={{0,1},{1,0},{2,3},{3,2},{4,5},{5,4},{6,7},{7,6},{8,9},{9,8},{10,11... | collective-permute-start | bytes 1572872 | tf_op jit(solution)/shard_map/ppermute | solution.py:289
  52.0 0.0 copy-done.4
  52.0 0.1 reshape.38
  52.1 0.1 reshape.39
  52.2 0.1 copy.16
  52.3 0.1 broadcast_in_dim.16
  52.4 0.1 copy.15
  52.5 0.1 broadcast_in_dim.14
  52.6 0.3 shard_map.111.gate
  53.0 0.1 broadcast_in_dim.15.gain
  53.0 0.1 broadcast_in_dim.17.bias
  53.1 0.5 shard_map.112.begun
  53.6 0.3 collective-permute-done.1.other
  53.9 0.5 shard_map.113
  54.4 40.6 %all_to_all.11 = bf16[256,16,128]{2,1,0:T(8,128)(2,1)S(1)} all-to-all(bf16[256,16,128]{2,1,0:T(8,128)(2,1)S(1)} %bitcast.31), channel_id=1, replica_groups={{0,2,4,6,64,66,68,70,128,130,132,134,192,194,196,198,256,258,260,262,32..., dimensions={0} | all-to-all | bytes 2097152 | tf_op jit(solution)/shard_map/all_to_all | solution.py:303
  95.0 1.8 %shard_map.114 = bf16[16,128,128]{2,1,0:T(8,128)(2,1)} custom-call(bf16[2,128,16,128]{3,2,1,0:T(8,128)(2,1)S(1)} %bitcast.32, f32[128,128]{1,0:T(8,128)S(1)} %broadcast_in_dim.15.gain, f32[128,128]{1,0:T(8,128)S(1)} %broadcast_in_dim.17.bias, bf16[128,128]{1,0:T(8,128)(2,1)S(1)} %bitcast.34, f32[16,128,128]{2,1,0:T(8,128)S(1)} %shard_map.111.gate), custom_call_target="tpu_custom_call" | custom-call | flops 67108864 | bytes 2621440 | tf_op jit(solution)/shard_map/pallas_call | solution.py:237
  (11 shorter events, 0.1 us)
Async XLA Ops:
  0.0 12.2 %copy-start.2 = (f32[128]{0:T(128)S(1)}, f32[128]{0:T(128)}, u32[]{:S(2)}) copy-start(f32[128]{0:T(128)} %param.13) | copy-start | bytes 1540
  0.0 12.2 %copy-start.1 = (f32[128]{0:T(128)S(1)}, f32[128]{0:T(128)}, u32[]{:S(2)}) copy-start(f32[128]{0:T(128)} %param.12) | copy-start | bytes 1540
  0.8 51.2 %copy-start.4 = (f32[128]{0:T(128)S(1)}, f32[128]{0:T(128)}, u32[]{:S(2)}) copy-start(f32[128]{0:T(128)} %param.19) | copy-start | bytes 1540
  0.8 51.3 %copy-start.5 = (f32[128]{0:T(128)S(1)}, f32[128]{0:T(128)}, u32[]{:S(2)}) copy-start(f32[128]{0:T(128)} %param.20) | copy-start | bytes 1540
  0.8 51.8 %copy-start.3 = (bf16[128,128]{1,0:T(8,128)(2,1)S(1)}, bf16[128,128]{1,0:T(8,128)(2,1)}, u32[]{:S(2)}) copy-start(bf16[128,128]{1,0:T(8,128)(2,1)} %param.21) | copy-start | bytes 98308
  0.8 51.8 %copy-start = (bf16[128,128]{1,0:T(8,128)(2,1)S(1)}, bf16[128,128]{1,0:T(8,128)(2,1)}, u32[]{:S(2)}) copy-start(bf16[128,128]{1,0:T(8,128)(2,1)} %weights) | copy-start | bytes 98308
  0.8 11.4 %collective-permute-start = (bf16[4,16,128]{2,1,0:T(8,128)(2,1)S(1)}, bf16[4,16,128]{2,1,0:T(8,128)(2,1)S(1)}, u32[]{:S(2)}, u32[]{:S(2)}) collective-permute-start(bf16[4,16,128]{2,1,0:T(8,128)(2,1)S(1)} %pad_maximum_fusion.mine), channel_id=1, source_target_pairs={{0,1},{1,0},{2,3},{3,2},{4,5},{5,4},{6,7},{7,6},{8,9},{9,8},{10,11... | collective-permute-start | bytes 49160 | tf_op jit(solution)/shard_map/ppermute | solution.py:268
  50.1 3.8 %collective-permute-start.1 = (bf16[32,4,16,128]{3,2,1,0:T(8,128)(2,1)S(1)}, bf16[32,4,16,128]{3,2,1,0:T(8,128)(2,1)S(1)}, u32[]{:S(2)}, u32[]{:S(2)}) collective-permute-start(bf16[32,4,16,128]{3,2,1,0:T(8,128)(2,1)S(1)} %slice.3), channel_id=1, source_target_pairs={{0,1},{1,0},{2,3},{3,2},{4,5},{5,4},{6,7},{7,6},{8,9},{9,8},{10,11... | collective-permute-start | bytes 1572872 | tf_op jit(solution)/shard_map/ppermute | solution.py:289

commit v14 on v13

--- a/solution.py
+++ b/solution.py
@@ -213,10 +213,10 @@
     _, chans, rows, width = mixed.shape
     places = [mirrored(at, chans, core) for at in range(chans)]
     values = jnp.stack([mixed[0, at].astype(F32) + mixed[1, at].astype(F32) for at in places], axis=0)
-    values = values - (jnp.sum(values, axis=0) / chans)[None]
-    scale = lax.rsqrt(jnp.sum(values * values, axis=0) / chans + EPS)
-    scaled = jnp.swapaxes(values * scale[None], 0, 1)
-    scaled = (scaled * gain[...][None] + bias[...][None]).astype(BF16)
+    values = jnp.swapaxes(values, 0, 1)
+    values = values - jnp.mean(values, axis=1, keepdims=True)
+    scale = lax.rsqrt(jnp.mean(values * values, axis=1, keepdims=True) + EPS)
+    scaled = (values * scale * gain[...][None] + bias[...][None]).astype(BF16)
     count = held.shape[0]
     step = rows // count
     copies = []

time: 97.1 us -> 97.1 us (level)
  no operation moved by 1% of the time
where the time goes in v14:
time: 97.1 us; the launch traced here: 96.7 us
  blocking collectives  76.6 us (79%)
  starting transfers between devices  10.8 us (11%)
  Pallas kernels  7.33 us (8%)
    all_to_all x1, blocking collectives, shards(): lax.all_to_all(mixed, ('row', 'x', 'core'), split_axis=0, concat_axis=0,...  40.6 us
    all_to_all x1, blocking collectives, shards(): lax.all_to_all(messages.reshape(half, -1, LANES), ('row', 'core'), split_...  36 us
    ppermute x1, starting transfers between devices, shards(): theirs = lax.ppermute(mine, 'core', SWAP)  8.92 us
    pallas_call x1, Pallas kernels, measure_columns(): pl.pallas_call(measure_kernel, out_shape=(jax.ShapeDtypeStruct((steps, ch...  2.42 us
  transfers between devices with their start and end apart: 2, of which 1 were waited for; matrix products, arithmetic and copies ran while one was open for 1% of the time, Pallas kernels for 3%

profile of v14, /device:TPU:1, one launch (start us, length us, event | category | flops | bytes accessed | tf_op | source)
XLA Modules:
  0.0 96.7 jit_solution(6643656553836308111)
XLA Ops:
  0.0 0.8 pad_maximum_fusion.mine
  0.8 0.0 copy-start.3
  0.8 0.0 copy-start
  0.8 8.9 %collective-permute-start = (bf16[4,16,128]{2,1,0:T(8,128)(2,1)S(1)}, bf16[4,16,128]{2,1,0:T(8,128)(2,1)S(1)}, u32[]{:S(2)}, u32[]{:S(2)}) collective-permute-start(bf16[4,16,128]{2,1,0:T(8,128)(2,1)S(1)} %pad_maximum_fusion.mine), channel_id=1, source_target_pairs={{0,1},{1,0},{2,3},{3,2},{4,5},{5,4},{6,7},{7,6},{8,9},{9,8},{10,11... | collective-permute-start | bytes 49160 | tf_op jit(solution)/shard_map/ppermute | solution.py:268
  9.7 2.4 %shard_map.109 = (bf16[4,128,2048]{2,1,0:T(8,128)(2,1)S(1)}, f32[4,2,2048]{2,1,0:T(2,128)S(1)}) custom-call(bf16[16,1024,128]{2,1,0:T(8,128)(2,1)} %pair.1), custom_call_target="tpu_custom_call" | custom-call | flops 6291456 | bytes 4194304 | tf_op jit(solution)/shard_map/pallas_call | solution.py:55
  12.2 0.0 collective-permute-done.theirs
  12.2 1.9 %shard_map.110 = (bf16[32,8,16,128]{3,2,1,0:T(8,128)(2,1)S(1)}, bf16[128,2048]{1,0:T(8,128)(2,1)S(1)}) custom-call(bf16[4,128,2048]{2,1,0:T(8,128)(2,1)S(1)} %get-tuple-element.20.values, f32[4,2,2048]{2,1,0:T(2,128)S(1)} %get-tuple-element.21.stats, f32[1,128]{1,0:T(1,128)S(1)} %bitcast.35, f32[1,128]{1,0:T(1,128)S(1)} %bitcast.36, ...), custom_call_target="tpu_custom_call" | custom-call | flops 268435456 | bytes 4194304 | tf_op jit(solution)/shard_map/pallas_call | solution.py:103
  14.1 36.0 %all_to_all.10 = bf16[32,128,128]{2,1,0:T(8,128)(2,1)S(1)} all-to-all(bf16[32,128,128]{2,1,0:T(8,128)(2,1)S(1)} %bitcast.33), channel_id=1, replica_groups={{0,64,128,192,256,320,384,448,8,72,136,200,264,328,392,456,16,80,144,20..., dimensions={0} | all-to-all | bytes 2097152 | tf_op jit(solution)/shard_map/all_to_all | solution.py:278
  50.1 1.9 %collective-permute-start.1 = (bf16[32,4,16,128]{3,2,1,0:T(8,128)(2,1)S(1)}, bf16[32,4,16,128]{3,2,1,0:T(8,128)(2,1)S(1)}, u32[]{:S(2)}, u32[]{:S(2)}) collective-permute-start(bf16[32,4,16,128]{3,2,1,0:T(8,128)(2,1)S(1)} %slice.3), channel_id=1, source_target_pairs={{0,1},{1,0},{2,3},{3,2},{4,5},{5,4},{6,7},{7,6},{8,9},{9,8},{10,11... | collective-permute-start | bytes 1572872 | tf_op jit(solution)/shard_map/ppermute | solution.py:289
  52.0 0.1 reshape.38
  52.1 0.0 copy-done.5
  52.1 0.1 reshape.39
  52.2 0.1 copy.16
  52.3 0.1 broadcast_in_dim.16
  52.4 0.1 copy.15
  52.5 0.1 broadcast_in_dim.14
  52.6 0.3 shard_map.111.gate
  53.0 0.1 broadcast_in_dim.15.gain
  53.0 0.1 broadcast_in_dim.17.bias
  53.1 0.5 shard_map.112.begun
  53.6 0.3 collective-permute-done.1.other
  53.9 0.5 shard_map.113
  54.4 40.6 %all_to_all.11 = bf16[256,16,128]{2,1,0:T(8,128)(2,1)S(1)} all-to-all(bf16[256,16,128]{2,1,0:T(8,128)(2,1)S(1)} %bitcast.31), channel_id=1, replica_groups={{0,2,4,6,64,66,68,70,128,130,132,134,192,194,196,198,256,258,260,262,32..., dimensions={0} | all-to-all | bytes 2097152 | tf_op jit(solution)/shard_map/all_to_all | solution.py:303
  95.0 1.7 %shard_map.114 = bf16[16,128,128]{2,1,0:T(8,128)(2,1)} custom-call(bf16[2,128,16,128]{3,2,1,0:T(8,128)(2,1)S(1)} %bitcast.32, f32[128,128]{1,0:T(8,128)S(1)} %broadcast_in_dim.15.gain, f32[128,128]{1,0:T(8,128)S(1)} %broadcast_in_dim.17.bias, bf16[128,128]{1,0:T(8,128)(2,1)S(1)} %bitcast.34, f32[16,128,128]{2,1,0:T(8,128)S(1)} %shard_map.111.gate), custom_call_target="tpu_custom_call" | custom-call | flops 67108864 | bytes 2621440 | tf_op jit(solution)/shard_map/pallas_call | solution.py:237
  (11 shorter events, 0.1 us)
Async XLA Ops:
  0.0 12.2 %copy-start.2 = (f32[128]{0:T(128)S(1)}, f32[128]{0:T(128)}, u32[]{:S(2)}) copy-start(f32[128]{0:T(128)} %param.13) | copy-start | bytes 1540
  0.0 12.2 %copy-start.1 = (f32[128]{0:T(128)S(1)}, f32[128]{0:T(128)}, u32[]{:S(2)}) copy-start(f32[128]{0:T(128)} %param.12) | copy-start | bytes 1540
  0.8 51.2 %copy-start.4 = (f32[128]{0:T(128)S(1)}, f32[128]{0:T(128)}, u32[]{:S(2)}) copy-start(f32[128]{0:T(128)} %param.19) | copy-start | bytes 1540
  0.8 51.3 %copy-start.5 = (f32[128]{0:T(128)S(1)}, f32[128]{0:T(128)}, u32[]{:S(2)}) copy-start(f32[128]{0:T(128)} %param.20) | copy-start | bytes 1540
  0.8 51.8 %copy-start.3 = (bf16[128,128]{1,0:T(8,128)(2,1)S(1)}, bf16[128,128]{1,0:T(8,128)(2,1)}, u32[]{:S(2)}) copy-start(bf16[128,128]{1,0:T(8,128)(2,1)} %param.21) | copy-start | bytes 98308
  0.8 51.8 %copy-start = (bf16[128,128]{1,0:T(8,128)(2,1)S(1)}, bf16[128,128]{1,0:T(8,128)(2,1)}, u32[]{:S(2)}) copy-start(bf16[128,128]{1,0:T(8,128)(2,1)} %weights) | copy-start | bytes 98308
  0.8 11.4 %collective-permute-start = (bf16[4,16,128]{2,1,0:T(8,128)(2,1)S(1)}, bf16[4,16,128]{2,1,0:T(8,128)(2,1)S(1)}, u32[]{:S(2)}, u32[]{:S(2)}) collective-permute-start(bf16[4,16,128]{2,1,0:T(8,128)(2,1)S(1)} %pad_maximum_fusion.mine), channel_id=1, source_target_pairs={{0,1},{1,0},{2,3},{3,2},{4,5},{5,4},{6,7},{7,6},{8,9},{9,8},{10,11... | collective-permute-start | bytes 49160 | tf_op jit(solution)/shard_map/ppermute | solution.py:268
  50.1 3.8 %collective-permute-start.1 = (bf16[32,4,16,128]{3,2,1,0:T(8,128)(2,1)S(1)}, bf16[32,4,16,128]{3,2,1,0:T(8,128)(2,1)S(1)}, u32[]{:S(2)}, u32[]{:S(2)}) collective-permute-start(bf16[32,4,16,128]{3,2,1,0:T(8,128)(2,1)S(1)} %slice.3), channel_id=1, source_target_pairs={{0,1},{1,0},{2,3},{3,2},{4,5},{5,4},{6,7},{7,6},{8,9},{9,8},{10,11... | collective-permute-start | bytes 1572872 | tf_op jit(solution)/shard_map/ppermute | solution.py:289
